TPU v7x, 32 devices: a whole 2x2x4 slice. The times are simulated.
32 devices in a mesh: seq: 8 (over y, x, core), fsdp: 4 (over z).
Axes of the slice: x: 2, y: 2, z: 4, core: 2. Of those that a mesh axis runs over, the one named last changes fastest.
Arguments:
- tokens: bfloat16 [2, 4, 1920, 2304], P(None, 'fsdp', 'seq'), may hold values from -6 to 6
- segments: int32 [2, 4, 1920], P(None, 'fsdp', 'seq'), may hold values from 0 to 3, as said below
- w_query: bfloat16 [2304, 2048], P('fsdp'), may hold values from -0.125 to 0.125
- key_weight: bfloat16 [2304, 1024], P('fsdp'), may hold values from -0.125 to 0.125
- value_weight: bfloat16 [2304, 1024], P('fsdp'), may hold values from -0.125 to 0.125
- w_out: bfloat16 [2048, 2304], P('fsdp'), may hold values from -0.125 to 0.125
- w_gate: bfloat16 [2304, 9216], P('fsdp'), may hold values from -0.125 to 0.125
- w_up: bfloat16 [2304, 9216], P('fsdp'), may hold values from -0.125 to 0.125
- w_down: bfloat16 [9216, 2304], P('fsdp'), may hold values from -0.0625 to 0.0625
- gain_attn_in: float32 [2304], replicated, may hold values from 0.5 to 1.5
- gain_attn_out: float32 [2304], replicated, may hold values from 0.5 to 1.5
- gain_ffn_in: float32 [2304], replicated, may hold values from 0.5 to 1.5
- gain_ffn_out: float32 [2304], replicated, may hold values from 0.5 to 1.5
- cotangent: bfloat16 [2, 4, 1920, 2304], P(None, 'fsdp', 'seq'), may hold values from -6 to 6
Outputs:
- mixed_out: bfloat16 [2, 4, 1920, 2304], P(None, 'fsdp', 'seq')
- grad_tokens: float32 [2, 4, 1920, 2304], P(None, 'fsdp', 'seq')
- grad_query: float32 [2304, 2048], P('fsdp', 'seq')
- grad_key: float32 [2304, 1024], P('fsdp', 'seq')
- grad_value: float32 [2304, 1024], P('fsdp', 'seq')
- grad_out: float32 [2048, 2304], P('fsdp', 'seq')
- grad_gate: float32 [2304, 9216], P('fsdp', 'seq')
- grad_up: float32 [2304, 9216], P('fsdp', 'seq')
- grad_down: float32 [9216, 2304], P('fsdp', 'seq')
- grad_attn_in: float32 [2304], replicated
- grad_attn_out: float32 [2304], replicated
- grad_ffn_in: float32 [2304], replicated
- grad_ffn_out: float32 [2304], replicated
Inputs may be any that keep to these rules, and one draw needn't show every extreme that they name: `segments`: in each sequence the segment numbers start at 0, never fall, and rise by at most one from token to token; tokens with equal numbers form one document. For every sequence index of a micro-batch, one of the 2 micro-batches, drawn from the seed, is a single document; every other sequence holds exactly four documents.
All inputs are finite; a program needn't handle non-finite values.
Results may differ from a plain program's by a relative error of at most 0.02.
Values may be sent and summed in bfloat16 or wider, within the bound.
A program may use at most 576 MiB of HBM per device.

v0:
```python
import math

import jax
import jax.numpy as jnp
from jax import lax
from jax.sharding import PartitionSpec as P

QUERY_HEADS = 8
KEY_VALUE_HEADS = 4
HEAD_SIZE = 256
CAP = 50
WIN = 1024


epsilon = 1e-06


def shifted(value, axis, steps):
    count = lax.axis_size(axis)
    initial, last = (max(0, -steps), min(count, count - steps))
    return lax.ppermute(value, axis, [(source, source + steps) for source in range(initial, last)])


def rms_gain(stream, gain):
    return stream * lax.rsqrt(jnp.mean(stream * stream, axis=-1, keepdims=True) + epsilon) * gain


def geglu(gate_proj, up_proj):
    return jax.nn.gelu(gate_proj, approximate=True) * up_proj


def angles(position, size):
    frequency = 10000.0 ** (-jnp.arange(size // 2, dtype=jnp.float32) * 2.0 / size)
    phase_angle = position.astype(jnp.float32)[:, None] * frequency[None, :]
    return (jnp.cos(phase_angle)[:, None, :], jnp.sin(phase_angle)[:, None, :])


def rotate(value_rows, cosine_table, sine_table, direction):
    half_size = value_rows.shape[-1] // 2
    first_half = value_rows[..., :half_size]
    second = value_rows[..., half_size:]
    return jnp.concatenate(
        [
            first_half * cosine_table - direction * second * sine_table,
            second * cosine_table + direction * first_half * sine_table,
        ],
        axis=-1,
    )


def doc_positions(segment):
    places = jnp.arange(segment.shape[0], dtype=jnp.int32)
    previous = jnp.concatenate([segment[:1] - 1, segment[:-1]])
    starts = jnp.where(segment != previous, places, 0)
    return places - lax.cummax(starts, axis=0)


def final_dot(left_side, right_side):
    return jnp.dot(left_side, right_side, preferred_element_type=jnp.float32)


def dot_back(left_side, right_side):
    return lax.dot_general(
        left_side, right_side, (((1,), (1,)), ((), ())), preferred_element_type=jnp.float32
    )


def dot_rows(left_side, right_side):
    return lax.dot_general(
        left_side, right_side, (((0,), (0,)), ((), ())), preferred_element_type=jnp.float32
    )


def fetch_attention(w_query, key_weight, value_weight, w_out):
    return (
        lax.all_gather(w_query, "fsdp", axis=0, tiled=True),
        lax.all_gather(key_weight, "fsdp", axis=0, tiled=True),
        lax.all_gather(value_weight, "fsdp", axis=0, tiled=True),
        lax.all_gather(w_out, "fsdp", axis=0, tiled=True),
    )


def fetch_ffn(w_gate, w_up, w_down):
    return (
        lax.all_gather(w_gate, "fsdp", axis=0, tiled=True),
        lax.all_gather(w_up, "fsdp", axis=0, tiled=True),
        lax.all_gather(w_down, "fsdp", axis=0, tiled=True),
    )


def key_window(kv_pair, halo_count):
    arrived = [shifted(kv_pair, "seq", offset) for offset in range(halo_count, 0, -1)]
    return jnp.concatenate(arrived + [kv_pair], axis=1)


def window_grads(paired_gradient, halo_count, token_rows):
    summed = paired_gradient[:, halo_count * token_rows :]
    for offset in range(1, halo_count + 1):
        begin = (halo_count - offset) * token_rows
        summed = summed + shifted(
            paired_gradient[:, begin : begin + token_rows].astype(jnp.bfloat16), "seq", -offset
        ).astype(jnp.float32)
    return summed


def window_mask(seg_here, seg_whole, seq_place, token_rows, halo_count):
    padded = jnp.concatenate([jnp.full((halo_count * token_rows,), -1, jnp.int32), seg_whole])
    key_seg = lax.dynamic_slice_in_dim(
        padded, seq_place * token_rows, (halo_count + 1) * token_rows
    )
    query_pos = seq_place * token_rows + jnp.arange(token_rows, dtype=jnp.int32)
    key_pos = (
        seq_place * token_rows
        - halo_count * token_rows
        + jnp.arange((halo_count + 1) * token_rows, dtype=jnp.int32)
    )
    distance = query_pos[:, None] - key_pos[None, :]
    return (seg_here[:, None] == key_seg[None, :]) & (distance >= 0) & (distance < WIN)


def forward_pass(stream, seg_whole, attn_w, ffn_w, gain_list, halo_count):
    token_rows = stream.shape[0]
    seq_place = lax.axis_index("seq")
    seg_here = lax.dynamic_slice_in_dim(seg_whole, seq_place * token_rows, token_rows)
    position = lax.dynamic_slice_in_dim(
        doc_positions(seg_whole), seq_place * token_rows, token_rows
    )
    cosine_table, sine_table = angles(position, HEAD_SIZE)
    w_query, key_weight, value_weight, w_out = attn_w
    w_gate, w_up, w_down = ffn_w
    normed_input = rms_gain(stream, gain_list[0]).astype(jnp.bfloat16)
    query_rows = rotate(
        final_dot(normed_input, w_query).reshape(token_rows, QUERY_HEADS, HEAD_SIZE),
        cosine_table,
        sine_table,
        1.0,
    )
    query_rows = (query_rows * (1.0 / math.sqrt(HEAD_SIZE))).astype(jnp.bfloat16)
    keys_here = rotate(
        final_dot(normed_input, key_weight).reshape(token_rows, KEY_VALUE_HEADS, HEAD_SIZE),
        cosine_table,
        sine_table,
        1.0,
    ).astype(jnp.bfloat16)
    local_values = (
        final_dot(normed_input, value_weight)
        .reshape(token_rows, KEY_VALUE_HEADS, HEAD_SIZE)
        .astype(jnp.bfloat16)
    )
    window_pair = key_window(jnp.stack([keys_here, local_values]), halo_count)
    allowed = window_mask(seg_here, seg_whole, seq_place, token_rows, halo_count)
    grouped_heads = query_rows.reshape(
        token_rows, KEY_VALUE_HEADS, QUERY_HEADS // KEY_VALUE_HEADS, HEAD_SIZE
    )
    raw_score = jnp.einsum(
        "qhgd,khd->hgqk", grouped_heads, window_pair[0], preferred_element_type=jnp.float32
    )
    capped = jnp.where(allowed, CAP * jnp.tanh(raw_score / CAP), -jnp.inf)
    row_peak = jnp.max(capped, axis=-1, keepdims=True)
    exponent = jnp.exp(capped - row_peak)
    row_total = jnp.sum(exponent, axis=-1, keepdims=True)
    log_total = row_peak + jnp.log(row_total)
    attended = jnp.einsum(
        "hgqk,khd->qhgd",
        (exponent / row_total).astype(jnp.bfloat16),
        window_pair[1],
        preferred_element_type=jnp.float32,
    )
    attended = attended.reshape(token_rows, QUERY_HEADS * HEAD_SIZE).astype(jnp.bfloat16)
    mixed = final_dot(attended, w_out)
    middle = stream + rms_gain(mixed, gain_list[1])
    ffn_in = rms_gain(middle, gain_list[2]).astype(jnp.bfloat16)
    gate_proj = final_dot(ffn_in, w_gate)
    up_proj = final_dot(ffn_in, w_up)
    hidden = geglu(gate_proj, up_proj).astype(jnp.bfloat16)
    down_proj = final_dot(hidden, w_down)
    result = middle + rms_gain(down_proj, gain_list[3])
    saved_state = (
        stream,
        normed_input,
        grouped_heads,
        window_pair,
        allowed,
        log_total,
        cosine_table,
        sine_table,
        attended,
        mixed,
        middle,
        ffn_in,
        gate_proj,
        up_proj,
        hidden,
        down_proj,
    )
    return (result, saved_state)


def backward_pass(grad_result, saved_state, attn_w, ffn_w, gain_list, halo_count):
    (
        stream,
        normed_input,
        grouped_heads,
        window_pair,
        allowed,
        log_total,
        cosine_table,
        sine_table,
        attended,
        mixed,
        middle,
        ffn_in,
        gate_proj,
        up_proj,
        hidden,
        down_proj,
    ) = saved_state
    token_rows = stream.shape[0]
    w_query, key_weight, value_weight, w_out = attn_w
    w_gate, w_up, w_down = ffn_w
    _, pullback = jax.vjp(rms_gain, down_proj, gain_list[3])
    grad_down_f, grad_gain_four = pullback(grad_result)
    grad_down_b = grad_down_f.astype(jnp.bfloat16)
    grad_hidden = dot_back(grad_down_b, w_down)
    _, pullback = jax.vjp(geglu, gate_proj, up_proj)
    grad_gate_f, grad_up_f = pullback(grad_hidden)
    grad_gate_b = grad_gate_f.astype(jnp.bfloat16)
    grad_up_b = grad_up_f.astype(jnp.bfloat16)
    grad_ffn_in = dot_back(grad_gate_b, w_gate) + dot_back(grad_up_b, w_up)
    _, pullback = jax.vjp(rms_gain, middle, gain_list[2])
    grad_middle_part, grad_gain_three = pullback(grad_ffn_in)
    grad_middle = grad_result + grad_middle_part
    _, pullback = jax.vjp(rms_gain, mixed, gain_list[1])
    grad_mixed_f, grad_gain_two = pullback(grad_middle)
    grad_mixed_b = grad_mixed_f.astype(jnp.bfloat16)
    attention_block_gradient = dot_back(grad_mixed_b, w_out).astype(jnp.bfloat16)
    grouped_gradient = attention_block_gradient.reshape(
        token_rows, KEY_VALUE_HEADS, QUERY_HEADS // KEY_VALUE_HEADS, HEAD_SIZE
    )
    raw_score = jnp.einsum(
        "qhgd,khd->hgqk", grouped_heads, window_pair[0], preferred_element_type=jnp.float32
    )
    tanh_value = jnp.tanh(raw_score / CAP)
    capped = jnp.where(allowed, CAP * tanh_value, -jnp.inf)
    soft_prob = jnp.exp(capped - log_total)
    grad_prob = jnp.einsum(
        "qhgd,khd->hgqk", grouped_gradient, window_pair[1], preferred_element_type=jnp.float32
    )
    row_delta = jnp.sum(soft_prob * grad_prob, axis=-1, keepdims=True)
    grad_score_b = (soft_prob * (grad_prob - row_delta) * (1.0 - tanh_value * tanh_value)).astype(
        jnp.bfloat16
    )
    grad_queries = jnp.einsum(
        "hgqk,khd->qhgd", grad_score_b, window_pair[0], preferred_element_type=jnp.float32
    )
    grad_keys_win = jnp.einsum(
        "hgqk,qhgd->khd", grad_score_b, grouped_heads, preferred_element_type=jnp.float32
    )
    grad_values_win = jnp.einsum(
        "hgqk,qhgd->khd",
        soft_prob.astype(jnp.bfloat16),
        grouped_gradient,
        preferred_element_type=jnp.float32,
    )
    paired_gradient = window_grads(
        jnp.stack([grad_keys_win, grad_values_win]), halo_count, token_rows
    )
    grad_q_b = rotate(
        grad_queries.reshape(token_rows, QUERY_HEADS, HEAD_SIZE) * (1.0 / math.sqrt(HEAD_SIZE)),
        cosine_table,
        sine_table,
        -1.0,
    )
    grad_q_b = grad_q_b.reshape(token_rows, QUERY_HEADS * HEAD_SIZE).astype(jnp.bfloat16)
    grad_k_b = (
        rotate(paired_gradient[0], cosine_table, sine_table, -1.0)
        .reshape(token_rows, KEY_VALUE_HEADS * HEAD_SIZE)
        .astype(jnp.bfloat16)
    )
    value_block_gradient = (
        paired_gradient[1].reshape(token_rows, KEY_VALUE_HEADS * HEAD_SIZE).astype(jnp.bfloat16)
    )
    grad_normed = (
        dot_back(grad_q_b, w_query)
        + dot_back(grad_k_b, key_weight)
        + dot_back(value_block_gradient, value_weight)
    )
    _, pullback = jax.vjp(rms_gain, stream, gain_list[0])
    grad_stream_part, grad_gain_one = pullback(grad_normed)
    grad_stream = grad_middle + grad_stream_part
    gain_stack = jnp.stack([grad_gain_one, grad_gain_two, grad_gain_three, grad_gain_four])
    record = (
        normed_input,
        grad_q_b,
        grad_k_b,
        value_block_gradient,
        attended,
        grad_mixed_b,
        ffn_in,
        grad_gate_b,
        grad_up_b,
        hidden,
        grad_down_b,
    )
    return (grad_stream, gain_stack, record)


def on_device(
    tokens,
    segments,
    w_query,
    key_weight,
    value_weight,
    w_out,
    w_gate,
    w_up,
    w_down,
    gain_attn_in,
    gain_attn_out,
    gain_ffn_in,
    gain_ffn_out,
    cotangent,
):
    micro_count = tokens.shape[0]
    token_rows = tokens.shape[2]
    width_model = tokens.shape[3]
    halo_count = (WIN - 2 + token_rows) // token_rows
    gain_list = (gain_attn_in, gain_attn_out, gain_ffn_in, gain_ffn_out)
    seg_gathered = lax.all_gather(segments, "seq", axis=2, tiled=True)
    attn_kept = fetch_attention(w_query, key_weight, value_weight, w_out)
    ffn_kept = fetch_ffn(w_gate, w_up, w_down)
    results = []
    input_grads = []
    records = []
    gain_grads = jnp.zeros((4, width_model), jnp.float32)
    for batch_index in range(micro_count):
        stream = tokens[batch_index, 0].astype(jnp.float32)
        attn_w, ffn_w = (attn_kept, ffn_kept)
        result, saved_state = forward_pass(
            stream, seg_gathered[batch_index, 0], attn_w, ffn_w, gain_list, halo_count
        )
        results.append(result.astype(jnp.bfloat16))
        grad_stream, gain_stack, record = backward_pass(
            cotangent[batch_index, 0].astype(jnp.float32),
            saved_state,
            attn_w,
            ffn_w,
            gain_list,
            halo_count,
        )
        input_grads.append(grad_stream)
        gain_grads = gain_grads + gain_stack
        records.append(record)
    joined = [jnp.concatenate([entry[member] for entry in records], axis=0) for member in range(11)]
    (
        normed_all,
        grad_q_all,
        grad_k_all,
        grad_v_all,
        attended_all,
        grad_mixed_all,
        ffn_in_all,
        grad_gate_all,
        grad_up_all,
        hidden_all,
        grad_down_all,
    ) = joined
    moved_grads = (
        lax.all_to_all(grad_q_all, "seq", split_axis=1, concat_axis=0, tiled=True),
        lax.all_to_all(grad_k_all, "seq", split_axis=1, concat_axis=0, tiled=True),
        lax.all_to_all(grad_v_all, "seq", split_axis=1, concat_axis=0, tiled=True),
        lax.all_to_all(grad_gate_all, "seq", split_axis=1, concat_axis=0, tiled=True),
        lax.all_to_all(grad_up_all, "seq", split_axis=1, concat_axis=0, tiled=True),
        lax.all_to_all(grad_mixed_all, "seq", split_axis=1, concat_axis=0, tiled=True),
        lax.all_to_all(grad_down_all, "seq", split_axis=1, concat_axis=0, tiled=True),
    )
    input_index = (0, 0, 0, 1, 1, 2, 3)
    pieces = (
        lax.all_gather(normed_all, "seq", axis=0, tiled=True),
        lax.all_gather(ffn_in_all, "seq", axis=0, tiled=True),
        lax.all_gather(attended_all, "seq", axis=0, tiled=True),
        lax.all_gather(hidden_all, "seq", axis=0, tiled=True),
    )
    updated = []
    for member in range(7):
        grad_rows = moved_grads[member]
        updated.append(dot_rows(pieces[input_index[member]], grad_rows))
    column_sums = tuple(updated)
    owned = (
        lax.psum_scatter(
            column_sums[0].astype(jnp.bfloat16), "fsdp", scatter_dimension=0, tiled=True
        ).astype(jnp.float32),
        lax.psum_scatter(
            column_sums[1].astype(jnp.bfloat16), "fsdp", scatter_dimension=0, tiled=True
        ).astype(jnp.float32),
        lax.psum_scatter(
            column_sums[2].astype(jnp.bfloat16), "fsdp", scatter_dimension=0, tiled=True
        ).astype(jnp.float32),
        lax.psum_scatter(
            column_sums[3].astype(jnp.bfloat16), "fsdp", scatter_dimension=0, tiled=True
        ).astype(jnp.float32),
        lax.psum_scatter(
            column_sums[4].astype(jnp.bfloat16), "fsdp", scatter_dimension=0, tiled=True
        ).astype(jnp.float32),
        lax.psum_scatter(
            column_sums[5].astype(jnp.bfloat16), "fsdp", scatter_dimension=0, tiled=True
        ).astype(jnp.float32),
        lax.psum_scatter(
            column_sums[6].astype(jnp.bfloat16), "fsdp", scatter_dimension=0, tiled=True
        ).astype(jnp.float32),
    )
    gain_total = lax.psum(gain_grads, ("seq", "fsdp"))
    mixed_out = jnp.stack(results)[:, None]
    grad_tokens = jnp.stack(input_grads)[:, None]
    return (
        mixed_out,
        grad_tokens,
        owned[0],
        owned[1],
        owned[2],
        owned[5],
        owned[3],
        owned[4],
        owned[6],
        gain_total[0],
        gain_total[1],
        gain_total[2],
        gain_total[3],
    )


def solution(mesh):
    in_specs = (
        P(None, "fsdp", "seq", None),
        P(None, "fsdp", "seq"),
        P("fsdp", None),
        P("fsdp", None),
        P("fsdp", None),
        P("fsdp", None),
        P("fsdp", None),
        P("fsdp", None),
        P("fsdp", None),
        P(),
        P(),
        P(),
        P(),
        P(None, "fsdp", "seq", None),
    )
    out_specs = (
        P(None, "fsdp", "seq", None),
        P(None, "fsdp", "seq", None),
        P("fsdp", "seq"),
        P("fsdp", "seq"),
        P("fsdp", "seq"),
        P("fsdp", "seq"),
        P("fsdp", "seq"),
        P("fsdp", "seq"),
        P("fsdp", "seq"),
        P(),
        P(),
        P(),
        P(),
    )
    return jax.shard_map(
        on_device, mesh=mesh, in_specs=in_specs, out_specs=out_specs, check_vma=False
    )
```

profile of v0, /device:TPU:0, one launch (start us, length us, event | category | flops | bytes accessed | tf_op | source)
XLA Modules:
  0.0 4291.6 jit_solution(11456683884188746099)
XLA Ops:
  26.4 114.8 %slice_reduce_fusion.1 = (s32[1919]{0:T(1024)S(1)}, s32[1919]{0:T(1024)S(1)}) fusion(s32[2,1,1920]{0,1,2:T(1,128)S(1)} %all_gather.37), kind=kLoop, calls=%fused_computation.245 | loop fusion | bytes 30704 | tf_op jit(solution)/shard_map/slice | solution.py:53
  141.2 79.1 %slice_reduce_fusion.9 = (s32[1920]{0:T(1024)S(1)}, s32[1920]{0:T(1024)S(1)}, s32[1,1,1920]{0,1,2:T(1,128)S(1)}, s32[1,1,1920]{0,1,2:T(1,128)}) fusion(s32[2,1,1920]{0,1,2:T(1,128)S(1)} %all_gather.37), kind=kLoop, calls=%fused_computation.361 | loop fusion | bytes 46080 | tf_op jit(solution)/shard_map/slice | solution.py:340
  268.0 52.3 %collective-permute-done.5 = bf16[2,240,4,256]{3,1,2,0:T(8,128)(2,1)S(1)} collective-permute-done((bf16[2,240,4,256]{3,1,2,0:T(8,128)(2,1)S(1)}, bf16[2,240,4,256]{3,1,2,0:T(8,128)(2,1)S(1)}, u32[]{:S(2)}, u32[]{:S(2)}) %collective-permute-start.5) | collective-permute-done | bytes 983072 | tf_op jit(solution)/shard_map/ppermute | solution.py:21
  324.6 37.9 collective-permute-done.6
  374.4 30.2 collective-permute-done
  405.6 20.0 collective-permute-done.1
  431.0 12.7 copy.110
  491.8 32.6 all-gather.18.cloned.1.call-done
  541.2 691.2 %all-gather.20.cloned.1.call-done = bf16[2304,9216]{1,0:T(8,128)(2,1)} async-done(((bf16[576,9216]{1,0:T(8,128)(2,1)}), bf16[2304,9216]{1,0:T(8,128)(2,1)}) %all-gather.20.cloned.1.call-update) | async-done | bytes 42467344 | tf_op jit(solution)/shard_map/all_gather | solution.py:85
  1232.4 28.7 fusion.194
  1261.1 679.3 %all-gather.22.cloned.1.call-done = bf16[2304,9216]{1,0:T(8,128)(2,1)} async-done(((bf16[576,9216]{1,0:T(8,128)(2,1)}), bf16[2304,9216]{1,0:T(8,128)(2,1)}) %all-gather.22.cloned.1.call-update) | async-done | bytes 42467344 | tf_op jit(solution)/shard_map/all_gather | solution.py:86
  1940.4 31.9 multiply_convert_fusion.2
  1972.3 676.1 %all-gather.24.cloned.1.call-done = bf16[9216,2304]{1,0:T(8,128)(2,1)} async-done(((bf16[2304,2304]{1,0:T(8,128)(2,1)}), bf16[9216,2304]{1,0:T(8,128)(2,1)}) %all-gather.24.cloned.1.call-update) | async-done | bytes 42467344 | tf_op jit(solution)/shard_map/all_gather | solution.py:87
  2648.5 23.5 multiply_reduce_fusion.8
  2672.0 21.2 fusion.193
  2693.2 25.6 multiply_convert_fusion.3
  2718.8 22.0 multiply_reduce_fusion.11
  2751.8 27.2 multiply_convert_fusion
  2779.0 22.2 fusion.197
  2801.2 20.1 convolution_add_fusion.4
  2821.3 26.4 multiply_convert_fusion.1
  2847.8 20.4 fusion.195
  2868.2 23.2 multiply_reduce_fusion.2
  2913.7 27.1 convolution_bitcast_fusion.1
  2969.9 19.8 fusion.107
  3007.0 19.3 fusion.106
  3027.7 28.0 convolution_bitcast_fusion
  3104.8 35.3 collective-permute-done.16
  3147.1 13.2 collective-permute-done.19
  3186.7 31.7 all-to-all-start.3
  3233.6 29.3 all-to-all-done.3
  3302.9 110.3 %all-to-all-done.5 = bf16[480,8,1152]{2,0,1:T(8,128)(2,1)} async-done(((bf16[480,8,1152]{2,0,1:T(8,128)(2,1)}), bf16[480,8,1152]{2,0,1:T(8,128)(2,1)}, u32[]{:S(2)}, u32[]{:S(2)}) %all-to-all-start.5) | async-done | bytes 8847392 | tf_op jit(solution)/shard_map/all_to_all | solution.py:373
  3418.4 30.8 convolution_convert_fusion.1
  3449.6 146.6 %all-to-all-done.4 = bf16[480,8,1152]{2,0,1:T(8,128)(2,1)} async-done(((bf16[480,8,1152]{2,0,1:T(8,128)(2,1)}), bf16[480,8,1152]{2,0,1:T(8,128)(2,1)}, u32[]{:S(2)}, u32[]{:S(2)}) %all-to-all-start.4) | async-done | bytes 8847392 | tf_op jit(solution)/shard_map/all_to_all | solution.py:372
  3596.3 30.1 convolution_convert_fusion.2
  3636.3 21.5 all-to-all-done.2
  3665.9 21.7 all-to-all-done.1
  3694.0 52.1 %all-to-all-done.6 = bf16[480,8,288]{0,2,1:T(8,128)(2,1)S(1)} async-done(((bf16[480,8,288]{0,2,1:T(8,128)(2,1)}), bf16[480,8,288]{0,2,1:T(8,128)(2,1)S(1)}, u32[]{:S(2)}, u32[]{:S(2)}) %all-to-all-start.6) | async-done | bytes 2211872 | tf_op jit(solution)/shard_map/all_to_all | solution.py:375
  3782.6 14.5 all-to-all-done
  3809.6 72.3 %all-gather.32.cloned.1.call-done = bf16[3840,9216]{1,0:T(8,128)(2,1)} async-done(((bf16[480,9216]{1,0:T(8,128)(2,1)}), bf16[3840,9216]{1,0:T(8,128)(2,1)}) %all-gather.32.cloned.1.call-update) | async-done | bytes 70778896 | tf_op jit(solution)/shard_map/all_gather | solution.py:382
  3881.9 31.4 convolution_convert_fusion
  3917.6 44.3 %psum.7 = f32[4,2304]{1,0:T(4,128)S(1)} all-reduce(f32[4,2304]{1,0:T(4,128)S(1)} %maximum_add_fusion), channel_id=1, replica_groups=mesh['seq'=8,'fsdp'=4] {'seq','fsdp'}, use_global_device_ids=true, to_apply=%region_41.42 | all-reduce | flops 9216 | bytes 73728 | tf_op jit(solution)/shard_map/psum | solution.py:412
  3971.8 38.4 reduce-scatter.18.cloned.1.call-done
  4013.3 94.5 %reduce-scatter.16.cloned.1.call-done = bf16[576,1152]{1,0:T(8,128)(2,1)} async-done(((bf16[2304,1152]{1,0:T(8,128)(2,1)}), bf16[576,1152]{1,0:T(8,128)(2,1)}) %reduce-scatter.16.cloned.1.call-update) | async-done | bytes 1327120 | tf_op jit(solution)/shard_map/reduce_scatter | solution.py:399
  4110.8 21.6 reduce-scatter.12.cloned.1.call-done
  4134.0 21.4 reduce-scatter.10.cloned.1.call-done
  4157.0 28.7 reduce-scatter.8.cloned.1.call-done
  4187.6 93.9 %reduce-scatter.20.cloned.1.call-done = bf16[2304,288]{0,1:T(8,128)(2,1)} async-done(((bf16[9216,288]{0,1:T(8,128)(2,1)}), bf16[2304,288]{0,1:T(8,128)(2,1)}) %reduce-scatter.20.cloned.1.call-update) | async-done | bytes 1327120 | tf_op jit(solution)/shard_map/reduce_scatter | solution.py:408
  (520 shorter events, 476.8 us)
Async XLA Ops:
  7.2 227.0 %all-gather.12.cloned.1.call-start = ((), (), s32[]{:S(2)}) async-start(), calls=%async_computation.14 | async-start | bytes 5898240 | tf_op jit(solution)/shard_map/all_gather | solution.py:77
  7.9 233.1 %all-gather.14.cloned.1.call-start = ((), (), s32[]{:S(2)}) async-start(), calls=%async_computation.15 | async-start | bytes 5898240 | tf_op jit(solution)/shard_map/all_gather | solution.py:78
  8.7 422.3 %all-gather.16.cloned.1.call-start = ((), (), s32[]{:S(2)}) async-start(), calls=%async_computation.16 | async-start | bytes 11796480 | tf_op jit(solution)/shard_map/all_gather | solution.py:76
  9.4 515.1 %all-gather.18.cloned.1.call-start = ((), (), s32[]{:S(2)}) async-start(), calls=%async_computation.17 | async-start | bytes 11796480 | tf_op jit(solution)/shard_map/all_gather | solution.py:79
  10.0 1222.4 %all-gather.20.cloned.1.call-start = ((), (), s32[]{:S(2)}) async-start(), calls=%async_computation.18 | async-start | bytes 53084160 | tf_op jit(solution)/shard_map/all_gather | solution.py:85
  10.6 1929.8 %all-gather.22.cloned.1.call-start = ((), (), s32[]{:S(2)}) async-start(), calls=%async_computation.19 | async-start | bytes 53084160 | tf_op jit(solution)/shard_map/all_gather | solution.py:86
  11.1 2637.3 %all-gather.24.cloned.1.call-start = ((), (), s32[]{:S(2)}) async-start(), calls=%async_computation.20 | async-start | bytes 53084160 | tf_op jit(solution)/shard_map/all_gather | solution.py:87
  11.9 3281.0 %all-gather.28.cloned.1.call-start = ((), (), s32[]{:S(2)}) async-start(), calls=%async_computation.25 | async-start | bytes 17694720 | tf_op jit(solution)/shard_map/all_gather | solution.py:381
  232.5 233.2 %copy-start.100 = (f32[240]{0:T(256)}, f32[240]{0:T(256)S(1)}, u32[]{:S(2)}) copy-start(f32[240]{0:T(256)S(1)} %get-tuple-element.191) | copy-start | bytes 2884
  234.2 238.0 %copy-start.37 = (f32[240,128]{1,0:T(8,128)}, f32[240,128]{1,0:T(8,128)S(1)}, u32[]{:S(2)}) copy-start(f32[240,128]{1,0:T(8,128)S(1)} %get-tuple-element.160) | copy-start | bytes 368644
  253.5 66.8 %collective-permute-start.5 = (bf16[2,240,4,256]{3,1,2,0:T(8,128)(2,1)S(1)}, bf16[2,240,4,256]{3,1,2,0:T(8,128)(2,1)S(1)}, u32[]{:S(2)}, u32[]{:S(2)}) collective-permute-start(bf16[2,240,4,256]{3,1,2,0:T(8,128)(2,1)S(1)} %pad_maximum_fusion.12), channel_id=1, source_target_pairs={{0,20},{4,24},{8,28},{1,21},{5,25},{9,29},{2,22},{6,26},{10,30},{3... | collective-permute-start | bytes 2949128 | tf_op jit(solution)/shard_map/ppermute | solution.py:21
  256.9 105.6 %collective-permute-start.6 = (bf16[2,240,4,256]{3,1,2,0:T(8,128)(2,1)S(1)}, bf16[2,240,4,256]{3,1,2,0:T(8,128)(2,1)S(1)}, u32[]{:S(2)}, u32[]{:S(2)}) collective-permute-start(bf16[2,240,4,256]{3,1,2,0:T(8,128)(2,1)S(1)} %pad_maximum_fusion.12), channel_id=1, source_target_pairs={{0,16},{4,20},{8,24},{12,28},{1,17},{5,21},{9,25},{13,29},{2,18},{... | collective-permute-start | bytes 2949128 | tf_op jit(solution)/shard_map/ppermute | solution.py:21
  258.2 110.9 %collective-permute-start.7 = (bf16[2,240,4,256]{3,1,2,0:T(8,128)(2,1)S(1)}, bf16[2,240,4,256]{3,1,2,0:T(8,128)(2,1)S(1)}, u32[]{:S(2)}, u32[]{:S(2)}) collective-permute-start(bf16[2,240,4,256]{3,1,2,0:T(8,128)(2,1)S(1)} %pad_maximum_fusion.12), channel_id=1, source_target_pairs={{0,12},{4,16},{8,20},{12,24},{16,28},{1,13},{5,17},{9,21},{13,25},... | collective-permute-start | bytes 2949128 | tf_op jit(solution)/shard_map/ppermute | solution.py:21
  260.4 110.2 %collective-permute-start.8 = (bf16[2,240,4,256]{3,1,2,0:T(8,128)(2,1)S(1)}, bf16[2,240,4,256]{3,1,2,0:T(8,128)(2,1)S(1)}, u32[]{:S(2)}, u32[]{:S(2)}) collective-permute-start(bf16[2,240,4,256]{3,1,2,0:T(8,128)(2,1)S(1)} %pad_maximum_fusion.12), channel_id=1, source_target_pairs={{0,8},{4,12},{8,16},{12,20},{16,24},{20,28},{1,9},{5,13},{9,17},{1... | collective-permute-start | bytes 2949128 | tf_op jit(solution)/shard_map/ppermute | solution.py:21
  262.9 109.1 %collective-permute-start.9 = (bf16[2,240,4,256]{3,1,2,0:T(8,128)(2,1)S(1)}, bf16[2,240,4,256]{3,1,2,0:T(8,128)(2,1)S(1)}, u32[]{:S(2)}, u32[]{:S(2)}) collective-permute-start(bf16[2,240,4,256]{3,1,2,0:T(8,128)(2,1)S(1)} %pad_maximum_fusion.12), channel_id=1, source_target_pairs={{0,4},{4,8},{8,12},{12,16},{16,20},{20,24},{24,28},{1,5},{5,9},{9,... | collective-permute-start | bytes 2949128 | tf_op jit(solution)/shard_map/ppermute | solution.py:21
  320.3 84.3 %collective-permute-start = (bf16[2,240,4,256]{3,1,2,0:T(8,128)(2,1)S(1)}, bf16[2,240,4,256]{3,1,2,0:T(8,128)(2,1)S(1)}, u32[]{:S(2)}, u32[]{:S(2)}) collective-permute-start(bf16[2,240,4,256]{3,1,2,0:T(8,128)(2,1)S(1)} %pad_maximum_fusion.11), channel_id=1, source_target_pairs={{0,20},{4,24},{8,28},{1,21},{5,25},{9,29},{2,22},{6,26},{10,30},{3... | collective-permute-start | bytes 2949128 | tf_op jit(solution)/shard_map/ppermute | solution.py:21
  362.4 63.2 %collective-permute-start.1 = (bf16[2,240,4,256]{3,1,2,0:T(8,128)(2,1)S(1)}, bf16[2,240,4,256]{3,1,2,0:T(8,128)(2,1)S(1)}, u32[]{:S(2)}, u32[]{:S(2)}) collective-permute-start(bf16[2,240,4,256]{3,1,2,0:T(8,128)(2,1)S(1)} %pad_maximum_fusion.11), channel_id=1, source_target_pairs={{0,16},{4,20},{8,24},{12,28},{1,17},{5,21},{9,25},{13,29},{2,18},{... | collective-permute-start | bytes 2949128 | tf_op jit(solution)/shard_map/ppermute | solution.py:21
  369.2 57.5 %collective-permute-start.2 = (bf16[2,240,4,256]{3,1,2,0:T(8,128)(2,1)S(1)}, bf16[2,240,4,256]{3,1,2,0:T(8,128)(2,1)S(1)}, u32[]{:S(2)}, u32[]{:S(2)}) collective-permute-start(bf16[2,240,4,256]{3,1,2,0:T(8,128)(2,1)S(1)} %pad_maximum_fusion.11), channel_id=1, source_target_pairs={{0,12},{4,16},{8,20},{12,24},{16,28},{1,13},{5,17},{9,21},{13,25},... | collective-permute-start | bytes 2949128 | tf_op jit(solution)/shard_map/ppermute | solution.py:21
  370.6 57.1 %collective-permute-start.3 = (bf16[2,240,4,256]{3,1,2,0:T(8,128)(2,1)S(1)}, bf16[2,240,4,256]{3,1,2,0:T(8,128)(2,1)S(1)}, u32[]{:S(2)}, u32[]{:S(2)}) collective-permute-start(bf16[2,240,4,256]{3,1,2,0:T(8,128)(2,1)S(1)} %pad_maximum_fusion.11), channel_id=1, source_target_pairs={{0,8},{4,12},{8,16},{12,20},{16,24},{20,28},{1,9},{5,13},{9,17},{1... | collective-permute-start | bytes 2949128 | tf_op jit(solution)/shard_map/ppermute | solution.py:21
  372.1 56.8 %collective-permute-start.4 = (bf16[2,240,4,256]{3,1,2,0:T(8,128)(2,1)S(1)}, bf16[2,240,4,256]{3,1,2,0:T(8,128)(2,1)S(1)}, u32[]{:S(2)}, u32[]{:S(2)}) collective-permute-start(bf16[2,240,4,256]{3,1,2,0:T(8,128)(2,1)S(1)} %pad_maximum_fusion.11), channel_id=1, source_target_pairs={{0,4},{4,8},{8,12},{12,16},{16,20},{20,24},{24,28},{1,5},{5,9},{9,... | collective-permute-start | bytes 2949128 | tf_op jit(solution)/shard_map/ppermute | solution.py:21
  491.8 2926.6 %all-gather.30.cloned.1.call-start = ((), (), s32[]{:S(2)}) async-start(), calls=%async_computation.27 | async-start | bytes 19906560 | tf_op jit(solution)/shard_map/all_gather | solution.py:380
  535.4 2211.6 %copy-start = (f32[240,2304]{1,0:T(8,128)}, f32[240,2304]{1,0:T(8,128)S(1)}, u32[]{:S(2)}) copy-start(f32[240,2304]{1,0:T(8,128)S(1)} %get-tuple-element.98) | copy-start | bytes 6635524
  540.8 3210.0 %all-gather.26.cloned.1.call-start = ((), (), s32[]{:S(2)}) async-start(), calls=%async_computation.21 | async-start | bytes 19906560 | tf_op jit(solution)/shard_map/all_gather | solution.py:379
  2963.3 129.7 %collective-permute-start.10 = (bf16[2,240,4,256]{3,1,2,0:T(8,128)(2,1)}, bf16[2,240,4,256]{3,1,2,0:T(8,128)(2,1)}, u32[]{:S(2)}, u32[]{:S(2)}) collective-permute-start(bf16[2,240,4,256]{3,1,2,0:T(8,128)(2,1)} %get-tuple-element.105), channel_id=1, source_target_pairs={{4,0},{8,4},{12,8},{16,12},{20,16},{24,20},{28,24},{5,1},{9,5},{13... | collective-permute-start | bytes 2949128 | tf_op jit(solution)/shard_map/ppermute | solution.py:21
  2964.6 129.7 %collective-permute-start.11 = (bf16[2,240,4,256]{3,1,2,0:T(8,128)(2,1)}, bf16[2,240,4,256]{3,1,2,0:T(8,128)(2,1)}, u32[]{:S(2)}, u32[]{:S(2)}) collective-permute-start(bf16[2,240,4,256]{3,1,2,0:T(8,128)(2,1)} %get-tuple-element.109), channel_id=1, source_target_pairs={{8,0},{12,4},{16,8},{20,12},{24,16},{28,20},{9,1},{13,5},{17,9},{2... | collective-permute-start | bytes 2949128 | tf_op jit(solution)/shard_map/ppermute | solution.py:21
  2965.9 129.7 %collective-permute-start.12 = (bf16[2,240,4,256]{3,1,2,0:T(8,128)(2,1)}, bf16[2,240,4,256]{3,1,2,0:T(8,128)(2,1)}, u32[]{:S(2)}, u32[]{:S(2)}) collective-permute-start(bf16[2,240,4,256]{3,1,2,0:T(8,128)(2,1)} %get-tuple-element.108), channel_id=1, source_target_pairs={{12,0},{16,4},{20,8},{24,12},{28,16},{13,1},{17,5},{21,9},{25,13},... | collective-permute-start | bytes 2949128 | tf_op jit(solution)/shard_map/ppermute | solution.py:21
  2967.2 129.7 %collective-permute-start.13 = (bf16[2,240,4,256]{3,1,2,0:T(8,128)(2,1)}, bf16[2,240,4,256]{3,1,2,0:T(8,128)(2,1)}, u32[]{:S(2)}, u32[]{:S(2)}) collective-permute-start(bf16[2,240,4,256]{3,1,2,0:T(8,128)(2,1)} %get-tuple-element.107), channel_id=1, source_target_pairs={{16,0},{20,4},{24,8},{28,12},{17,1},{21,5},{25,9},{29,13},{18,2},{... | collective-permute-start | bytes 2949128 | tf_op jit(solution)/shard_map/ppermute | solution.py:21
  2968.5 129.7 %collective-permute-start.14 = (bf16[2,240,4,256]{3,1,2,0:T(8,128)(2,1)}, bf16[2,240,4,256]{3,1,2,0:T(8,128)(2,1)}, u32[]{:S(2)}, u32[]{:S(2)}) collective-permute-start(bf16[2,240,4,256]{3,1,2,0:T(8,128)(2,1)} %get-tuple-element.106), channel_id=1, source_target_pairs={{20,0},{24,4},{28,8},{21,1},{25,5},{29,9},{22,2},{26,6},{30,10},{2... | collective-permute-start | bytes 2949128 | tf_op jit(solution)/shard_map/ppermute | solution.py:21
  3093.0 11.8 collective-permute-start.15
  3094.3 45.9 %collective-permute-start.16 = (bf16[2,240,4,256]{3,1,2,0:T(8,128)(2,1)}, bf16[2,240,4,256]{3,1,2,0:T(8,128)(2,1)}, u32[]{:S(2)}, u32[]{:S(2)}) collective-permute-start(bf16[2,240,4,256]{3,1,2,0:T(8,128)(2,1)} %get-tuple-element.114), channel_id=1, source_target_pairs={{8,0},{12,4},{16,8},{20,12},{24,16},{28,20},{9,1},{13,5},{17,9},{2... | collective-permute-start | bytes 2949128 | tf_op jit(solution)/shard_map/ppermute | solution.py:21
  3095.6 47.0 %collective-permute-start.17 = (bf16[2,240,4,256]{3,1,2,0:T(8,128)(2,1)}, bf16[2,240,4,256]{3,1,2,0:T(8,128)(2,1)}, u32[]{:S(2)}, u32[]{:S(2)}) collective-permute-start(bf16[2,240,4,256]{3,1,2,0:T(8,128)(2,1)} %get-tuple-element.113), channel_id=1, source_target_pairs={{12,0},{16,4},{20,8},{24,12},{28,16},{13,1},{17,5},{21,9},{25,13},... | collective-permute-start | bytes 2949128 | tf_op jit(solution)/shard_map/ppermute | solution.py:21
  3096.9 50.2 %collective-permute-start.18 = (bf16[2,240,4,256]{3,1,2,0:T(8,128)(2,1)}, bf16[2,240,4,256]{3,1,2,0:T(8,128)(2,1)}, u32[]{:S(2)}, u32[]{:S(2)}) collective-permute-start(bf16[2,240,4,256]{3,1,2,0:T(8,128)(2,1)} %get-tuple-element.112), channel_id=1, source_target_pairs={{16,0},{20,4},{24,8},{28,12},{17,1},{21,5},{25,9},{29,13},{18,2},{... | collective-permute-start | bytes 2949128 | tf_op jit(solution)/shard_map/ppermute | solution.py:21
  3098.2 62.1 %collective-permute-start.19 = (bf16[2,240,4,256]{3,1,2,0:T(8,128)(2,1)}, bf16[2,240,4,256]{3,1,2,0:T(8,128)(2,1)}, u32[]{:S(2)}, u32[]{:S(2)}) collective-permute-start(bf16[2,240,4,256]{3,1,2,0:T(8,128)(2,1)} %get-tuple-element.111), channel_id=1, source_target_pairs={{20,0},{24,4},{28,8},{21,1},{25,5},{29,9},{22,2},{26,6},{30,10},{2... | collective-permute-start | bytes 2949128 | tf_op jit(solution)/shard_map/ppermute | solution.py:21
  3174.8 707.1 %all-gather.32.cloned.1.call-start = ((), (), s32[]{:S(2)}) async-start(), calls=%async_computation.30 | async-start | bytes 79626240 | tf_op jit(solution)/shard_map/all_gather | solution.py:382
  3186.7 76.1 %all-to-all-start.3 = ((bf16[480,8,288]{0,2,1:T(8,128)(2,1)}), bf16[480,8,288]{0,2,1:T(8,128)(2,1)S(1)}, u32[]{:S(2)}, u32[]{:S(2)}) async-start(bf16[480,8,288]{0,2,1:T(8,128)(2,1)} %bitcast.541), calls=%async_computation.6 | async-start | bytes 4718592 | tf_op jit(solution)/shard_map/all_to_all | solution.py:374
  3262.8 150.5 %all-to-all-start.5 = ((bf16[480,8,1152]{2,0,1:T(8,128)(2,1)}), bf16[480,8,1152]{2,0,1:T(8,128)(2,1)}, u32[]{:S(2)}, u32[]{:S(2)}) async-start(bf16[480,8,1152]{2,0,1:T(8,128)(2,1)} %bitcast.523), calls=%async_computation.10 | async-start | bytes 17694720 | tf_op jit(solution)/shard_map/all_to_all | solution.py:373
  3267.8 702.1 %reduce-scatter.14.cloned.1.call-start = ((), (), s32[]{:S(2)}) async-start(), calls=%async_computation.26 | async-start | bytes 1474560 | tf_op jit(solution)/shard_map/reduce_scatter | solution.py:405
  3413.3 183.0 %all-to-all-start.4 = ((bf16[480,8,1152]{2,0,1:T(8,128)(2,1)}), bf16[480,8,1152]{2,0,1:T(8,128)(2,1)}, u32[]{:S(2)}, u32[]{:S(2)}) async-start(bf16[480,8,1152]{2,0,1:T(8,128)(2,1)} %bitcast.522), calls=%async_computation.8 | async-start | bytes 17694720 | tf_op jit(solution)/shard_map/all_to_all | solution.py:372
  3418.3 591.9 %reduce-scatter.18.cloned.1.call-start = ((), (), s32[]{:S(2)}) async-start(), calls=%async_computation.29 | async-start | bytes 6635520 | tf_op jit(solution)/shard_map/reduce_scatter | solution.py:402
  3449.2 658.6 %reduce-scatter.16.cloned.1.call-start = ((), (), s32[]{:S(2)}) async-start(), calls=%async_computation.28 | async-start | bytes 6635520 | tf_op jit(solution)/shard_map/reduce_scatter | solution.py:399
  3628.0 29.8 all-to-all-start.2
  3657.8 29.8 all-to-all-start.1
  3687.6 58.6 %all-to-all-start.6 = ((bf16[480,8,288]{0,2,1:T(8,128)(2,1)}), bf16[480,8,288]{0,2,1:T(8,128)(2,1)S(1)}, u32[]{:S(2)}, u32[]{:S(2)}) async-start(bf16[480,8,288]{0,2,1:T(8,128)(2,1)} %bitcast.540), calls=%async_computation.12 | async-start | bytes 4718592 | tf_op jit(solution)/shard_map/all_to_all | solution.py:375
  3746.2 50.9 %all-to-all-start = ((bf16[480,8,256]{2,0,1:T(8,128)(2,1)}), bf16[480,8,256]{2,0,1:T(8,128)(2,1)}, u32[]{:S(2)}, u32[]{:S(2)}) async-start(bf16[480,8,256]{2,0,1:T(8,128)(2,1)} %pad_maximum_fusion.9), calls=%async_computation | async-start | bytes 3932160 | tf_op jit(solution)/shard_map/all_to_all | solution.py:369
  3750.5 381.9 %reduce-scatter.12.cloned.1.call-start = ((), (), s32[]{:S(2)}) async-start(), calls=%async_computation.24 | async-start | bytes 737280 | tf_op jit(solution)/shard_map/reduce_scatter | solution.py:396
  3762.6 392.7 %reduce-scatter.10.cloned.1.call-start = ((), (), s32[]{:S(2)}) async-start(), calls=%async_computation.23 | async-start | bytes 737280 | tf_op jit(solution)/shard_map/reduce_scatter | solution.py:393
  3782.4 403.4 %reduce-scatter.8.cloned.1.call-start = ((), (), s32[]{:S(2)}) async-start(), calls=%async_computation.22 | async-start | bytes 1474560 | tf_op jit(solution)/shard_map/reduce_scatter | solution.py:390
  3809.5 471.9 %reduce-scatter.20.cloned.1.call-start = ((), (), s32[]{:S(2)}) async-start(), calls=%async_computation.31 | async-start | bytes 6635520 | tf_op jit(solution)/shard_map/reduce_scatter | solution.py:408
  (122 other events, 2381.8 us)
Sparse Core Ops, SparseCore 0:
  9.6 92.0 all-gather.11
  103.3 87.8 all-gather.13
  192.8 165.2 all-gather.15
  359.5 164.9 all-gather.17
  525.9 706.4 all-gather.19
  1233.8 706.4 all-gather.21
  1941.9 706.4 all-gather.23
  2650.3 83.6 all-gather.27
  2735.9 93.7 all-gather.29
  3174.9 215.7 all-gather.25
  3392.6 489.2 all-gather.31
  3884.1 29.1 reduce-scatter.13
  3915.6 94.5 reduce-scatter.17
  4012.5 95.2 reduce-scatter.15
  4109.9 22.4 reduce-scatter.11
  4135.1 20.2 reduce-scatter.9
  4158.1 27.6 reduce-scatter.7
  4187.9 93.5 reduce-scatter.19
where the time goes:
time: 4300 us; the launch traced here: 4290 us
  waiting for transfers between devices  3050 us (71%)
  matrix products  647 us (15%)
  local copies, waits for them, and re-layouts  306 us (7%)
  other arithmetic  119 us (3%)
  starting transfers between devices  98.6 us (2%)
  blocking collectives  56.7 us (1%)
    all_gather x1, waiting for transfers between devices, fetch_ffn(): lax.all_gather(w_gate, 'fsdp', axis=0, tiled=True)  691 us
    all_gather x1, waiting for transfers between devices, fetch_ffn(): lax.all_gather(w_up, 'fsdp', axis=0, tiled=True)  679 us
    all_gather x1, waiting for transfers between devices, fetch_ffn(): lax.all_gather(w_down, 'fsdp', axis=0, tiled=True)  676 us
    ppermute x20, waiting for transfers between devices, shifted(): lax.ppermute(value, axis, [(source, source + steps) for source in range(i...  196 us
    dot_general x14, matrix products, final_dot(): return jnp.dot(left_side, right_side, preferred_element_type=jnp.float32)  183 us
    dot_general x14, matrix products, dot_back(): lax.dot_general(left_side, right_side, (((1,), (1,)), ((), ())), preferre...  172 us
    all_to_all x1, waiting for transfers between devices, on_device(): lax.all_to_all(grad_gate_all, 'seq', split_axis=1, concat_axis=0, tiled=T...  147 us
    dot_general x7, matrix products, dot_rows(): lax.dot_general(left_side, right_side, (((0,), (0,)), ((), ())), preferre...  139 us
  transfers between devices with their start and end apart: 45, of which 26 were waited for; matrix products, arithmetic and copies ran while one was open for 24% of the time, Pallas kernels for 0%

commit v1 on v0

v1 whole, which is shorter than its diff:
```python
import functools
import math

import jax
import jax.numpy as jnp
from jax import lax
from jax.experimental import pallas as pl
from jax.experimental.pallas import tpu as pltpu
from jax.sharding import PartitionSpec as P

QUERY_HEADS = 8
KEY_VALUE_HEADS = 4
HEAD_SIZE = 256
CAP = 50
WIN = 1024


epsilon = 1e-06


def shifted(value, axis, steps):
    count = lax.axis_size(axis)
    initial, last = (max(0, -steps), min(count, count - steps))
    return lax.ppermute(value, axis, [(source, source + steps) for source in range(initial, last)])


def rms_gain(stream, gain):
    return stream * lax.rsqrt(jnp.mean(stream * stream, axis=-1, keepdims=True) + epsilon) * gain


def geglu(gate_proj, up_proj):
    return jax.nn.gelu(gate_proj, approximate=True) * up_proj


def angles(position, size):
    frequency = 10000.0 ** (-jnp.arange(size // 2, dtype=jnp.float32) * 2.0 / size)
    phase_angle = position.astype(jnp.float32)[:, None] * frequency[None, :]
    return (jnp.cos(phase_angle)[:, None, :], jnp.sin(phase_angle)[:, None, :])


def rotate(value_rows, cosine_table, sine_table, direction):
    half_size = value_rows.shape[-1] // 2
    first_half = value_rows[..., :half_size]
    second = value_rows[..., half_size:]
    return jnp.concatenate(
        [
            first_half * cosine_table - direction * second * sine_table,
            second * cosine_table + direction * first_half * sine_table,
        ],
        axis=-1,
    )


def doc_starts(segment):
    lower = segment[None, :] < segment[:, None]
    return jnp.sum(lower.astype(jnp.int32), axis=1)


def final_dot(left_side, right_side):
    return jnp.dot(left_side, right_side, preferred_element_type=jnp.float32)


def dot_back(left_side, right_side):
    return lax.dot_general(
        left_side, right_side, (((1,), (1,)), ((), ())), preferred_element_type=jnp.float32
    )


def dot_rows(left_side, right_side):
    return lax.dot_general(
        left_side, right_side, (((0,), (0,)), ((), ())), preferred_element_type=jnp.float32
    )


def fetch_attention(w_query, key_weight, value_weight, w_out):
    return (
        lax.all_gather(w_query, "fsdp", axis=0, tiled=True),
        lax.all_gather(key_weight, "fsdp", axis=0, tiled=True),
        lax.all_gather(value_weight, "fsdp", axis=0, tiled=True),
        lax.all_gather(w_out, "fsdp", axis=0, tiled=True),
    )


def key_window(kv_pair, halo_count):
    arrived = [shifted(kv_pair, "seq", offset) for offset in range(halo_count, 0, -1)]
    return jnp.concatenate(arrived + [kv_pair], axis=1)


def window_grads(paired_gradient, halo_count, token_rows):
    summed = paired_gradient[:, halo_count * token_rows :]
    for offset in range(1, halo_count + 1):
        begin = (halo_count - offset) * token_rows
        summed = summed + shifted(
            paired_gradient[:, begin : begin + token_rows].astype(jnp.bfloat16), "seq", -offset
        ).astype(jnp.float32)
    return summed


def window_mask(seg_here, seg_whole, seq_place, token_rows, halo_count):
    padded = jnp.concatenate([jnp.full((halo_count * token_rows,), -1, jnp.int32), seg_whole])
    key_seg = lax.dynamic_slice_in_dim(
        padded, seq_place * token_rows, (halo_count + 1) * token_rows
    )
    query_pos = seq_place * token_rows + jnp.arange(token_rows, dtype=jnp.int32)
    key_pos = (
        seq_place * token_rows
        - halo_count * token_rows
        + jnp.arange((halo_count + 1) * token_rows, dtype=jnp.int32)
    )
    distance = query_pos[:, None] - key_pos[None, :]
    return (seg_here[:, None] == key_seg[None, :]) & (distance >= 0) & (distance < WIN)


def line_gather(rows):
    count = lax.axis_size("fsdp")
    place = lax.axis_index("fsdp")
    up, down = [rows], [rows]
    for hop in range(1, count):
        up.append(
            lax.ppermute(up[-1], "fsdp", [(i, i + 1) for i in range(hop - 1, count - 1)])
        )
        down.append(
            lax.ppermute(down[-1], "fsdp", [(i, i - 1) for i in range(1, count - hop + 1)])
        )

    def assemble(here, from_low, from_high):
        parts = [from_low[here - j] if j <= here else from_high[j - here] for j in range(count)]
        return jnp.concatenate(parts, axis=0)

    return lax.switch(
        place, [functools.partial(assemble, here) for here in range(count)], up, down
    )


def line_scatter(partial):
    count = lax.axis_size("fsdp")
    place = lax.axis_index("fsdp")
    rows = partial.shape[0] // count

    def piece(offset):
        index = jnp.clip(place + offset, 0, count - 1)
        return lax.dynamic_slice_in_dim(partial, index * rows, rows).astype(jnp.float32)

    total = piece(0)
    for sign in (1, -1):
        carried = None
        for hop in range(count - 1, 0, -1):
            running = piece(sign * hop)
            if carried is not None:
                running = running + carried.astype(jnp.float32)
            if sign > 0:
                pairs = [(i, i + 1) for i in range(count - hop)]
            else:
                pairs = [(i, i - 1) for i in range(hop, count)]
            carried = lax.ppermute(running.astype(jnp.bfloat16), "fsdp", pairs)
        if carried is not None:
            total = total + carried.astype(jnp.float32)
    return total


def gather_tokens(rows):
    return lax.all_gather(rows, "seq", axis=0, tiled=True)


def scatter_tokens(partial):
    return lax.psum_scatter(
        partial.astype(jnp.bfloat16), "seq", scatter_dimension=0, tiled=True
    ).astype(jnp.float32)


def swap_parts(value, split_axis, concat_axis):
    return lax.all_to_all(
        value, "seq", split_axis=split_axis, concat_axis=concat_axis, tiled=True
    )


def score_parts(query, key, low_bound, row_start, col_start):
    raw = lax.dot_general(
        query, key, (((1,), (1,)), ((), ())), preferred_element_type=jnp.float32
    )
    bent = jnp.tanh(raw * (1.0 / CAP))
    shape = raw.shape
    row = row_start + lax.broadcasted_iota(jnp.int32, shape, 0)
    col = col_start + lax.broadcasted_iota(jnp.int32, shape, 1)
    allowed = (col <= row) & (col >= low_bound)
    return bent, jnp.where(allowed, CAP * bent, -1e30)


def attend_kernel(block, reach, q_ref, k_ref, v_ref, low_ref, out_ref, log_ref):
    index = pl.program_id(0)

    def run(blocks):
        first = (index - (blocks - 1)) * block
        span = pl.ds(pl.multiple_of(first, block), blocks * block)
        _, capped = score_parts(
            q_ref[...], k_ref[span, :], low_ref[...], index * block, first
        )
        peak = jnp.max(capped, axis=-1, keepdims=True)
        power = jnp.exp(capped - peak)
        total = jnp.sum(power, axis=-1, keepdims=True)
        prob = (power * (1.0 / total)).astype(jnp.bfloat16)
        out = jnp.dot(prob, v_ref[span, :], preferred_element_type=jnp.float32)
        out_ref[...] = out.astype(jnp.bfloat16)
        log_ref[...] = peak + jnp.log(total)

    for blocks in range(1, reach + 1):
        if blocks < reach:
            pl.when(index == blocks - 1)(functools.partial(run, blocks))
        else:
            pl.when(index >= blocks - 1)(functools.partial(run, blocks))


def turn_back(value, cosine, sine):
    half = value.shape[-1] // 2
    first, second = value[:, :half], value[:, half:]
    return jnp.concatenate(
        [first * cosine + second * sine, second * cosine - first * sine], axis=-1
    )


def attend_back_kernel(
    block,
    reach,
    q_ref,
    k_ref,
    v_ref,
    g_ref,
    low_ref,
    log_ref,
    cos_ref,
    sin_ref,
    dq_ref,
    dk_ref,
    dv_ref,
):
    index = pl.program_id(0)
    steps = pl.num_programs(0)

    @pl.when(index == 0)
    def _():
        dk_ref[...] = jnp.zeros_like(dk_ref)
        dv_ref[...] = jnp.zeros_like(dv_ref)

    own = pl.ds(pl.multiple_of(index * block, block), block)

    def run(blocks):
        first = (index - (blocks - 1)) * block
        span = pl.ds(pl.multiple_of(first, block), blocks * block)
        query, grad = q_ref[...], g_ref[...]
        key = k_ref[span, :]
        bent, capped = score_parts(query, key, low_ref[...], index * block, first)
        prob = jnp.exp(capped - log_ref[...])
        grad_prob = lax.dot_general(
            grad, v_ref[span, :], (((1,), (1,)), ((), ())), preferred_element_type=jnp.float32
        )
        delta = jnp.sum(prob * grad_prob, axis=-1, keepdims=True)
        grad_score = (prob * (grad_prob - delta) * (1.0 - bent * bent)).astype(jnp.bfloat16)
        dq = jnp.dot(grad_score, key, preferred_element_type=jnp.float32)
        dq = dq * (1.0 / math.sqrt(HEAD_SIZE))
        dq_ref[...] = turn_back(dq, cos_ref[own, :], sin_ref[own, :]).astype(jnp.bfloat16)
        across = (((0,), (0,)), ((), ()))
        dk_ref[span, :] += lax.dot_general(
            grad_score, query, across, preferred_element_type=jnp.float32
        )
        dv_ref[span, :] += lax.dot_general(
            prob.astype(jnp.bfloat16), grad, across, preferred_element_type=jnp.float32
        )

    for blocks in range(1, reach + 1):
        if blocks < reach:
            pl.when(index == blocks - 1)(functools.partial(run, blocks))
        else:
            pl.when(index >= blocks - 1)(functools.partial(run, blocks))

    @pl.when(index == steps - 1)
    def _():
        dk_ref[...] = turn_back(dk_ref[...], cos_ref[...], sin_ref[...])


def block_shape(length):
    for block in (384, 256, 128):
        if length % block == 0:
            reach = min(length // block, (WIN - 1 + block - 1) // block + 1)
            return block, reach
    raise ValueError("sequence length")


def attend(query, key, value, low_bound):
    length = query.shape[0]
    block, reach = block_shape(length)
    whole = pl.BlockSpec((length, HEAD_SIZE), lambda i: (0, 0))
    rows = pl.BlockSpec((block, HEAD_SIZE), lambda i: (i, 0))
    line = pl.BlockSpec((block, 1), lambda i: (i, 0))
    area = block * block * reach * (length // block)
    return pl.pallas_call(
        functools.partial(attend_kernel, block, reach),
        grid=(length // block,),
        in_specs=[rows, whole, whole, line],
        out_specs=[rows, line],
        out_shape=[
            jax.ShapeDtypeStruct((length, HEAD_SIZE), jnp.bfloat16),
            jax.ShapeDtypeStruct((length, 1), jnp.float32),
        ],
        compiler_params=pltpu.CompilerParams(vmem_limit_bytes=40 * 2**20),
        cost_estimate=pl.CostEstimate(
            flops=4 * area * HEAD_SIZE, bytes_accessed=10 * length * HEAD_SIZE, transcendentals=2 * area
        ),
        name="attend",
    )(query, key, value, low_bound)


def attend_back(query, key, value, grad, low_bound, log_total, cosine, sine):
    length = query.shape[0]
    block, reach = block_shape(length)
    whole = pl.BlockSpec((length, HEAD_SIZE), lambda i: (0, 0))
    half = pl.BlockSpec((length, HEAD_SIZE // 2), lambda i: (0, 0))
    rows = pl.BlockSpec((block, HEAD_SIZE), lambda i: (i, 0))
    line = pl.BlockSpec((block, 1), lambda i: (i, 0))
    area = block * block * reach * (length // block)
    return pl.pallas_call(
        functools.partial(attend_back_kernel, block, reach),
        grid=(length // block,),
        in_specs=[rows, whole, whole, rows, line, line, half, half],
        out_specs=[rows, whole, whole],
        out_shape=[
            jax.ShapeDtypeStruct((length, HEAD_SIZE), jnp.bfloat16),
            jax.ShapeDtypeStruct((length, HEAD_SIZE), jnp.float32),
            jax.ShapeDtypeStruct((length, HEAD_SIZE), jnp.float32),
        ],
        compiler_params=pltpu.CompilerParams(vmem_limit_bytes=48 * 2**20),
        cost_estimate=pl.CostEstimate(
            flops=10 * area * HEAD_SIZE, bytes_accessed=24 * length * HEAD_SIZE, transcendentals=2 * area
        ),
        name="attend_back",
    )(query, key, value, grad, low_bound, log_total, cosine, sine)


class ByHeads:
    def __init__(self, w_query, key_weight, value_weight, w_out):
        place = lax.axis_index("seq")
        count = lax.axis_size("seq")
        layers = lax.axis_size("fsdp")
        half = HEAD_SIZE // 2

        def columns(weight, width):
            return lax.dynamic_slice_in_dim(weight, place * width, width, axis=1)

        joined = jnp.concatenate(
            [columns(w_query, HEAD_SIZE), columns(key_weight, half), columns(value_weight, half)],
            axis=1,
        )
        self.joined = line_gather(joined)
        own = self.joined[:, HEAD_SIZE:]
        other = lax.ppermute(own, "seq", [(i, i ^ 1) for i in range(count)])
        odd = place % 2 == 1
        low, high = jnp.where(odd, other, own), jnp.where(odd, own, other)
        self.weights = jnp.concatenate(
            [self.joined[:, :HEAD_SIZE], low[:, :half], high[:, :half], low[:, half:], high[:, half:]],
            axis=1,
        )
        depth = HEAD_SIZE // count
        here = QUERY_HEADS // layers
        part = w_out.reshape(here, count, depth, w_out.shape[1])
        part = lax.dynamic_index_in_dim(part, place, axis=1, keepdims=False)
        part = line_gather(part.reshape(here * depth, -1))
        self.out_rows = swap_parts(part, 0, 0)
        self.records = []

    def forward(self, normed, seg_whole):
        length = seg_whole.shape[0]
        whole = gather_tokens(normed)
        starts = doc_starts(seg_whole)
        places = jnp.arange(length, dtype=jnp.int32)
        low_bound = jnp.maximum(starts, places - (WIN - 1))[:, None]
        cosine, sine = angles(places - starts, HEAD_SIZE)
        cosine, sine = cosine[:, 0], sine[:, 0]
        rows = final_dot(whole, self.weights)
        query, key, value = (rows[:, HEAD_SIZE * i : HEAD_SIZE * (i + 1)] for i in range(3))
        query = rotate(query, cosine, sine, 1.0) * (1.0 / math.sqrt(HEAD_SIZE))
        query = query.astype(jnp.bfloat16)
        key = rotate(key, cosine, sine, 1.0).astype(jnp.bfloat16)
        value = value.astype(jnp.bfloat16)
        attended, log_total = attend(query, key, value, low_bound)
        mixed = scatter_tokens(final_dot(attended, self.out_rows))
        return mixed, (whole, query, key, value, low_bound, log_total, cosine, sine, attended)

    def backward(self, grad_mixed_b, saved):
        whole, query, key, value, low_bound, log_total, cosine, sine, attended = saved
        half = HEAD_SIZE // 2
        count = lax.axis_size("seq")
        grad_whole = gather_tokens(grad_mixed_b)
        grad_att = dot_back(grad_whole, self.out_rows).astype(jnp.bfloat16)
        dq, dk, dv = attend_back(
            query, key, value, grad_att, low_bound, log_total, cosine, sine
        )
        odd = lax.axis_index("seq") % 2 == 1
        low = jnp.concatenate([dk[:, :half], dv[:, :half]], axis=1)
        high = jnp.concatenate([dk[:, half:], dv[:, half:]], axis=1)
        away = jnp.where(odd, low, high)
        kept = jnp.where(odd, high, low)
        came = lax.ppermute(away, "seq", [(i, i ^ 1) for i in range(count)])
        dkv = (kept + came).astype(jnp.bfloat16)
        grads = jnp.concatenate([dq, dkv], axis=1)
        self.records.append((whole, grads, attended, grad_whole))
        return scatter_tokens(dot_back(grads, self.joined))

    def weight_grads(self):
        half = HEAD_SIZE // 2
        out = sum(dot_rows(r[2], r[3]) for r in self.records).astype(jnp.bfloat16)
        out = line_scatter(swap_parts(out, 1, 0))
        joined = sum(dot_rows(r[0], r[1]) for r in self.records).astype(jnp.bfloat16)
        joined = line_scatter(joined)
        return (
            joined[:, :HEAD_SIZE],
            joined[:, HEAD_SIZE : HEAD_SIZE + half],
            joined[:, HEAD_SIZE + half :],
            out,
        )


class ByTokens:
    def __init__(self, w_query, key_weight, value_weight, w_out):
        self.weights = fetch_attention(w_query, key_weight, value_weight, w_out)
        self.records = []

    def forward(self, normed, seg_whole):
        token_rows = normed.shape[0]
        halo_count = (WIN - 2 + token_rows) // token_rows
        w_query, key_weight, value_weight, w_out = self.weights
        seq_place = lax.axis_index("seq")
        seg_here = lax.dynamic_slice_in_dim(seg_whole, seq_place * token_rows, token_rows)
        position = jnp.arange(seg_whole.shape[0], dtype=jnp.int32) - doc_starts(seg_whole)
        position = lax.dynamic_slice_in_dim(position, seq_place * token_rows, token_rows)
        cosine, sine = angles(position, HEAD_SIZE)
        query = rotate(
            final_dot(normed, w_query).reshape(token_rows, QUERY_HEADS, HEAD_SIZE),
            cosine,
            sine,
            1.0,
        )
        query = (query * (1.0 / math.sqrt(HEAD_SIZE))).astype(jnp.bfloat16)
        key = rotate(
            final_dot(normed, key_weight).reshape(token_rows, KEY_VALUE_HEADS, HEAD_SIZE),
            cosine,
            sine,
            1.0,
        ).astype(jnp.bfloat16)
        value = final_dot(normed, value_weight).reshape(token_rows, KEY_VALUE_HEADS, HEAD_SIZE)
        pair = key_window(jnp.stack([key, value.astype(jnp.bfloat16)]), halo_count)
        allowed = window_mask(seg_here, seg_whole, seq_place, token_rows, halo_count)
        query = query.reshape(token_rows, KEY_VALUE_HEADS, -1, HEAD_SIZE)
        score = jnp.einsum("qhgd,khd->hgqk", query, pair[0], preferred_element_type=jnp.float32)
        capped = jnp.where(allowed, CAP * jnp.tanh(score / CAP), -jnp.inf)
        peak = jnp.max(capped, axis=-1, keepdims=True)
        power = jnp.exp(capped - peak)
        total = jnp.sum(power, axis=-1, keepdims=True)
        attended = jnp.einsum(
            "hgqk,khd->qhgd",
            (power / total).astype(jnp.bfloat16),
            pair[1],
            preferred_element_type=jnp.float32,
        )
        attended = attended.reshape(token_rows, QUERY_HEADS * HEAD_SIZE).astype(jnp.bfloat16)
        mixed = final_dot(attended, w_out)
        log_total = peak + jnp.log(total)
        return mixed, (normed, query, pair, allowed, log_total, cosine, sine, attended)

    def backward(self, grad_mixed_b, saved):
        normed, query, pair, allowed, log_total, cosine, sine, attended = saved
        token_rows = normed.shape[0]
        halo_count = (WIN - 2 + token_rows) // token_rows
        w_query, key_weight, value_weight, w_out = self.weights
        grad_att = dot_back(grad_mixed_b, w_out).astype(jnp.bfloat16)
        grad_att = grad_att.reshape(token_rows, KEY_VALUE_HEADS, -1, HEAD_SIZE)
        score = jnp.einsum("qhgd,khd->hgqk", query, pair[0], preferred_element_type=jnp.float32)
        bent = jnp.tanh(score / CAP)
        prob = jnp.exp(jnp.where(allowed, CAP * bent, -jnp.inf) - log_total)
        grad_prob = jnp.einsum(
            "qhgd,khd->hgqk", grad_att, pair[1], preferred_element_type=jnp.float32
        )
        delta = jnp.sum(prob * grad_prob, axis=-1, keepdims=True)
        grad_score = (prob * (grad_prob - delta) * (1.0 - bent * bent)).astype(jnp.bfloat16)
        dq = jnp.einsum("hgqk,khd->qhgd", grad_score, pair[0], preferred_element_type=jnp.float32)
        dk = jnp.einsum("hgqk,qhgd->khd", grad_score, query, preferred_element_type=jnp.float32)
        dv = jnp.einsum(
            "hgqk,qhgd->khd", prob.astype(jnp.bfloat16), grad_att, preferred_element_type=jnp.float32
        )
        paired = window_grads(jnp.stack([dk, dv]), halo_count, token_rows)
        dq = rotate(
            dq.reshape(token_rows, QUERY_HEADS, HEAD_SIZE) * (1.0 / math.sqrt(HEAD_SIZE)),
            cosine,
            sine,
            -1.0,
        )
        dq = dq.reshape(token_rows, -1).astype(jnp.bfloat16)
        dk = rotate(paired[0], cosine, sine, -1.0).reshape(token_rows, -1).astype(jnp.bfloat16)
        dv = paired[1].reshape(token_rows, -1).astype(jnp.bfloat16)
        self.records.append((normed, dq, dk, dv, attended, grad_mixed_b))
        return dot_back(dq, w_query) + dot_back(dk, key_weight) + dot_back(dv, value_weight)

    def weight_grads(self):
        normed, dq, dk, dv, attended, grad_mixed_b = (
            jnp.concatenate(parts, axis=0) for parts in zip(*self.records)
        )
        normed, attended = gather_tokens(normed), gather_tokens(attended)
        sums = []
        for rows, grads in ((normed, dq), (normed, dk), (normed, dv), (attended, grad_mixed_b)):
            column_sum = dot_rows(rows, swap_parts(grads, 1, 0)).astype(jnp.bfloat16)
            owned = lax.psum_scatter(column_sum, "fsdp", scatter_dimension=0, tiled=True)
            sums.append(owned.astype(jnp.float32))
        return tuple(sums)


class FeedForward:
    def __init__(self, w_gate, w_up, w_down):
        place = lax.axis_index("seq")
        count = lax.axis_size("seq")
        hidden = w_gate.shape[1]
        self.run = hidden // (count * count)

        def columns(weight):
            parts = [
                lax.dynamic_slice_in_dim(
                    weight, (t * count + place) * self.run, self.run, axis=1
                )
                for t in range(count)
            ]
            return jnp.concatenate(parts, axis=1)

        here = w_down.shape[0] // (count * self.run)
        part = w_down.reshape(here, count, self.run, w_down.shape[1])
        part = lax.dynamic_index_in_dim(part, place, axis=1, keepdims=False)
        self.gate = line_gather(columns(w_gate))
        self.up = line_gather(columns(w_up))
        self.down = line_gather(part.reshape(here * self.run, -1))
        self.records = []

    def forward(self, ffn_in):
        whole = gather_tokens(ffn_in)
        gate_proj = final_dot(whole, self.gate)
        up_proj = final_dot(whole, self.up)
        hidden = geglu(gate_proj, up_proj).astype(jnp.bfloat16)
        down_proj = scatter_tokens(final_dot(hidden, self.down))
        return down_proj, (whole, gate_proj, up_proj, hidden)

    def backward(self, grad_down_b, saved):
        whole, gate_proj, up_proj, hidden = saved
        grad_whole = gather_tokens(grad_down_b)
        grad_hidden = dot_back(grad_whole, self.down)
        _, pullback = jax.vjp(geglu, gate_proj, up_proj)
        grad_gate, grad_up = pullback(grad_hidden)
        grad_gate, grad_up = grad_gate.astype(jnp.bfloat16), grad_up.astype(jnp.bfloat16)
        self.records.append((whole, hidden, grad_whole, grad_gate, grad_up))
        return scatter_tokens(dot_back(grad_gate, self.gate) + dot_back(grad_up, self.up))

    def weight_grads(self):
        down = sum(dot_rows(r[1], r[2]) for r in self.records).astype(jnp.bfloat16)
        gate = sum(dot_rows(r[0], r[3]) for r in self.records).astype(jnp.bfloat16)
        up = sum(dot_rows(r[0], r[4]) for r in self.records).astype(jnp.bfloat16)
        count = lax.axis_size("seq")

        down = line_scatter(down).astype(jnp.bfloat16)
        here = down.shape[0] // self.run
        down = swap_parts(down.reshape(1, here, self.run, -1), 3, 0)
        down = down.transpose(1, 0, 2, 3).reshape(here * count * self.run, -1)

        def columns(summed):
            summed = line_scatter(summed).astype(jnp.bfloat16)
            return swap_parts(summed, 1, 1).astype(jnp.float32)

        return columns(gate), columns(up), down.astype(jnp.float32)


def on_device(
    tokens,
    segments,
    w_query,
    key_weight,
    value_weight,
    w_out,
    w_gate,
    w_up,
    w_down,
    gain_attn_in,
    gain_attn_out,
    gain_ffn_in,
    gain_ffn_out,
    cotangent,
):
    micro_count = tokens.shape[0]
    seg_gathered = lax.all_gather(segments, "seq", axis=2, tiled=True)
    by_heads = lax.axis_size("seq") == QUERY_HEADS and QUERY_HEADS % lax.axis_size("fsdp") == 0
    attention = (ByHeads if by_heads else ByTokens)(w_query, key_weight, value_weight, w_out)
    ffn = FeedForward(w_gate, w_up, w_down)
    results, input_grads = [], []
    gain_early = jnp.zeros((3, tokens.shape[3]), jnp.float32)
    gain_late = jnp.zeros((1, tokens.shape[3]), jnp.float32)
    for batch_index in range(micro_count):
        stream = tokens[batch_index, 0].astype(jnp.float32)
        normed = rms_gain(stream, gain_attn_in).astype(jnp.bfloat16)
        mixed, attention_saved = attention.forward(normed, seg_gathered[batch_index, 0])
        middle = stream + rms_gain(mixed, gain_attn_out)
        ffn_in = rms_gain(middle, gain_ffn_in).astype(jnp.bfloat16)
        down_proj, ffn_saved = ffn.forward(ffn_in)
        result = middle + rms_gain(down_proj, gain_ffn_out)
        results.append(result.astype(jnp.bfloat16))

        grad_result = cotangent[batch_index, 0].astype(jnp.float32)
        _, pullback = jax.vjp(rms_gain, down_proj, gain_ffn_out)
        grad_down, grad_gain_four = pullback(grad_result)
        grad_ffn_in = ffn.backward(grad_down.astype(jnp.bfloat16), ffn_saved)
        _, pullback = jax.vjp(rms_gain, middle, gain_ffn_in)
        grad_middle, grad_gain_three = pullback(grad_ffn_in)
        grad_middle = grad_result + grad_middle
        _, pullback = jax.vjp(rms_gain, mixed, gain_attn_out)
        grad_mixed, grad_gain_two = pullback(grad_middle)
        grad_normed = attention.backward(grad_mixed.astype(jnp.bfloat16), attention_saved)
        _, pullback = jax.vjp(rms_gain, stream, gain_attn_in)
        grad_stream, grad_gain_one = pullback(grad_normed)
        input_grads.append(grad_middle + grad_stream)
        gain_early = gain_early + jnp.stack([grad_gain_two, grad_gain_three, grad_gain_four])
        gain_late = gain_late + grad_gain_one[None]
    grad_gate, grad_up, grad_down = ffn.weight_grads()
    grad_query, grad_key, grad_value, grad_out = attention.weight_grads()
    gain_early = lax.psum(gain_early, ("seq", "fsdp"))
    gain_late = lax.psum(gain_late, ("seq", "fsdp"))
    return (
        jnp.stack(results)[:, None],
        jnp.stack(input_grads)[:, None],
        grad_query,
        grad_key,
        grad_value,
        grad_out,
        grad_gate,
        grad_up,
        grad_down,
        gain_late[0],
        gain_early[0],
        gain_early[1],
        gain_early[2],
    )


def solution(mesh):
    in_specs = (
        P(None, "fsdp", "seq", None),
        P(None, "fsdp", "seq"),
        P("fsdp", None),
        P("fsdp", None),
        P("fsdp", None),
        P("fsdp", None),
        P("fsdp", None),
        P("fsdp", None),
        P("fsdp", None),
        P(),
        P(),
        P(),
        P(),
        P(None, "fsdp", "seq", None),
    )
    out_specs = (
        P(None, "fsdp", "seq", None),
        P(None, "fsdp", "seq", None),
        P("fsdp", "seq"),
        P("fsdp", "seq"),
        P("fsdp", "seq"),
        P("fsdp", "seq"),
        P("fsdp", "seq"),
        P("fsdp", "seq"),
        P("fsdp", "seq"),
        P(),
        P(),
        P(),
        P(),
    )
    return jax.shard_map(
        on_device, mesh=mesh, in_specs=in_specs, out_specs=out_specs, check_vma=False
    )
```

time: 4300 us -> 1820 us (0.42)
  waiting for transfers between devices: 3050 us -> 719 us
  matrix products: 647 us -> 433 us
  local copies, waits for them, and re-layouts: 306 us -> 204 us
  starting transfers between devices: 98.6 us -> 199 us
  Pallas kernels: 0 us -> 46.7 us
    all_gather x11 -> x8, waiting for transfers between devices: 2150 us -> 55.9 us  [gather_tokens(): return lax.all_gather(rows, 'seq', axis=0, tiled=True)]
    all_to_all x7 -> x5, waiting for transfers between devices: 396 us -> 7.77 us  [swap_parts(): lax.all_to_all(value, 'seq', split_axis=split_axis, concat_axis=concat_ax...]
    dot_general x12 -> x0, matrix products: 154 us -> none  [the longest x2 55.1 us: backward_pass(): jnp.einsum('hgqk,qhgd->khd', grad_score_b, grouped_heads, preferred_eleme...]
    ppermute x20 -> x63, waiting for transfers between devices: 196 us -> 348 us  [the longest x15 178 us: line_gather(): lax.ppermute(down[-1], 'fsdp', [(i, i - 1) for i in range(1, count - hop...]
    ppermute x20 -> x63, starting transfers between devices: 38.4 us -> 178 us  [the longest x30 119 us: line_scatter(): carried = lax.ppermute(running.astype(jnp.bfloat16), 'fsdp', pairs)]
    slice x8 -> x10, local copies, waits for them, and re-layouts: 126 us -> 12.2 us  [the longest x4 4.31 us: backward(): high = jnp.concatenate([dk[:, half:], dv[:, half:]], axis=1)]
    pallas_call x0 -> x4, Pallas kernels: none -> 46.7 us  [the longest x2 30.5 us: attend_back(): pl.pallas_call(functools.partial(attend_back_kernel, block, reach), grid=...]
    dot_general x14 -> x10, matrix products: 183 us -> 137 us  [final_dot(): return jnp.dot(left_side, right_side, preferred_element_type=jnp.float32)]
  transfers between devices with their start and end apart: 45 -> 84, of which waited for: 26 -> 33; matrix products, arithmetic and copies ran while one was open for 24% -> 39% of each run, Pallas kernels for 0% -> 3%
where the time goes in v1:
time: 1820 us
  waiting for transfers between devices  719 us (40%)
  matrix products  433 us (24%)
  local copies, waits for them, and re-layouts  204 us (11%)
  starting transfers between devices  199 us (11%)
  other arithmetic  136 us (7%)
  blocking collectives  62 us (3%)
  Pallas kernels  46.7 us (3%)
    reduce_scatter x8, waiting for transfers between devices, scatter_tokens(): lax.psum_scatter(partial.astype(jnp.bfloat16), 'seq', scatter_dimension=0...  305 us
    ppermute x15, waiting for transfers between devices, line_gather(): lax.ppermute(down[-1], 'fsdp', [(i, i - 1) for i in range(1, count - hop...  178 us
    dot_general x10, matrix products, dot_back(): lax.dot_general(left_side, right_side, (((1,), (1,)), ((), ())), preferre...  163 us
    dot_general x10, matrix products, final_dot(): return jnp.dot(left_side, right_side, preferred_element_type=jnp.float32)  137 us
    dot_general x10, matrix products, dot_rows(): lax.dot_general(left_side, right_side, (((0,), (0,)), ((), ())), preferre...  133 us
    ppermute x30, starting transfers between devices, line_scatter(): carried = lax.ppermute(running.astype(jnp.bfloat16), 'fsdp', pairs)  119 us
    ppermute x30, waiting for transfers between devices, line_scatter(): carried = lax.ppermute(running.astype(jnp.bfloat16), 'fsdp', pairs)  118 us
    slice x1, local copies, waits for them, and re-layouts, on_device(): seg_gathered[batch_index, 0]  99 us
  transfers between devices with their start and end apart: 84, of which 33 were waited for; matrix products, arithmetic and copies ran while one was open for 39% of the time, Pallas kernels for 3%

profile of v1, /device:TPU:0, one launch (start us, length us, event | category | flops | bytes accessed | tf_op | source)
XLA Modules:
  0.0 1816.2 jit_solution(14016423653132929479)
XLA Ops:
  23.5 10.5 collective-permute-done.3
  46.4 16.0 all_gather.28
  64.4 99.0 %slice_reduce_fusion.1 = (s32[1920]{0:T(1024)S(1)}, s32[1920]{0:T(1024)S(1)}) fusion(s32[2,1,1920]{0,1,2:T(1,128)S(1)} %all_gather.28), kind=kLoop, calls=%fused_computation.260 | loop fusion | bytes 30720 | tf_op jit(solution)/shard_map/slice | solution.py:601
  185.5 10.9 collective-permute-done.9
  208.7 12.4 fusion.129
  221.1 10.7 fusion.127
  279.3 54.3 %reduce-scatter.13.cloned.1.call-done = bf16[240,2304]{1,0:T(8,128)(2,1)} async-done(((bf16[1920,2304]{1,0:T(8,128)(2,1)}), bf16[240,2304]{1,0:T(8,128)(2,1)}) %reduce-scatter.13.cloned.1.call-update) | async-done | bytes 1105936 | tf_op jit(solution)/shard_map/reduce_scatter | solution.py:166
  335.3 75.3 %reduce-scatter.9.cloned.1.call-done = bf16[240,2304]{1,0:T(8,128)(2,1)} async-done(((bf16[1920,2304]{1,0:T(8,128)(2,1)}), bf16[240,2304]{1,0:T(8,128)(2,1)}) %reduce-scatter.9.cloned.1.call-update) | async-done | bytes 1105936 | tf_op jit(solution)/shard_map/reduce_scatter | solution.py:166
  461.0 21.2 %collective-permute-done.16 = bf16[576,1152]{1,0:T(8,128)(2,1)} collective-permute-done((bf16[576,1152]{1,0:T(8,128)(2,1)}, bf16[576,1152]{1,0:T(8,128)(2,1)}, u32[]{:S(2)}, u32[]{:S(2)}) %collective-permute-start.16) | collective-permute-done | bytes 1327136 | tf_op jit(solution)/shard_map/ppermute | solution.py:120
  489.5 20.0 %collective-permute-done.22 = bf16[576,1152]{1,0:T(8,128)(2,1)S(1)} collective-permute-done((bf16[576,1152]{1,0:T(8,128)(2,1)}, bf16[576,1152]{1,0:T(8,128)(2,1)S(1)}, u32[]{:S(2)}, u32[]{:S(2)}) %collective-permute-start.22) | collective-permute-done | bytes 1327136 | tf_op jit(solution)/shard_map/ppermute | solution.py:120
  519.1 25.4 %collective-permute-done.26 = bf16[288,2304]{1,0:T(8,128)(2,1)S(1)} collective-permute-done((bf16[288,2304]{1,0:T(8,128)(2,1)}, bf16[288,2304]{1,0:T(8,128)(2,1)S(1)}, u32[]{:S(2)}, u32[]{:S(2)}) %collective-permute-start.26) | collective-permute-done | bytes 1327136 | tf_op jit(solution)/shard_map/ppermute | solution.py:123
  547.5 25.5 %collective-permute-done.14 = bf16[576,1152]{1,0:T(8,128)(2,1)} collective-permute-done((bf16[576,1152]{1,0:T(8,128)(2,1)}, bf16[576,1152]{1,0:T(8,128)(2,1)}, u32[]{:S(2)}, u32[]{:S(2)}) %collective-permute-start.14) | collective-permute-done | bytes 1327136 | tf_op jit(solution)/shard_map/ppermute | solution.py:123
  576.1 25.4 %collective-permute-done.20 = bf16[576,1152]{1,0:T(8,128)(2,1)} collective-permute-done((bf16[576,1152]{1,0:T(8,128)(2,1)S(1)}, bf16[576,1152]{1,0:T(8,128)(2,1)}, u32[]{:S(2)}, u32[]{:S(2)}) %collective-permute-start.20) | collective-permute-done | bytes 1327136 | tf_op jit(solution)/shard_map/ppermute | solution.py:123
  604.6 25.2 %collective-permute-done.27 = bf16[288,2304]{1,0:T(8,128)(2,1)S(1)} collective-permute-done((bf16[288,2304]{1,0:T(8,128)(2,1)S(1)}, bf16[288,2304]{1,0:T(8,128)(2,1)S(1)}, u32[]{:S(2)}, u32[]{:S(2)}) %collective-permute-start.27) | collective-permute-done | bytes 1327136 | tf_op jit(solution)/shard_map/ppermute | solution.py:123
  633.7 24.6 %collective-permute-done.15 = bf16[576,1152]{1,0:T(8,128)(2,1)} collective-permute-done((bf16[576,1152]{1,0:T(8,128)(2,1)}, bf16[576,1152]{1,0:T(8,128)(2,1)}, u32[]{:S(2)}, u32[]{:S(2)}) %collective-permute-start.15) | collective-permute-done | bytes 1327136 | tf_op jit(solution)/shard_map/ppermute | solution.py:123
  664.4 21.0 %collective-permute-done.21 = bf16[576,1152]{1,0:T(8,128)(2,1)} collective-permute-done((bf16[576,1152]{1,0:T(8,128)(2,1)}, bf16[576,1152]{1,0:T(8,128)(2,1)}, u32[]{:S(2)}, u32[]{:S(2)}) %collective-permute-start.21) | collective-permute-done | bytes 1327136 | tf_op jit(solution)/shard_map/ppermute | solution.py:123
  690.9 17.1 fusion.128
  708.0 18.4 %multiply_convert_fusion.3 = (bf16[1920,1152]{1,0:T(8,128)(2,1)S(1)}, f32[1920,1152]{1,0:T(8,128)}) fusion(f32[1920,1152]{1,0:T(8,128)} %fusion.128, bf16[1920,2304]{1,0:T(8,128)(2,1)} %all-gather.11.cloned.1.call-done, bf16[2304,1152]{1,0:T(8,128)(2,1)S(1)} %copy-done.51), kind=kOutput, calls=%fused_computation.69 | convolution fusion | flops 10214277120 | bytes 36274176 | tf_op jit(solution)/shard_map/dot_general | solution.py:60
  728.4 13.6 convolution_convert_fusion.4
  742.5 18.5 %fusion.130 = f32[1920,1152]{1,0:T(8,128)} fusion(bf16[1920,2304]{1,0:T(8,128)(2,1)} %all-gather.15.cloned.1.call-done, bf16[2304,1152]{1,0:T(8,128)(2,1)} %get-tuple-element.588), kind=kOutput, calls=%fused_computation.355 | convolution fusion | flops 10192158720 | bytes 23003136 | tf_op jit(solution)/shard_map/dot_general | solution.py:60
  761.0 18.3 %multiply_convert_fusion.2 = (bf16[1920,1152]{1,0:T(8,128)(2,1)}, f32[1920,1152]{1,0:T(8,128)}) fusion(f32[1920,1152]{1,0:T(8,128)} %fusion.130, bf16[1920,2304]{1,0:T(8,128)(2,1)S(1)} %copy-done.107, bf16[2304,1152]{1,0:T(8,128)(2,1)} %get-tuple-element.589), kind=kOutput, calls=%fused_computation.68 | convolution fusion | flops 10214277120 | bytes 36274176 | tf_op jit(solution)/shard_map/dot_general | solution.py:60
  779.4 16.3 convolution_convert_fusion.2
  795.9 17.0 reduce-scatter.11.cloned.1.call-done
  814.6 75.5 %reduce-scatter.15.cloned.1.call-done = bf16[240,2304]{1,0:T(8,128)(2,1)} async-done(((bf16[1920,2304]{1,0:T(8,128)(2,1)}), bf16[240,2304]{1,0:T(8,128)(2,1)}) %reduce-scatter.15.cloned.1.call-update) | async-done | bytes 1105936 | tf_op jit(solution)/shard_map/reduce_scatter | solution.py:166
  899.2 55.8 %all-gather.21.cloned.1.call-done = bf16[1920,2304]{1,0:T(8,128)(2,1)} async-done(((bf16[240,2304]{1,0:T(8,128)(2,1)}), bf16[1920,2304]{1,0:T(8,128)(2,1)}) %all-gather.21.cloned.1.call-update) | async-done | bytes 8847376 | tf_op jit(solution)/shard_map/all_gather | solution.py:162
  955.1 27.5 %fusion.16 = (bf16[1920,1152]{1,0:T(8,128)(2,1)}, bf16[1920,1152]{1,0:T(8,128)(2,1)}) fusion(f32[1920,1152]{1,0:T(8,128)} %fusion.130, f32[1920,1152]{1,0:T(8,128)} %get-tuple-element.570, bf16[1920,2304]{1,0:T(8,128)(2,1)} %all-gather.21.cloned.1.call-done, bf16[1152,2304]{1,0:T(8,128)(2,1)} %get-tuple-element.590), kind=kOutput, calls=%fused_computation.65 | convolution fusion | flops 10245242880 | bytes 40697856 | tf_op jit(solution)/shard_map/dot_general | solution.py:64
  982.5 17.6 fusion.132
  1000.1 20.0 %add_convert_fusion = bf16[1920,2304]{1,0:T(8,128)(2,1)} fusion(f32[1920,2304]{1,0:T(8,128)} %fusion.132, bf16[1920,1152]{1,0:T(8,128)(2,1)} %get-tuple-element.484, bf16[2304,1152]{1,0:T(8,128)(2,1)} %get-tuple-element.588), kind=kOutput, calls=%fused_computation.32 | convolution fusion | flops 10201006080 | bytes 36274176 | tf_op jit(solution)/shard_map/dot_general | solution.py:64
  1020.2 29.6 %fusion.9 = (bf16[1920,1152]{1,0:T(8,128)(2,1)}, bf16[1920,1152]{1,0:T(8,128)(2,1)}) fusion(f32[1920,1152]{1,0:T(8,128)} %fusion.128, f32[1920,1152]{1,0:T(8,128)} %get-tuple-element.572, bf16[1920,2304]{1,0:T(8,128)(2,1)} %all-gather.17.cloned.1.call-done, bf16[1152,2304]{1,0:T(8,128)(2,1)} %get-tuple-element.590), kind=kOutput, calls=%fused_computation.58 | convolution fusion | flops 10245242880 | bytes 40697856 | tf_op jit(solution)/shard_map/dot_general | solution.py:64
  1049.7 17.6 fusion.131
  1067.3 20.2 %add_convert_fusion.1 = bf16[1920,2304]{1,0:T(8,128)(2,1)} fusion(f32[1920,2304]{1,0:T(8,128)} %fusion.131, bf16[1920,1152]{1,0:T(8,128)(2,1)} %get-tuple-element.486, bf16[2304,1152]{1,0:T(8,128)(2,1)} %get-tuple-element.588), kind=kOutput, calls=%fused_computation.33 | convolution fusion | flops 10201006080 | bytes 36274176 | tf_op jit(solution)/shard_map/dot_general | solution.py:64
  1093.7 77.0 %reduce-scatter.17.cloned.1.call-done = bf16[240,2304]{1,0:T(8,128)(2,1)} async-done(((bf16[1920,2304]{1,0:T(8,128)(2,1)}), bf16[240,2304]{1,0:T(8,128)(2,1)}) %reduce-scatter.17.cloned.1.call-update) | async-done | bytes 1105936 | tf_op jit(solution)/shard_map/reduce_scatter | solution.py:166
  1187.6 17.1 fusion.136
  1204.8 15.3 fusion
  1229.4 15.6 fusion.135
  1251.5 15.5 attend_back.2
  1270.0 19.7 %fusion.2 = bf16[2304,1152]{1,0:T(8,128)(2,1)S(1)} fusion(f32[2304,1152]{1,0:T(8,128)} %fusion.135, bf16[1920,2304]{1,0:T(8,128)(2,1)} %all-gather.15.cloned.1.call-done, bf16[1920,1152]{1,0:T(8,128)(2,1)} %get-tuple-element.485), kind=kOutput, calls=%fused_computation.45 | convolution fusion | flops 10197467136 | bytes 29196288 | tf_op jit(solution)/shard_map/dot_general | solution.py:70
  1306.1 16.9 fusion.134
  1323.0 16.3 fusion.1
  1352.1 19.5 %collective-permute-done.45 = bf16[576,1152]{1,0:T(8,128)(2,1)S(1)} collective-permute-done((bf16[576,1152]{1,0:T(8,128)(2,1)S(1)}, bf16[576,1152]{1,0:T(8,128)(2,1)S(1)}, u32[]{:S(2)}, u32[]{:S(2)}) %collective-permute-start.45) | collective-permute-done | bytes 1327136 | tf_op jit(solution)/shard_map/ppermute | solution.py:155
  1385.1 15.0 attend_back.3
  1412.6 15.9 collective-permute-done.52
  1435.3 21.5 %collective-permute-done.46 = bf16[576,1152]{1,0:T(8,128)(2,1)S(1)} collective-permute-done((bf16[576,1152]{1,0:T(8,128)(2,1)S(1)}, bf16[576,1152]{1,0:T(8,128)(2,1)S(1)}, u32[]{:S(2)}, u32[]{:S(2)}) %collective-permute-start.46) | collective-permute-done | bytes 1327136 | tf_op jit(solution)/shard_map/ppermute | solution.py:155
  1483.4 13.3 collective-permute-start.47
  1533.4 21.0 %collective-permute-done.56 = bf16[576,1152]{1,0:T(8,128)(2,1)} collective-permute-done((bf16[576,1152]{1,0:T(8,128)(2,1)}, bf16[576,1152]{1,0:T(8,128)(2,1)}, u32[]{:S(2)}, u32[]{:S(2)}) %collective-permute-start.56) | collective-permute-done | bytes 1327136 | tf_op jit(solution)/shard_map/ppermute | solution.py:155
  1558.7 20.8 %collective-permute-done.50 = bf16[576,1152]{1,0:T(8,128)(2,1)} collective-permute-done((bf16[576,1152]{1,0:T(8,128)(2,1)}, bf16[576,1152]{1,0:T(8,128)(2,1)}, u32[]{:S(2)}, u32[]{:S(2)}) %collective-permute-start.50) | collective-permute-done | bytes 1327136 | tf_op jit(solution)/shard_map/ppermute | solution.py:155
  1590.6 29.2 %collective-permute-start.39 = (bf16[512,288]{0,1:T(8,128)(2,1)}, bf16[512,288]{0,1:T(8,128)(2,1)}, u32[]{:S(2)}, u32[]{:S(2)}) collective-permute-start(bf16[512,288]{0,1:T(8,128)(2,1)} %get-tuple-element.553), channel_id=1, source_target_pairs={{0,1},{4,5},{8,9},{12,13},{16,17},{20,21},{24,25},{28,29}} | collective-permute-start | bytes 884744 | tf_op jit(solution)/shard_map/ppermute | solution.py:155
  1756.3 45.9 %all-reduce = (f32[2304]{0:T(1024)}, f32[3,2304]{1,0:T(4,128)S(1)}) all-reduce(f32[2304]{0:T(1024)S(1)} %add.612, f32[3,2304]{1,0:T(4,128)S(1)} %maximum_add_fusion), channel_id=1, replica_groups=mesh['seq'=8,'fsdp'=4] {'seq','fsdp'}, use_global_device_ids=true, to_apply=%region_48.49 | all-reduce | flops 9216 | bytes 73728 | tf_op jit(solution)/shard_map/psum | solution.py:626
  (569 shorter events, 570.1 us)
Async XLA Ops:
  7.2 201.5 %all-gather.13.cloned.1.call-start = ((), (), s32[]{:S(2)}) async-start(), calls=%async_computation.17 | async-start | bytes 9953280 | tf_op jit(solution)/shard_map/all_gather | solution.py:162
  12.8 208.3 %all-gather.9.cloned.1.call-start = ((), (), s32[]{:S(2)}) async-start(), calls=%async_computation.13 | async-start | bytes 9953280 | tf_op jit(solution)/shard_map/all_gather | solution.py:162
  40.3 126.3 %collective-permute-start.10 = (bf16[64,2304]{1,0:T(8,128)(2,1)S(1)}, bf16[64,2304]{1,0:T(8,128)(2,1)S(1)}, u32[]{:S(2)}, u32[]{:S(2)}) collective-permute-start(bf16[64,2304]{1,0:T(8,128)(2,1)S(1)} %bitcast.183), channel_id=1, source_target_pairs={{0,1},{1,2},{2,3},{4,5},{5,6},{6,7},{8,9},{9,10},{10,11},{12,13},{... | collective-permute-start | bytes 884744 | tf_op jit(solution)/shard_map/ppermute | solution.py:120
  44.9 122.4 %collective-permute-start.7 = (bf16[64,2304]{1,0:T(8,128)(2,1)S(1)}, bf16[64,2304]{1,0:T(8,128)(2,1)S(1)}, u32[]{:S(2)}, u32[]{:S(2)}) collective-permute-start(bf16[64,2304]{1,0:T(8,128)(2,1)S(1)} %bitcast.184), channel_id=1, source_target_pairs={{1,0},{2,1},{3,2},{5,4},{6,5},{7,6},{9,8},{10,9},{11,10},{13,12},{... | collective-permute-start | bytes 884744 | tf_op jit(solution)/shard_map/ppermute | solution.py:123
  62.4 106.3 %collective-permute-start.5 = (bf16[576,512]{1,0:T(8,128)(2,1)}, bf16[576,512]{1,0:T(8,128)(2,1)S(1)}, u32[]{:S(2)}, u32[]{:S(2)}) collective-permute-start(bf16[576,512]{1,0:T(8,128)(2,1)} %collective-permute-done.4), channel_id=1, source_target_pairs={{2,3},{6,7},{10,11},{14,15},{18,19},{22,23},{26,27},{30,31}} | collective-permute-start | bytes 1769480 | tf_op jit(solution)/shard_map/ppermute | solution.py:120
  63.1 105.6 %collective-permute-start.2 = (bf16[576,512]{1,0:T(8,128)(2,1)}, bf16[576,512]{1,0:T(8,128)(2,1)}, u32[]{:S(2)}, u32[]{:S(2)}) collective-permute-start(bf16[576,512]{1,0:T(8,128)(2,1)} %collective-permute-done.1), channel_id=1, source_target_pairs={{1,0},{5,4},{9,8},{13,12},{17,16},{21,20},{25,24},{29,28}} | collective-permute-start | bytes 1769480 | tf_op jit(solution)/shard_map/ppermute | solution.py:123
  197.5 56.3 %all-to-all-start = ((bf16[8,32,2304]{2,1,0:T(8,128)(2,1)}), bf16[8,32,2304]{2,1,0:T(8,128)(2,1)S(1)}, u32[]{:S(2)}, u32[]{:S(2)}) async-start(bf16[8,32,2304]{2,1,0:T(8,128)(2,1)} %bitcast.197), calls=%async_computation | async-start | bytes 2359296 | tf_op jit(solution)/shard_map/all_to_all | solution.py:172
  201.1 132.6 %reduce-scatter.13.cloned.1.call-start = ((), (), s32[]{:S(2)}) async-start(), calls=%async_computation.18 | async-start | bytes 9953280 | tf_op jit(solution)/shard_map/reduce_scatter | solution.py:166
  259.7 150.9 %reduce-scatter.9.cloned.1.call-start = ((), (), s32[]{:S(2)}) async-start(), calls=%async_computation.14 | async-start | bytes 9953280 | tf_op jit(solution)/shard_map/reduce_scatter | solution.py:166
  279.1 411.7 %all-gather.11.cloned.1.call-start = ((), (), s32[]{:S(2)}) async-start(), calls=%async_computation.15 | async-start | bytes 9953280 | tf_op jit(solution)/shard_map/all_gather | solution.py:162
  418.7 323.8 %all-gather.15.cloned.1.call-start = ((), (), s32[]{:S(2)}) async-start(), calls=%async_computation.19 | async-start | bytes 9953280 | tf_op jit(solution)/shard_map/all_gather | solution.py:162
  419.3 393.6 %reduce-scatter.11.cloned.1.call-start = ((), (), s32[]{:S(2)}) async-start(), calls=%async_computation.16 | async-start | bytes 9953280 | tf_op jit(solution)/shard_map/reduce_scatter | solution.py:166
  450.5 59.0 %collective-permute-start.22 = (bf16[576,1152]{1,0:T(8,128)(2,1)}, bf16[576,1152]{1,0:T(8,128)(2,1)S(1)}, u32[]{:S(2)}, u32[]{:S(2)}) collective-permute-start(bf16[576,1152]{1,0:T(8,128)(2,1)} %concatenate.113), channel_id=1, source_target_pairs={{0,1},{1,2},{2,3},{4,5},{5,6},{6,7},{8,9},{9,10},{10,11},{12,13},{... | collective-permute-start | bytes 3981320 | tf_op jit(solution)/shard_map/ppermute | solution.py:120
  455.3 60.8 %collective-permute-start.19 = (bf16[576,1152]{1,0:T(8,128)(2,1)}, bf16[576,1152]{1,0:T(8,128)(2,1)S(1)}, u32[]{:S(2)}, u32[]{:S(2)}) collective-permute-start(bf16[576,1152]{1,0:T(8,128)(2,1)} %concatenate.113), channel_id=1, source_target_pairs={{1,0},{2,1},{3,2},{5,4},{6,5},{7,6},{9,8},{10,9},{11,10},{13,12},{... | collective-permute-start | bytes 3981320 | tf_op jit(solution)/shard_map/ppermute | solution.py:123
  459.3 58.5 %collective-permute-start.29 = (bf16[288,2304]{1,0:T(8,128)(2,1)}, bf16[288,2304]{1,0:T(8,128)(2,1)}, u32[]{:S(2)}, u32[]{:S(2)}) collective-permute-start(bf16[288,2304]{1,0:T(8,128)(2,1)} %collective-permute-done.28), channel_id=1, source_target_pairs={{1,2},{2,3},{5,6},{6,7},{9,10},{10,11},{13,14},{14,15},{17,18},{18... | collective-permute-start | bytes 3981320 | tf_op jit(solution)/shard_map/ppermute | solution.py:120
  482.2 62.3 %collective-permute-start.26 = (bf16[288,2304]{1,0:T(8,128)(2,1)}, bf16[288,2304]{1,0:T(8,128)(2,1)S(1)}, u32[]{:S(2)}, u32[]{:S(2)}) collective-permute-start(bf16[288,2304]{1,0:T(8,128)(2,1)} %collective-permute-done.25), channel_id=1, source_target_pairs={{1,0},{2,1},{5,4},{6,5},{9,8},{10,9},{13,12},{14,13},{17,16},{18,1... | collective-permute-start | bytes 3981320 | tf_op jit(solution)/shard_map/ppermute | solution.py:123
  487.7 58.5 %collective-permute-start.17 = (bf16[576,1152]{1,0:T(8,128)(2,1)}, bf16[576,1152]{1,0:T(8,128)(2,1)}, u32[]{:S(2)}, u32[]{:S(2)}) collective-permute-start(bf16[576,1152]{1,0:T(8,128)(2,1)} %collective-permute-done.16), channel_id=1, source_target_pairs={{1,2},{2,3},{5,6},{6,7},{9,10},{10,11},{13,14},{14,15},{17,18},{18... | collective-permute-start | bytes 3981320 | tf_op jit(solution)/shard_map/ppermute | solution.py:120
  509.5 63.6 %collective-permute-start.14 = (bf16[576,1152]{1,0:T(8,128)(2,1)}, bf16[576,1152]{1,0:T(8,128)(2,1)}, u32[]{:S(2)}, u32[]{:S(2)}) collective-permute-start(bf16[576,1152]{1,0:T(8,128)(2,1)} %collective-permute-done.13), channel_id=1, source_target_pairs={{1,0},{2,1},{5,4},{6,5},{9,8},{10,9},{13,12},{14,13},{17,16},{18,1... | collective-permute-start | bytes 3981320 | tf_op jit(solution)/shard_map/ppermute | solution.py:123
  516.1 58.7 %collective-permute-start.23 = (bf16[576,1152]{1,0:T(8,128)(2,1)S(1)}, bf16[576,1152]{1,0:T(8,128)(2,1)}, u32[]{:S(2)}, u32[]{:S(2)}) collective-permute-start(bf16[576,1152]{1,0:T(8,128)(2,1)S(1)} %collective-permute-done.22), channel_id=1, source_target_pairs={{1,2},{2,3},{5,6},{6,7},{9,10},{10,11},{13,14},{14,15},{17,18},{18... | collective-permute-start | bytes 3981320 | tf_op jit(solution)/shard_map/ppermute | solution.py:120
  517.8 83.7 %collective-permute-start.20 = (bf16[576,1152]{1,0:T(8,128)(2,1)S(1)}, bf16[576,1152]{1,0:T(8,128)(2,1)}, u32[]{:S(2)}, u32[]{:S(2)}) collective-permute-start(bf16[576,1152]{1,0:T(8,128)(2,1)S(1)} %collective-permute-done.19), channel_id=1, source_target_pairs={{1,0},{2,1},{5,4},{6,5},{9,8},{10,9},{13,12},{14,13},{17,16},{18,1... | collective-permute-start | bytes 3981320 | tf_op jit(solution)/shard_map/ppermute | solution.py:123
  544.5 58.8 %collective-permute-start.30 = (bf16[288,2304]{1,0:T(8,128)(2,1)}, bf16[288,2304]{1,0:T(8,128)(2,1)}, u32[]{:S(2)}, u32[]{:S(2)}) collective-permute-start(bf16[288,2304]{1,0:T(8,128)(2,1)} %collective-permute-done.29), channel_id=1, source_target_pairs={{2,3},{6,7},{10,11},{14,15},{18,19},{22,23},{26,27},{30,31}} | collective-permute-start | bytes 3981320 | tf_op jit(solution)/shard_map/ppermute | solution.py:120
  546.2 83.6 %collective-permute-start.27 = (bf16[288,2304]{1,0:T(8,128)(2,1)S(1)}, bf16[288,2304]{1,0:T(8,128)(2,1)S(1)}, u32[]{:S(2)}, u32[]{:S(2)}) collective-permute-start(bf16[288,2304]{1,0:T(8,128)(2,1)S(1)} %collective-permute-done.26), channel_id=1, source_target_pairs={{1,0},{5,4},{9,8},{13,12},{17,16},{21,20},{25,24},{29,28}} | collective-permute-start | bytes 3981320 | tf_op jit(solution)/shard_map/ppermute | solution.py:123
  573.0 60.7 %collective-permute-start.18 = (bf16[576,1152]{1,0:T(8,128)(2,1)}, bf16[576,1152]{1,0:T(8,128)(2,1)}, u32[]{:S(2)}, u32[]{:S(2)}) collective-permute-start(bf16[576,1152]{1,0:T(8,128)(2,1)} %collective-permute-done.17), channel_id=1, source_target_pairs={{2,3},{6,7},{10,11},{14,15},{18,19},{22,23},{26,27},{30,31}} | collective-permute-start | bytes 3981320 | tf_op jit(solution)/shard_map/ppermute | solution.py:120
  574.8 83.6 %collective-permute-start.15 = (bf16[576,1152]{1,0:T(8,128)(2,1)}, bf16[576,1152]{1,0:T(8,128)(2,1)}, u32[]{:S(2)}, u32[]{:S(2)}) collective-permute-start(bf16[576,1152]{1,0:T(8,128)(2,1)} %collective-permute-done.14), channel_id=1, source_target_pairs={{1,0},{5,4},{9,8},{13,12},{17,16},{21,20},{25,24},{29,28}} | collective-permute-start | bytes 3981320 | tf_op jit(solution)/shard_map/ppermute | solution.py:123
  601.5 62.9 %collective-permute-start.24 = (bf16[576,1152]{1,0:T(8,128)(2,1)}, bf16[576,1152]{1,0:T(8,128)(2,1)}, u32[]{:S(2)}, u32[]{:S(2)}) collective-permute-start(bf16[576,1152]{1,0:T(8,128)(2,1)} %collective-permute-done.23), channel_id=1, source_target_pairs={{2,3},{6,7},{10,11},{14,15},{18,19},{22,23},{26,27},{30,31}} | collective-permute-start | bytes 3981320 | tf_op jit(solution)/shard_map/ppermute | solution.py:120
  603.3 82.0 %collective-permute-start.21 = (bf16[576,1152]{1,0:T(8,128)(2,1)}, bf16[576,1152]{1,0:T(8,128)(2,1)}, u32[]{:S(2)}, u32[]{:S(2)}) collective-permute-start(bf16[576,1152]{1,0:T(8,128)(2,1)} %collective-permute-done.20), channel_id=1, source_target_pairs={{1,0},{5,4},{9,8},{13,12},{17,16},{21,20},{25,24},{29,28}} | collective-permute-start | bytes 3981320 | tf_op jit(solution)/shard_map/ppermute | solution.py:123
  742.0 148.1 %reduce-scatter.15.cloned.1.call-start = ((), (), s32[]{:S(2)}) async-start(), calls=%async_computation.20 | async-start | bytes 9953280 | tf_op jit(solution)/shard_map/reduce_scatter | solution.py:166
  795.7 159.4 %all-gather.21.cloned.1.call-start = ((), (), s32[]{:S(2)}) async-start(), calls=%async_computation.25 | async-start | bytes 9953280 | tf_op jit(solution)/shard_map/all_gather | solution.py:162
  898.6 121.6 %all-gather.17.cloned.1.call-start = ((), (), s32[]{:S(2)}) async-start(), calls=%async_computation.21 | async-start | bytes 9953280 | tf_op jit(solution)/shard_map/all_gather | solution.py:162
  899.2 194.6 %reduce-scatter.21.cloned.1.call-start = ((), (), s32[]{:S(2)}) async-start(), calls=%async_computation.26 | async-start | bytes 9953280 | tf_op jit(solution)/shard_map/reduce_scatter | solution.py:166
  1020.1 150.7 %reduce-scatter.17.cloned.1.call-start = ((), (), s32[]{:S(2)}) async-start(), calls=%async_computation.22 | async-start | bytes 9953280 | tf_op jit(solution)/shard_map/reduce_scatter | solution.py:166
  1087.7 157.4 %all-gather.19.cloned.1.call-start = ((), (), s32[]{:S(2)}) async-start(), calls=%async_computation.23 | async-start | bytes 9953280 | tf_op jit(solution)/shard_map/all_gather | solution.py:162
  1186.9 191.8 %all-gather.23.cloned.1.call-start = ((), (), s32[]{:S(2)}) async-start(), calls=%async_computation.27 | async-start | bytes 9953280 | tf_op jit(solution)/shard_map/all_gather | solution.py:162
  1187.5 565.4 %reduce-scatter.19.cloned.1.call-start = ((), (), s32[]{:S(2)}) async-start(), calls=%async_computation.24 | async-start | bytes 9953280 | tf_op jit(solution)/shard_map/reduce_scatter | solution.py:166
  1223.2 118.9 %collective-permute-start.57 = (bf16[288,2304]{1,0:T(8,128)(2,1)}, bf16[288,2304]{1,0:T(8,128)(2,1)}, u32[]{:S(2)}, u32[]{:S(2)}) collective-permute-start(bf16[288,2304]{1,0:T(8,128)(2,1)} %get-tuple-element.514), channel_id=1, source_target_pairs={{0,1},{4,5},{8,9},{12,13},{16,17},{20,21},{24,25},{28,29}} | collective-permute-start | bytes 3981320 | tf_op jit(solution)/shard_map/ppermute | solution.py:155
  1227.7 175.3 %collective-permute-start.60 = (bf16[288,2304]{1,0:T(8,128)(2,1)}, bf16[288,2304]{1,0:T(8,128)(2,1)}, u32[]{:S(2)}, u32[]{:S(2)}) collective-permute-start(bf16[288,2304]{1,0:T(8,128)(2,1)} %get-tuple-element.515), channel_id=1, source_target_pairs={{3,2},{7,6},{11,10},{15,14},{19,18},{23,22},{27,26},{31,30}} | collective-permute-start | bytes 3981320 | tf_op jit(solution)/shard_map/ppermute | solution.py:155
  1294.2 115.8 %collective-permute-start.54 = (bf16[576,1152]{1,0:T(8,128)(2,1)}, bf16[576,1152]{1,0:T(8,128)(2,1)}, u32[]{:S(2)}, u32[]{:S(2)}) collective-permute-start(bf16[576,1152]{1,0:T(8,128)(2,1)} %get-tuple-element.519), channel_id=1, source_target_pairs={{3,2},{7,6},{11,10},{15,14},{19,18},{23,22},{27,26},{31,30}} | collective-permute-start | bytes 3981320 | tf_op jit(solution)/shard_map/ppermute | solution.py:155
  1306.1 446.8 %reduce-scatter.23.cloned.1.call-start = ((), (), s32[]{:S(2)}) async-start(), calls=%async_computation.28 | async-start | bytes 9953280 | tf_op jit(solution)/shard_map/reduce_scatter | solution.py:166
  1342.1 91.5 %collective-permute-start.48 = (bf16[576,1152]{1,0:T(8,128)(2,1)}, bf16[576,1152]{1,0:T(8,128)(2,1)}, u32[]{:S(2)}, u32[]{:S(2)}) collective-permute-start(bf16[576,1152]{1,0:T(8,128)(2,1)} %get-tuple-element.523), channel_id=1, source_target_pairs={{3,2},{7,6},{11,10},{15,14},{19,18},{23,22},{27,26},{31,30}} | collective-permute-start | bytes 3981320 | tf_op jit(solution)/shard_map/ppermute | solution.py:155
  1347.0 59.3 %collective-permute-start.58 = (bf16[288,2304]{1,0:T(8,128)(2,1)}, bf16[288,2304]{1,0:T(8,128)(2,1)}, u32[]{:S(2)}, u32[]{:S(2)}) collective-permute-start(bf16[288,2304]{1,0:T(8,128)(2,1)} %add_convert_fusion.6), channel_id=1, source_target_pairs={{0,1},{1,2},{4,5},{5,6},{8,9},{9,10},{12,13},{13,14},{16,17},{17,1... | collective-permute-start | bytes 3981320 | tf_op jit(solution)/shard_map/ppermute | solution.py:155
  1371.5 57.0 %collective-permute-start.52 = (bf16[576,1152]{1,0:T(8,128)(2,1)}, bf16[576,1152]{1,0:T(8,128)(2,1)}, u32[]{:S(2)}, u32[]{:S(2)}) collective-permute-start(bf16[576,1152]{1,0:T(8,128)(2,1)} %add_convert_fusion.11), channel_id=1, source_target_pairs={{0,1},{1,2},{4,5},{5,6},{8,9},{9,10},{12,13},{13,14},{16,17},{17,1... | collective-permute-start | bytes 3981320 | tf_op jit(solution)/shard_map/ppermute | solution.py:155
  1406.3 55.8 %collective-permute-start.32 = (f32[1920,256]{1,0:T(8,128)S(1)}, f32[1920,256]{1,0:T(8,128)S(1)}, u32[]{:S(2)}, u32[]{:S(2)}) collective-permute-start(f32[1920,256]{1,0:T(8,128)S(1)} %fusion.73), channel_id=1, source_target_pairs={{0,4},{4,0},{8,12},{12,8},{16,20},{20,16},{24,28},{28,24},{1,5},{5... | collective-permute-start | bytes 5898248 | tf_op jit(solution)/shard_map/ppermute | solution.py:401
  1410.0 94.4 %collective-permute-start.59 = (bf16[288,2304]{1,0:T(8,128)(2,1)S(1)}, bf16[288,2304]{1,0:T(8,128)(2,1)}, u32[]{:S(2)}, u32[]{:S(2)}) collective-permute-start(bf16[288,2304]{1,0:T(8,128)(2,1)S(1)} %get-tuple-element.512), channel_id=1, source_target_pairs={{0,1},{1,2},{2,3},{4,5},{5,6},{6,7},{8,9},{9,10},{10,11},{12,13},{... | collective-permute-start | bytes 3981320 | tf_op jit(solution)/shard_map/ppermute | solution.py:155
  1477.8 55.6 %collective-permute-start.53 = (bf16[576,1152]{1,0:T(8,128)(2,1)}, bf16[576,1152]{1,0:T(8,128)(2,1)}, u32[]{:S(2)}, u32[]{:S(2)}) collective-permute-start(bf16[576,1152]{1,0:T(8,128)(2,1)} %get-tuple-element.516), channel_id=1, source_target_pairs={{0,1},{1,2},{2,3},{4,5},{5,6},{6,7},{8,9},{9,10},{10,11},{12,13},{... | collective-permute-start | bytes 3981320 | tf_op jit(solution)/shard_map/ppermute | solution.py:155
  1483.4 75.3 %collective-permute-start.47 = (bf16[576,1152]{1,0:T(8,128)(2,1)}, bf16[576,1152]{1,0:T(8,128)(2,1)}, u32[]{:S(2)}, u32[]{:S(2)}) collective-permute-start(bf16[576,1152]{1,0:T(8,128)(2,1)} %get-tuple-element.520), channel_id=1, source_target_pairs={{0,1},{1,2},{2,3},{4,5},{5,6},{6,7},{8,9},{9,10},{10,11},{12,13},{... | collective-permute-start | bytes 3981320 | tf_op jit(solution)/shard_map/ppermute | solution.py:155
  1500.0 54.3 %collective-permute-start.56 = (bf16[576,1152]{1,0:T(8,128)(2,1)}, bf16[576,1152]{1,0:T(8,128)(2,1)}, u32[]{:S(2)}, u32[]{:S(2)}) collective-permute-start(bf16[576,1152]{1,0:T(8,128)(2,1)} %add_convert_fusion.8), channel_id=1, source_target_pairs={{1,0},{2,1},{3,2},{5,4},{6,5},{7,6},{9,8},{10,9},{11,10},{13,12},{... | collective-permute-start | bytes 3981320 | tf_op jit(solution)/shard_map/ppermute | solution.py:155
  1504.4 75.1 %collective-permute-start.50 = (bf16[576,1152]{1,0:T(8,128)(2,1)}, bf16[576,1152]{1,0:T(8,128)(2,1)}, u32[]{:S(2)}, u32[]{:S(2)}) collective-permute-start(bf16[576,1152]{1,0:T(8,128)(2,1)} %add_convert_fusion.13), channel_id=1, source_target_pairs={{1,0},{2,1},{3,2},{5,4},{6,5},{7,6},{9,8},{10,9},{11,10},{13,12},{... | collective-permute-start | bytes 3981320 | tf_op jit(solution)/shard_map/ppermute | solution.py:155
  1590.6 72.3 %collective-permute-start.39 = (bf16[512,288]{0,1:T(8,128)(2,1)}, bf16[512,288]{0,1:T(8,128)(2,1)}, u32[]{:S(2)}, u32[]{:S(2)}) collective-permute-start(bf16[512,288]{0,1:T(8,128)(2,1)} %get-tuple-element.553), channel_id=1, source_target_pairs={{0,1},{4,5},{8,9},{12,13},{16,17},{20,21},{24,25},{28,29}} | collective-permute-start | bytes 884744 | tf_op jit(solution)/shard_map/ppermute | solution.py:155
  (163 other events, 4100.9 us)
Sparse Core Ops, SparseCore 0:
  12.9 62.9 all-gather.12
  77.8 56.3 all-gather.8
  259.8 73.7 reduce-scatter.12
  337.1 73.5 reduce-scatter.8
  418.8 56.3 all-gather.10
  476.9 56.3 all-gather.14
  742.1 70.7 reduce-scatter.10
  816.5 73.5 reduce-scatter.14
  898.7 56.2 all-gather.20
  957.4 56.3 all-gather.16
  1020.2 73.4 reduce-scatter.20
  1097.2 73.5 reduce-scatter.16
  1187.0 56.3 all-gather.18
  1245.1 56.3 all-gather.22
  1306.2 72.2 reduce-scatter.18
  1472.2 83.4 reduce-scatter.22

commit v2 on v1

--- a/solution.py
+++ b/solution.py
@@ -13,6 +13,9 @@
 HEAD_SIZE = 256
 CAP = 50
 WIN = 1024
+DOCUMENTS = 4
+VMEM_LIMIT = 60 * 2**20
+SPAN_BYTES = 270_000_000
 
 
 epsilon = 1e-06
@@ -34,8 +37,8 @@
 
 def angles(position, size):
     frequency = 10000.0 ** (-jnp.arange(size // 2, dtype=jnp.float32) * 2.0 / size)
-    phase_angle = position.astype(jnp.float32)[:, None] * frequency[None, :]
-    return (jnp.cos(phase_angle)[:, None, :], jnp.sin(phase_angle)[:, None, :])
+    phase_angle = position.astype(jnp.float32)[..., None] * frequency
+    return (jnp.cos(phase_angle), jnp.sin(phase_angle))
 
 
 def rotate(value_rows, cosine_table, sine_table, direction):
@@ -52,8 +55,11 @@
 
 
 def doc_starts(segment):
-    lower = segment[None, :] < segment[:, None]
-    return jnp.sum(lower.astype(jnp.int32), axis=1)
+    starts = jnp.zeros_like(segment)
+    for number in range(1, DOCUMENTS):
+        count = jnp.sum((segment < number).astype(jnp.int32), axis=-1, keepdims=True)
+        starts = jnp.where(segment >= number, count, starts)
+    return starts
 
 
 def final_dot(left_side, right_side):
@@ -61,12 +67,13 @@
 
 
 def dot_back(left_side, right_side):
-    return lax.dot_general(
-        left_side, right_side, (((1,), (1,)), ((), ())), preferred_element_type=jnp.float32
-    )
+    contract = (((left_side.ndim - 1,), (1,)), ((), ()))
+    return lax.dot_general(left_side, right_side, contract, preferred_element_type=jnp.float32)
 
 
 def dot_rows(left_side, right_side):
+    left_side = left_side.reshape(-1, left_side.shape[-1])
+    right_side = right_side.reshape(-1, right_side.shape[-1])
     return lax.dot_general(
         left_side, right_side, (((0,), (0,)), ((), ())), preferred_element_type=jnp.float32
     )
@@ -111,67 +118,434 @@
     return (seg_here[:, None] == key_seg[None, :]) & (distance >= 0) & (distance < WIN)
 
 
-def line_gather(rows):
-    count = lax.axis_size("fsdp")
-    place = lax.axis_index("fsdp")
-    up, down = [rows], [rows]
-    for hop in range(1, count):
-        up.append(
-            lax.ppermute(up[-1], "fsdp", [(i, i + 1) for i in range(hop - 1, count - 1)])
-        )
-        down.append(
-            lax.ppermute(down[-1], "fsdp", [(i, i - 1) for i in range(1, count - hop + 1)])
-        )
-
-    def assemble(here, from_low, from_high):
-        parts = [from_low[here - j] if j <= here else from_high[j - here] for j in range(count)]
-        return jnp.concatenate(parts, axis=0)
-
-    return lax.switch(
-        place, [functools.partial(assemble, here) for here in range(count)], up, down
-    )
-
-
-def line_scatter(partial):
-    count = lax.axis_size("fsdp")
-    place = lax.axis_index("fsdp")
-    rows = partial.shape[0] // count
-
-    def piece(offset):
-        index = jnp.clip(place + offset, 0, count - 1)
-        return lax.dynamic_slice_in_dim(partial, index * rows, rows).astype(jnp.float32)
-
-    total = piece(0)
-    for sign in (1, -1):
-        carried = None
-        for hop in range(count - 1, 0, -1):
-            running = piece(sign * hop)
-            if carried is not None:
-                running = running + carried.astype(jnp.float32)
-            if sign > 0:
-                pairs = [(i, i + 1) for i in range(count - hop)]
-            else:
-                pairs = [(i, i - 1) for i in range(hop, count)]
-            carried = lax.ppermute(running.astype(jnp.bfloat16), "fsdp", pairs)
-        if carried is not None:
-            total = total + carried.astype(jnp.float32)
-    return total
-
-
-def gather_tokens(rows):
-    return lax.all_gather(rows, "seq", axis=0, tiled=True)
-
-
-def scatter_tokens(partial):
-    return lax.psum_scatter(
-        partial.astype(jnp.bfloat16), "seq", scatter_dimension=0, tiled=True
-    ).astype(jnp.float32)
+def gather_rows(rows):
+    return lax.all_gather(rows, "fsdp", axis=0, tiled=True)
+
+
+def scatter_rows(partial):
+    summed = lax.psum_scatter(
+        partial.astype(jnp.bfloat16), "fsdp", scatter_dimension=0, tiled=True
+    )
+    return summed.astype(jnp.float32)
 
 
 def swap_parts(value, split_axis, concat_axis):
     return lax.all_to_all(
         value, "seq", split_axis=split_axis, concat_axis=concat_axis, tiled=True
     )
+
+
+MESH = pl.DeviceIdType.MESH
+
+
+def plane_places():
+    me = lax.axis_index("seq")
+    other_core = me + 1 - 2 * (me % 2)
+    along_x = me + 2 - 4 * ((me // 2) % 2)
+    along_y = me + 4 - 8 * (me // 4)
+    return me, other_core, along_x, along_y
+
+
+def greet(neighbours):
+    barrier = pltpu.get_barrier_semaphore()
+    for neighbour in neighbours:
+        pl.semaphore_signal(barrier, inc=1, device_id={"seq": neighbour}, device_id_type=MESH)
+    pl.semaphore_wait(barrier, len(neighbours))
+
+
+def gather_kernel(counts, rows, compute, *refs):
+    weight_count, extra_count, out_count = counts
+    refs = list(refs)
+    take = lambda n: [refs.pop(0) for _ in range(n)]
+    (local_ref,), weight_refs, extra_refs = take(1), take(weight_count), take(extra_count)
+    (whole_ref,), out_refs = take(1), take(out_count)
+    send_sem, recv_sem, own_sem = take(3)
+    if compute is not None:
+        (x_buf,), weight_bufs, extra_bufs, out_bufs = (
+            take(1),
+            take(weight_count),
+            take(extra_count),
+            take(out_count),
+        )
+        weight_sem, load_sem, store_sem = take(3)
+
+    me, other_core, along_x, along_y = plane_places()
+    across = along_x + along_y - me
+
+    def piece(batch, place):
+        return whole_ref.at[batch, pl.ds(pl.multiple_of(place * rows, 16), rows)]
+
+    def transfer(slot, source, batch, place, target):
+        return pltpu.make_async_remote_copy(
+            src_ref=source,
+            dst_ref=piece(batch, place),
+            send_sem=send_sem.at[slot],
+            recv_sem=recv_sem.at[slot],
+            device_id={"seq": target},
+            device_id_type=MESH,
+        )
+
+    def forward(slot, batch, place, target):
+        return transfer(slot, piece(batch, place), batch, place, target)
+
+    moves = [
+        transfer(0, local_ref.at[0], 0, me, along_x),
+        transfer(1, local_ref.at[1], 1, me, along_x),
+        transfer(2, local_ref.at[1], 1, me, along_y),
+        transfer(3, local_ref.at[0], 0, me, along_y),
+        forward(4, 0, along_x, along_y),
+        forward(5, 1, along_y, along_x),
+        transfer(6, local_ref.at[0], 0, me, other_core),
+        transfer(7, local_ref.at[1], 1, me, other_core),
+        forward(8, 0, along_x, other_core),
+        forward(9, 1, along_x, other_core),
+        forward(10, 1, along_y, other_core),
+        forward(11, 0, along_y, other_core),
+        forward(12, 0, across, other_core),
+        forward(13, 1, across, other_core),
+    ]
+    greet((other_core, along_x, along_y))
+    for slot in (0, 2, 6, 7, 1, 3):
+        moves[slot].start()
+    owns = [
+        pltpu.make_async_copy(local_ref.at[batch], piece(batch, me), own_sem.at[batch])
+        for batch in range(2)
+    ]
+    for own in owns:
+        own.start()
+    if compute is not None:
+        fetches = [
+            pltpu.make_async_copy(ref, buf, weight_sem.at[i])
+            for i, (ref, buf) in enumerate(zip(weight_refs, weight_bufs))
+        ]
+        for fetch in fetches:
+            fetch.start()
+    stores = []
+
+    def unit(place, batch):
+        if compute is None:
+            return
+        span = pl.ds(pl.multiple_of((place // 2) * (2 * rows), 16), 2 * rows)
+        loads = [
+            pltpu.make_async_copy(ref.at[batch, span], buf, load_sem.at[i])
+            for i, (ref, buf) in enumerate(
+                zip([whole_ref] + extra_refs, [x_buf] + extra_bufs)
+            )
+        ]
+        for load in loads:
+            load.start()
+        step = len(stores)
+        if step == 0:
+            for fetch in fetches:
+                fetch.wait()
+        if step >= 2:
+            for store in stores[step - 2]:
+                store.wait()
+        for load in loads:
+            load.wait()
+        slot = step % 2
+        compute(x_buf, weight_bufs, extra_bufs, [buf.at[slot] for buf in out_bufs])
+        stores.append(
+            [
+                pltpu.make_async_copy(buf.at[slot], ref.at[batch, span], store_sem.at[slot, i])
+                for i, (ref, buf) in enumerate(zip(out_refs, out_bufs))
+            ]
+        )
+        for store in stores[-1]:
+            store.start()
+
+    for batch in range(2):
+        owns[batch].wait()
+        moves[6 + batch].wait_recv()
+        unit(me, batch)
+    moves[0].wait_recv()
+    moves[4].start()
+    moves[8].start()
+    moves[2].wait_recv()
+    moves[5].start()
+    moves[10].start()
+    moves[8].wait_recv()
+    unit(along_x, 0)
+    moves[10].wait_recv()
+    unit(along_y, 1)
+    moves[1].wait_recv()
+    moves[9].start()
+    moves[3].wait_recv()
+    moves[11].start()
+    moves[9].wait_recv()
+    unit(along_x, 1)
+    moves[11].wait_recv()
+    unit(along_y, 0)
+    moves[4].wait_recv()
+    moves[12].start()
+    moves[5].wait_recv()
+    moves[13].start()
+    moves[12].wait_recv()
+    unit(across, 0)
+    moves[13].wait_recv()
+    unit(across, 1)
+    for move in moves:
+        move.wait_send()
+    for group in stores[-2:]:
+        for store in group:
+            store.wait()
+
+
+def plane_gather(local, ident, name, weights=(), extras=(), outs=(), compute=None, flops=0):
+    batches, rows, width = local.shape
+    length = rows * lax.axis_size("seq")
+    whole = jax.ShapeDtypeStruct((batches, length, width), local.dtype)
+    scratch = [
+        pltpu.SemaphoreType.DMA((14,)),
+        pltpu.SemaphoreType.DMA((14,)),
+        pltpu.SemaphoreType.DMA((2,)),
+    ]
+    if compute is not None:
+        scratch += [pltpu.VMEM((2 * rows, width), local.dtype)]
+        scratch += [pltpu.VMEM(weight.shape, weight.dtype) for weight in weights]
+        scratch += [pltpu.VMEM((2 * rows, extra.shape[2]), extra.dtype) for extra in extras]
+        scratch += [pltpu.VMEM((2, 2 * rows, wide), kind) for wide, kind in outs]
+        scratch += [
+            pltpu.SemaphoreType.DMA((len(weights),)),
+            pltpu.SemaphoreType.DMA((1 + len(extras),)),
+            pltpu.SemaphoreType.DMA((2, len(outs))),
+        ]
+    any_space = pl.BlockSpec(memory_space=pl.ANY)
+    out_shape = [whole] + [
+        jax.ShapeDtypeStruct((batches, length, wide), kind) for wide, kind in outs
+    ]
+    return pl.pallas_call(
+        functools.partial(
+            gather_kernel, (len(weights), len(extras), len(outs)), rows, compute
+        ),
+        in_specs=[any_space] * (1 + len(weights) + len(extras)),
+        out_specs=[any_space] * len(out_shape),
+        out_shape=out_shape,
+        scratch_shapes=scratch,
+        compiler_params=pltpu.CompilerParams(
+            collective_id=ident, has_side_effects=True, vmem_limit_bytes=VMEM_LIMIT
+        ),
+        cost_estimate=pl.CostEstimate(
+            flops=flops, bytes_accessed=SPAN_BYTES, transcendentals=0
+        ),
+        name=name,
+    )(local, *weights, *extras)
+
+
+def scatter_kernel(counts, rows, compute, *refs):
+    part_count, weight_count = counts
+    refs = list(refs)
+    take = lambda n: [refs.pop(0) for _ in range(n)]
+    part_refs, weight_refs, (out_ref,) = take(part_count), take(weight_count), take(1)
+    part_bufs, weight_bufs = take(part_count), take(weight_count)
+    sums, from_core, from_link, out_buf = take(4)
+    weight_sem, load_sem, out_sem, core_send, core_recv, link_send, link_recv = take(7)
+
+    me, other_core, along_x, along_y = plane_places()
+    across = along_x + along_y - me
+    core = me % 2
+    kept = pl.ds(pl.multiple_of(core * rows, 16), rows)
+    given = pl.ds(pl.multiple_of((1 - core) * rows, 16), rows)
+    units = [
+        (across, 0),
+        (across, 1),
+        (along_x, 0),
+        (along_y, 1),
+        (along_x, 1),
+        (along_y, 0),
+        (me, 0),
+        (me, 1),
+    ]
+    targets = [along_x, along_y, along_x, along_y, along_x, along_y]
+    added = {4: (1,), 5: (0,), 6: (2, 5), 7: (3, 4)}
+
+    def load(step):
+        place, batch = units[step]
+        span = pl.ds(pl.multiple_of((place // 2) * (2 * rows), 16), 2 * rows)
+        return [
+            pltpu.make_async_copy(ref.at[batch, span], buf.at[step % 2], load_sem.at[step % 2, i])
+            for i, (ref, buf) in enumerate(zip(part_refs, part_bufs))
+        ]
+
+    loads = [load(step) for step in range(8)]
+    fetches = [
+        pltpu.make_async_copy(ref, buf, weight_sem.at[i])
+        for i, (ref, buf) in enumerate(zip(weight_refs, weight_bufs))
+    ]
+    for copy in loads[0] + fetches:
+        copy.start()
+    gives = [
+        pltpu.make_async_remote_copy(
+            src_ref=sums.at[step, given],
+            dst_ref=from_core.at[step],
+            send_sem=core_send.at[step],
+            recv_sem=core_recv.at[step],
+            device_id={"seq": other_core},
+            device_id_type=MESH,
+        )
+        for step in range(8)
+    ]
+    sends = [
+        pltpu.make_async_remote_copy(
+            src_ref=sums.at[step, kept],
+            dst_ref=from_link.at[step],
+            send_sem=link_send.at[step],
+            recv_sem=link_recv.at[step],
+            device_id={"seq": targets[step]},
+            device_id_type=MESH,
+        )
+        for step in range(6)
+    ]
+    greet((other_core, along_x, along_y))
+    outs = []
+
+    def finish(step):
+        gives[step].wait_recv()
+        total = sums[step, kept].astype(jnp.float32) + from_core[step].astype(jnp.float32)
+        for arrived in added.get(step, ()):
+            sends[arrived].wait_recv()
+            total = total + from_link[arrived].astype(jnp.float32)
+        if step < 6:
+            sums[step, kept] = total.astype(jnp.bfloat16)
+            sends[step].start()
+        else:
+            out_buf[step - 6] = total
+            outs.append(
+                pltpu.make_async_copy(
+                    out_buf.at[step - 6], out_ref.at[step - 6], out_sem.at[step - 6]
+                )
+            )
+            outs[-1].start()
+
+    for step in range(8):
+        for copy in loads[step]:
+            copy.wait()
+        if step == 0:
+            for fetch in fetches:
+                fetch.wait()
+        if step < 7:
+            for copy in loads[step + 1]:
+                copy.start()
+        compute([buf.at[step % 2] for buf in part_bufs], weight_bufs, sums.at[step])
+        gives[step].start()
+        if step >= 1:
+            finish(step - 1)
+    finish(7)
+    for move in gives + sends:
+        move.wait_send()
+    for out in outs:
+        out.wait()
+
+
+def plane_scatter(parts, weights, compute, width, ident, name, flops):
+    batches, length = parts[0].shape[:2]
+    rows = length // lax.axis_size("seq")
+    any_space = pl.BlockSpec(memory_space=pl.ANY)
+    scratch = [pltpu.VMEM((2, 2 * rows, part.shape[2]), part.dtype) for part in parts]
+    scratch += [pltpu.VMEM(weight.shape, weight.dtype) for weight in weights]
+    scratch += [
+        pltpu.VMEM((8, 2 * rows, width), jnp.bfloat16),
+        pltpu.VMEM((8, rows, width), jnp.bfloat16),
+        pltpu.VMEM((6, rows, width), jnp.bfloat16),
+        pltpu.VMEM((2, rows, width), jnp.float32),
+        pltpu.SemaphoreType.DMA((len(weights),)),
+        pltpu.SemaphoreType.DMA((2, len(parts))),
+        pltpu.SemaphoreType.DMA((2,)),
+        pltpu.SemaphoreType.DMA((8,)),
+        pltpu.SemaphoreType.DMA((8,)),
+        pltpu.SemaphoreType.DMA((6,)),
+        pltpu.SemaphoreType.DMA((6,)),
+    ]
+    return pl.pallas_call(
+        functools.partial(scatter_kernel, (len(parts), len(weights)), rows, compute),
+        in_specs=[any_space] * (len(parts) + len(weights)),
+        out_specs=any_space,
+        out_shape=jax.ShapeDtypeStruct((batches, rows, width), jnp.float32),
+        scratch_shapes=scratch,
+        compiler_params=pltpu.CompilerParams(
+            collective_id=ident, has_side_effects=True, vmem_limit_bytes=VMEM_LIMIT
+        ),
+        cost_estimate=pl.CostEstimate(
+            flops=flops, bytes_accessed=SPAN_BYTES, transcendentals=0
+        ),
+        name=name,
+    )(*parts, *weights)
+
+
+TILE = 384
+
+
+def tiles(width, body):
+    tile = TILE if width % TILE == 0 else 128
+
+    def step(index, carry):
+        body(pl.ds(pl.multiple_of(index * tile, tile), tile))
+        return carry
+
+    lax.fori_loop(0, width // tile, step, 0)
+
+
+GELU_SCALE = 0.7978845608
+GELU_CUBE = 0.044715
+
+
+def gelu_parts(gate):
+    square = gate * gate
+    bent = jnp.tanh(GELU_SCALE * gate * (1.0 + GELU_CUBE * square))
+    half = 0.5 * (1.0 + bent)
+    slope = half + 0.5 * gate * (1.0 - bent * bent) * GELU_SCALE * (1.0 + 3.0 * GELU_CUBE * square)
+    return gate * half, slope
+
+
+def hidden_compute(x_buf, weights, extras, outs):
+    gate_w, up_w = weights
+    gate_out, up_out, hidden_out = outs
+
+    def body(span):
+        gate = final_dot(x_buf[...], gate_w[:, span])
+        up = final_dot(x_buf[...], up_w[:, span])
+        gate_out[:, span] = gate.astype(gate_out.dtype)
+        up_out[:, span] = up.astype(up_out.dtype)
+        hidden_out[:, span] = (gelu_parts(gate)[0] * up).astype(hidden_out.dtype)
+
+    tiles(gate_w.shape[1], body)
+
+
+def hidden_back_compute(x_buf, weights, extras, outs):
+    (down_w,) = weights
+    gate_in, up_in = extras
+    gate_out, up_out = outs
+
+    def body(span):
+        grad = dot_back(x_buf[...], down_w[span, :])
+        value, slope = gelu_parts(gate_in[:, span].astype(jnp.float32))
+        gate_out[:, span] = (grad * up_in[:, span].astype(jnp.float32) * slope).astype(
+            gate_out.dtype
+        )
+        up_out[:, span] = (grad * value).astype(up_out.dtype)
+
+    tiles(down_w.shape[0], body)
+
+
+def rows_compute(parts, weights, out):
+    def body(span):
+        out[:, span] = final_dot(parts[0][...], weights[0][:, span]).astype(out.dtype)
+
+    tiles(weights[0].shape[1], body)
+
+
+def back_compute(parts, weights, out):
+    def body(span):
+        total = dot_back(parts[0][...], weights[0][span, :])
+        for part, weight in zip(parts[1:], weights[1:]):
+            total = total + dot_back(part[...], weight[span, :])
+        out[:, span] = total.astype(out.dtype)
+
+    tiles(weights[0].shape[0], body)
+
+
+def head_back_compute(x_buf, weights, extras, outs):
+    outs[0][...] = dot_back(x_buf[...], weights[0][...]).astype(outs[0].dtype)
 
 
 def score_parts(query, key, low_bound, row_start, col_start):
@@ -187,7 +561,7 @@
 
 
 def attend_kernel(block, reach, q_ref, k_ref, v_ref, low_ref, out_ref, log_ref):
-    index = pl.program_id(0)
+    index = pl.program_id(1)
 
     def run(blocks):
         first = (index - (blocks - 1)) * block
@@ -230,11 +604,13 @@
     cos_ref,
     sin_ref,
     dq_ref,
+    low_out_ref,
+    high_out_ref,
     dk_ref,
     dv_ref,
 ):
-    index = pl.program_id(0)
-    steps = pl.num_programs(0)
+    index = pl.program_id(1)
+    steps = pl.num_programs(1)
 
     @pl.when(index == 0)
     def _():
@@ -274,7 +650,12 @@
 
     @pl.when(index == steps - 1)
     def _():
-        dk_ref[...] = turn_back(dk_ref[...], cos_ref[...], sin_ref[...])
+        half = HEAD_SIZE // 2
+        dk = turn_back(dk_ref[...], cos_ref[...], sin_ref[...])
+        for part, out_ref in enumerate((low_out_ref, high_out_ref)):
+            lanes = slice(part * half, (part + 1) * half)
+            out_ref[:, :half] = dk[:, lanes].astype(jnp.bfloat16)
+            out_ref[:, half:] = dv_ref[:, lanes].astype(jnp.bfloat16)
 
 
 def block_shape(length):
@@ -285,51 +666,55 @@
     raise ValueError("sequence length")
 
 
+def attend_specs(length, block):
+    whole = pl.BlockSpec((None, length, HEAD_SIZE), lambda m, i: (m, 0, 0))
+    half = pl.BlockSpec((None, length, HEAD_SIZE // 2), lambda m, i: (m, 0, 0))
+    rows = pl.BlockSpec((None, block, HEAD_SIZE), lambda m, i: (m, i, 0))
+    line = pl.BlockSpec((None, block, 1), lambda m, i: (m, i, 0))
+    return whole, half, rows, line
+
+
 def attend(query, key, value, low_bound):
-    length = query.shape[0]
+    batches, length = query.shape[:2]
     block, reach = block_shape(length)
-    whole = pl.BlockSpec((length, HEAD_SIZE), lambda i: (0, 0))
-    rows = pl.BlockSpec((block, HEAD_SIZE), lambda i: (i, 0))
-    line = pl.BlockSpec((block, 1), lambda i: (i, 0))
-    area = block * block * reach * (length // block)
+    whole, half, rows, line = attend_specs(length, block)
+    area = batches * block * block * reach * (length // block)
     return pl.pallas_call(
         functools.partial(attend_kernel, block, reach),
-        grid=(length // block,),
+        grid=(batches, length // block),
         in_specs=[rows, whole, whole, line],
         out_specs=[rows, line],
         out_shape=[
-            jax.ShapeDtypeStruct((length, HEAD_SIZE), jnp.bfloat16),
-            jax.ShapeDtypeStruct((length, 1), jnp.float32),
+            jax.ShapeDtypeStruct((batches, length, HEAD_SIZE), jnp.bfloat16),
+            jax.ShapeDtypeStruct((batches, length, 1), jnp.float32),
         ],
         compiler_params=pltpu.CompilerParams(vmem_limit_bytes=40 * 2**20),
         cost_estimate=pl.CostEstimate(
-            flops=4 * area * HEAD_SIZE, bytes_accessed=10 * length * HEAD_SIZE, transcendentals=2 * area
+            flops=4 * area * HEAD_SIZE,
+            bytes_accessed=10 * batches * length * HEAD_SIZE,
+            transcendentals=2 * area,
         ),
         name="attend",
     )(query, key, value, low_bound)
 
 
 def attend_back(query, key, value, grad, low_bound, log_total, cosine, sine):
-    length = query.shape[0]
+    batches, length = query.shape[:2]
     block, reach = block_shape(length)
-    whole = pl.BlockSpec((length, HEAD_SIZE), lambda i: (0, 0))
-    half = pl.BlockSpec((length, HEAD_SIZE // 2), lambda i: (0, 0))
-    rows = pl.BlockSpec((block, HEAD_SIZE), lambda i: (i, 0))
-    line = pl.BlockSpec((block, 1), lambda i: (i, 0))
-    area = block * block * reach * (length // block)
+    whole, half, rows, line = attend_specs(length, block)
+    area = batches * block * block * reach * (length // block)
     return pl.pallas_call(
         functools.partial(attend_back_kernel, block, reach),
-        grid=(length // block,),
+        grid=(batches, length // block),
         in_specs=[rows, whole, whole, rows, line, line, half, half],
         out_specs=[rows, whole, whole],
-        out_shape=[
-            jax.ShapeDtypeStruct((length, HEAD_SIZE), jnp.bfloat16),
-            jax.ShapeDtypeStruct((length, HEAD_SIZE), jnp.float32),
-            jax.ShapeDtypeStruct((length, HEAD_SIZE), jnp.float32),
-        ],
+        out_shape=[jax.ShapeDtypeStruct((batches, length, HEAD_SIZE), jnp.bfloat16)] * 3,
+        scratch_shapes=[pltpu.VMEM((length, HEAD_SIZE), jnp.float32)] * 2,
         compiler_params=pltpu.CompilerParams(vmem_limit_bytes=48 * 2**20),
         cost_estimate=pl.CostEstimate(
-            flops=10 * area * HEAD_SIZE, bytes_accessed=24 * length * HEAD_SIZE, transcendentals=2 * area
+            flops=10 * area * HEAD_SIZE,
+            bytes_accessed=24 * batches * length * HEAD_SIZE,
+            transcendentals=2 * area,
         ),
         name="attend_back",
     )(query, key, value, grad, low_bound, log_total, cosine, sine)
@@ -349,7 +734,7 @@
             [columns(w_query, HEAD_SIZE), columns(key_weight, half), columns(value_weight, half)],
             axis=1,
         )
-        self.joined = line_gather(joined)
+        self.joined = gather_rows(joined)
         own = self.joined[:, HEAD_SIZE:]
         other = lax.ppermute(own, "seq", [(i, i ^ 1) for i in range(count)])
         odd = place % 2 == 1
@@ -362,54 +747,66 @@
         here = QUERY_HEADS // layers
         part = w_out.reshape(here, count, depth, w_out.shape[1])
         part = lax.dynamic_index_in_dim(part, place, axis=1, keepdims=False)
-        part = line_gather(part.reshape(here * depth, -1))
+        part = gather_rows(part.reshape(here * depth, -1))
         self.out_rows = swap_parts(part, 0, 0)
-        self.records = []
 
     def forward(self, normed, seg_whole):
-        length = seg_whole.shape[0]
-        whole = gather_tokens(normed)
+        batches, length = seg_whole.shape
+        (whole,) = plane_gather(normed, 0, "gather_normed")
         starts = doc_starts(seg_whole)
         places = jnp.arange(length, dtype=jnp.int32)
-        low_bound = jnp.maximum(starts, places - (WIN - 1))[:, None]
+        low_bound = jnp.maximum(starts, places - (WIN - 1))[..., None]
         cosine, sine = angles(places - starts, HEAD_SIZE)
-        cosine, sine = cosine[:, 0], sine[:, 0]
         rows = final_dot(whole, self.weights)
-        query, key, value = (rows[:, HEAD_SIZE * i : HEAD_SIZE * (i + 1)] for i in range(3))
+        query, key, value = (rows[..., HEAD_SIZE * i : HEAD_SIZE * (i + 1)] for i in range(3))
         query = rotate(query, cosine, sine, 1.0) * (1.0 / math.sqrt(HEAD_SIZE))
         query = query.astype(jnp.bfloat16)
         key = rotate(key, cosine, sine, 1.0).astype(jnp.bfloat16)
         value = value.astype(jnp.bfloat16)
         attended, log_total = attend(query, key, value, low_bound)
-        mixed = scatter_tokens(final_dot(attended, self.out_rows))
+        width = normed.shape[-1]
+        flops = 2 * batches * length * HEAD_SIZE * width
+        mixed = plane_scatter(
+            [attended], [self.out_rows], rows_compute, width, 1, "scatter_mixed", flops
+        )
         return mixed, (whole, query, key, value, low_bound, log_total, cosine, sine, attended)
 
     def backward(self, grad_mixed_b, saved):
         whole, query, key, value, low_bound, log_total, cosine, sine, attended = saved
-        half = HEAD_SIZE // 2
+        batches, length = key.shape[:2]
+        width = grad_mixed_b.shape[-1]
         count = lax.axis_size("seq")
-        grad_whole = gather_tokens(grad_mixed_b)
-        grad_att = dot_back(grad_whole, self.out_rows).astype(jnp.bfloat16)
-        dq, dk, dv = attend_back(
+        grad_whole, grad_att = plane_gather(
+            grad_mixed_b,
+            2,
+            "gather_grad_mixed",
+            weights=[self.out_rows],
+            outs=[(HEAD_SIZE, jnp.bfloat16)],
+            compute=head_back_compute,
+            flops=2 * batches * length * HEAD_SIZE * width,
+        )
+        dq, low, high = attend_back(
             query, key, value, grad_att, low_bound, log_total, cosine, sine
         )
         odd = lax.axis_index("seq") % 2 == 1
-        low = jnp.concatenate([dk[:, :half], dv[:, :half]], axis=1)
-        high = jnp.concatenate([dk[:, half:], dv[:, half:]], axis=1)
-        away = jnp.where(odd, low, high)
+        came = lax.ppermute(
+            jnp.where(odd, low, high), "seq", [(i, i ^ 1) for i in range(count)]
+        )
         kept = jnp.where(odd, high, low)
-        came = lax.ppermute(away, "seq", [(i, i ^ 1) for i in range(count)])
-        dkv = (kept + came).astype(jnp.bfloat16)
-        grads = jnp.concatenate([dq, dkv], axis=1)
-        self.records.append((whole, grads, attended, grad_whole))
-        return scatter_tokens(dot_back(grads, self.joined))
+        dkv = (kept.astype(jnp.float32) + came.astype(jnp.float32)).astype(jnp.bfloat16)
+        grads = jnp.concatenate([dq, dkv], axis=-1)
+        self.record = (whole, grads, attended, grad_whole)
+        flops = 4 * batches * length * HEAD_SIZE * width
+        return plane_scatter(
+            [grads], [self.joined], back_compute, width, 3, "scatter_grad_normed", flops
+        )
 
     def weight_grads(self):
         half = HEAD_SIZE // 2
-        out = sum(dot_rows(r[2], r[3]) for r in self.records).astype(jnp.bfloat16)
-        out = line_scatter(swap_parts(out, 1, 0))
-        joined = sum(dot_rows(r[0], r[1]) for r in self.records).astype(jnp.bfloat16)
-        joined = line_scatter(joined)
+        whole, grads, attended, grad_whole = self.record
+        out = dot_rows(attended, grad_whole).astype(jnp.bfloat16)
+        out = scatter_rows(swap_parts(out, 1, 0))
+        joined = scatter_rows(dot_rows(whole, grads))
         return (
             joined[:, :HEAD_SIZE],
             joined[:, HEAD_SIZE : HEAD_SIZE + half],
@@ -424,6 +821,10 @@
         self.records = []
 
     def forward(self, normed, seg_whole):
+        done = [self.forward_one(*pair) for pair in zip(normed, seg_whole)]
+        return jnp.stack([mixed for mixed, _ in done]), [saved for _, saved in done]
+
+    def forward_one(self, normed, seg_whole):
         token_rows = normed.shape[0]
         halo_count = (WIN - 2 + token_rows) // token_rows
         w_query, key_weight, value_weight, w_out = self.weights
@@ -431,7 +832,7 @@
         seg_here = lax.dynamic_slice_in_dim(seg_whole, seq_place * token_rows, token_rows)
         position = jnp.arange(seg_whole.shape[0], dtype=jnp.int32) - doc_starts(seg_whole)
         position = lax.dynamic_slice_in_dim(position, seq_place * token_rows, token_rows)
-        cosine, sine = angles(position, HEAD_SIZE)
+        cosine, sine = (table[:, None] for table in angles(position, HEAD_SIZE))
         query = rotate(
             final_dot(normed, w_query).reshape(token_rows, QUERY_HEADS, HEAD_SIZE),
             cosine,
@@ -466,6 +867,9 @@
         return mixed, (normed, query, pair, allowed, log_total, cosine, sine, attended)
 
     def backward(self, grad_mixed_b, saved):
+        return jnp.stack([self.backward_one(*pair) for pair in zip(grad_mixed_b, saved)])
+
+    def backward_one(self, grad_mixed_b, saved):
         normed, query, pair, allowed, log_total, cosine, sine, attended = saved
         token_rows = normed.shape[0]
         halo_count = (WIN - 2 + token_rows) // token_rows
@@ -502,7 +906,8 @@
         normed, dq, dk, dv, attended, grad_mixed_b = (
             jnp.concatenate(parts, axis=0) for parts in zip(*self.records)
         )
-        normed, attended = gather_tokens(normed), gather_tokens(attended)
+        normed = lax.all_gather(normed, "seq", axis=0, tiled=True)
+        attended = lax.all_gather(attended, "seq", axis=0, tiled=True)
         sums = []
         for rows, grads in ((normed, dq), (normed, dk), (normed, dv), (attended, grad_mixed_b)):
             column_sum = dot_rows(rows, swap_parts(grads, 1, 0)).astype(jnp.bfloat16)
@@ -512,11 +917,11 @@
 
 
 class FeedForward:
-    def __init__(self, w_gate, w_up, w_down):
+    def __init__(self, w_gate, w_up, w_down, by_kernel):
         place = lax.axis_index("seq")
         count = lax.axis_size("seq")
-        hidden = w_gate.shape[1]
-        self.run = hidden // (count * count)
+        self.by_kernel = by_kernel
+        self.run = w_gate.shape[1] // (count * count)
 
         def columns(weight):
             parts = [
@@ -530,45 +935,90 @@
         here = w_down.shape[0] // (count * self.run)
         part = w_down.reshape(here, count, self.run, w_down.shape[1])
         part = lax.dynamic_index_in_dim(part, place, axis=1, keepdims=False)
-        self.gate = line_gather(columns(w_gate))
-        self.up = line_gather(columns(w_up))
-        self.down = line_gather(part.reshape(here * self.run, -1))
-        self.records = []
+        self.gate = gather_rows(columns(w_gate))
+        self.up = gather_rows(columns(w_up))
+        self.down = gather_rows(part.reshape(here * self.run, -1))
 
     def forward(self, ffn_in):
-        whole = gather_tokens(ffn_in)
-        gate_proj = final_dot(whole, self.gate)
-        up_proj = final_dot(whole, self.up)
-        hidden = geglu(gate_proj, up_proj).astype(jnp.bfloat16)
-        down_proj = scatter_tokens(final_dot(hidden, self.down))
+        hidden_width, width = self.down.shape
+        if self.by_kernel:
+            rows = ffn_in.shape[0] * ffn_in.shape[1] * lax.axis_size("seq")
+            whole, gate_proj, up_proj, hidden = plane_gather(
+                ffn_in,
+                4,
+                "gather_ffn_in",
+                weights=[self.gate, self.up],
+                outs=[(hidden_width, jnp.bfloat16)] * 3,
+                compute=hidden_compute,
+                flops=4 * rows * width * hidden_width,
+            )
+            flops = 2 * rows * width * hidden_width
+            down_proj = plane_scatter(
+                [hidden], [self.down], rows_compute, width, 5, "scatter_down", flops
+            )
+        else:
+            whole = lax.all_gather(ffn_in, "seq", axis=1, tiled=True)
+            gate_proj = final_dot(whole, self.gate)
+            up_proj = final_dot(whole, self.up)
+            hidden = geglu(gate_proj, up_proj).astype(jnp.bfloat16)
+            down_proj = lax.psum_scatter(
+                final_dot(hidden, self.down).astype(jnp.bfloat16),
+                "seq",
+                scatter_dimension=1,
+                tiled=True,
+            ).astype(jnp.float32)
         return down_proj, (whole, gate_proj, up_proj, hidden)
 
     def backward(self, grad_down_b, saved):
         whole, gate_proj, up_proj, hidden = saved
-        grad_whole = gather_tokens(grad_down_b)
-        grad_hidden = dot_back(grad_whole, self.down)
-        _, pullback = jax.vjp(geglu, gate_proj, up_proj)
-        grad_gate, grad_up = pullback(grad_hidden)
-        grad_gate, grad_up = grad_gate.astype(jnp.bfloat16), grad_up.astype(jnp.bfloat16)
-        self.records.append((whole, hidden, grad_whole, grad_gate, grad_up))
-        return scatter_tokens(dot_back(grad_gate, self.gate) + dot_back(grad_up, self.up))
+        hidden_width, width = self.down.shape
+        if self.by_kernel:
+            rows = whole.shape[0] * whole.shape[1]
+            grad_whole, grad_gate, grad_up = plane_gather(
+                grad_down_b,
+                6,
+                "gather_grad_down",
+                weights=[self.down],
+                extras=[gate_proj, up_proj],
+                outs=[(hidden_width, jnp.bfloat16)] * 2,
+                compute=hidden_back_compute,
+                flops=2 * rows * width * hidden_width,
+            )
+            grad_ffn_in = plane_scatter(
+                [grad_gate, grad_up],
+                [self.gate, self.up],
+                back_compute,
+                width,
+                7,
+                "scatter_grad_ffn_in",
+                4 * rows * width * hidden_width,
+            )
+        else:
+            grad_whole = lax.all_gather(grad_down_b, "seq", axis=1, tiled=True)
+            grad_hidden = dot_back(grad_whole, self.down)
+            _, pullback = jax.vjp(geglu, gate_proj, up_proj)
+            grad_gate, grad_up = (g.astype(jnp.bfloat16) for g in pullback(grad_hidden))
+            partial = dot_back(grad_gate, self.gate) + dot_back(grad_up, self.up)
+            grad_ffn_in = lax.psum_scatter(
+                partial.astype(jnp.bfloat16), "seq", scatter_dimension=1, tiled=True
+            ).astype(jnp.float32)
+        self.record = (whole, hidden, grad_whole, grad_gate, grad_up)
+        return grad_ffn_in
 
     def weight_grads(self):
-        down = sum(dot_rows(r[1], r[2]) for r in self.records).astype(jnp.bfloat16)
-        gate = sum(dot_rows(r[0], r[3]) for r in self.records).astype(jnp.bfloat16)
-        up = sum(dot_rows(r[0], r[4]) for r in self.records).astype(jnp.bfloat16)
+        whole, hidden, grad_whole, grad_gate, grad_up = self.record
         count = lax.axis_size("seq")
 
-        down = line_scatter(down).astype(jnp.bfloat16)
+        down = scatter_rows(dot_rows(hidden, grad_whole)).astype(jnp.bfloat16)
         here = down.shape[0] // self.run
         down = swap_parts(down.reshape(1, here, self.run, -1), 3, 0)
         down = down.transpose(1, 0, 2, 3).reshape(here * count * self.run, -1)
 
-        def columns(summed):
-            summed = line_scatter(summed).astype(jnp.bfloat16)
+        def columns(grads):
+            summed = scatter_rows(dot_rows(whole, grads)).astype(jnp.bfloat16)
             return swap_parts(summed, 1, 1).astype(jnp.float32)
 
-        return columns(gate), columns(up), down.astype(jnp.float32)
+        return columns(grad_gate), columns(grad_up), down.astype(jnp.float32)
 
 
 def on_device(
@@ -587,54 +1037,53 @@
     gain_ffn_out,
     cotangent,
 ):
-    micro_count = tokens.shape[0]
-    seg_gathered = lax.all_gather(segments, "seq", axis=2, tiled=True)
-    by_heads = lax.axis_size("seq") == QUERY_HEADS and QUERY_HEADS % lax.axis_size("fsdp") == 0
-    attention = (ByHeads if by_heads else ByTokens)(w_query, key_weight, value_weight, w_out)
-    ffn = FeedForward(w_gate, w_up, w_down)
-    results, input_grads = [], []
-    gain_early = jnp.zeros((3, tokens.shape[3]), jnp.float32)
-    gain_late = jnp.zeros((1, tokens.shape[3]), jnp.float32)
-    for batch_index in range(micro_count):
-        stream = tokens[batch_index, 0].astype(jnp.float32)
-        normed = rms_gain(stream, gain_attn_in).astype(jnp.bfloat16)
-        mixed, attention_saved = attention.forward(normed, seg_gathered[batch_index, 0])
-        middle = stream + rms_gain(mixed, gain_attn_out)
-        ffn_in = rms_gain(middle, gain_ffn_in).astype(jnp.bfloat16)
-        down_proj, ffn_saved = ffn.forward(ffn_in)
-        result = middle + rms_gain(down_proj, gain_ffn_out)
-        results.append(result.astype(jnp.bfloat16))
-
-        grad_result = cotangent[batch_index, 0].astype(jnp.float32)
-        _, pullback = jax.vjp(rms_gain, down_proj, gain_ffn_out)
-        grad_down, grad_gain_four = pullback(grad_result)
-        grad_ffn_in = ffn.backward(grad_down.astype(jnp.bfloat16), ffn_saved)
-        _, pullback = jax.vjp(rms_gain, middle, gain_ffn_in)
-        grad_middle, grad_gain_three = pullback(grad_ffn_in)
-        grad_middle = grad_result + grad_middle
-        _, pullback = jax.vjp(rms_gain, mixed, gain_attn_out)
-        grad_mixed, grad_gain_two = pullback(grad_middle)
-        grad_normed = attention.backward(grad_mixed.astype(jnp.bfloat16), attention_saved)
-        _, pullback = jax.vjp(rms_gain, stream, gain_attn_in)
-        grad_stream, grad_gain_one = pullback(grad_normed)
-        input_grads.append(grad_middle + grad_stream)
-        gain_early = gain_early + jnp.stack([grad_gain_two, grad_gain_three, grad_gain_four])
-        gain_late = gain_late + grad_gain_one[None]
-    grad_gate, grad_up, grad_down = ffn.weight_grads()
-    grad_query, grad_key, grad_value, grad_out = attention.weight_grads()
+    seg_whole = lax.all_gather(segments, "seq", axis=2, tiled=True)[:, 0]
+    by_kernel = (
+        lax.axis_size("seq") == QUERY_HEADS
+        and tokens.shape[0] == 2
+        and QUERY_HEADS % lax.axis_size("fsdp") == 0
+    )
+    attention = (ByHeads if by_kernel else ByTokens)(w_query, key_weight, value_weight, w_out)
+    ffn = FeedForward(w_gate, w_up, w_down, by_kernel)
+
+    stream = tokens[:, 0].astype(jnp.float32)
+    normed = rms_gain(stream, gain_attn_in).astype(jnp.bfloat16)
+    mixed, attention_saved = attention.forward(normed, seg_whole)
+    middle = stream + rms_gain(mixed, gain_attn_out)
+    ffn_in = rms_gain(middle, gain_ffn_in).astype(jnp.bfloat16)
+    down_proj, ffn_saved = ffn.forward(ffn_in)
+    result = middle + rms_gain(down_proj, gain_ffn_out)
+
+    grad_result = cotangent[:, 0].astype(jnp.float32)
+    _, pullback = jax.vjp(rms_gain, down_proj, gain_ffn_out)
+    grad_down, grad_gain_four = pullback(grad_result)
+    grad_ffn_in = ffn.backward(grad_down.astype(jnp.bfloat16), ffn_saved)
+    _, pullback = jax.vjp(rms_gain, middle, gain_ffn_in)
+    grad_middle, grad_gain_three = pullback(grad_ffn_in)
+    grad_middle = grad_result + grad_middle
+    _, pullback = jax.vjp(rms_gain, mixed, gain_attn_out)
+    grad_mixed, grad_gain_two = pullback(grad_middle)
+    grad_normed = attention.backward(grad_mixed.astype(jnp.bfloat16), attention_saved)
+    _, pullback = jax.vjp(rms_gain, stream, gain_attn_in)
+    grad_stream, grad_gain_one = pullback(grad_normed)
+    grad_stream = grad_middle + grad_stream
+
+    w_gate_grad, w_up_grad, w_down_grad = ffn.weight_grads()
+    query_grad, key_grad, value_grad, out_grad = attention.weight_grads()
+    gain_early = jnp.stack([grad_gain_two, grad_gain_three, grad_gain_four])
     gain_early = lax.psum(gain_early, ("seq", "fsdp"))
-    gain_late = lax.psum(gain_late, ("seq", "fsdp"))
+    gain_late = lax.psum(grad_gain_one, ("seq", "fsdp"))
     return (
-        jnp.stack(results)[:, None],
-        jnp.stack(input_grads)[:, None],
-        grad_query,
-        grad_key,
-        grad_value,
-        grad_out,
-        grad_gate,
-        grad_up,
-        grad_down,
-        gain_late[0],
+        result.astype(jnp.bfloat16)[:, None],
+        grad_stream[:, None],
+        query_grad,
+        key_grad,
+        value_grad,
+        out_grad,
+        w_gate_grad,
+        w_up_grad,
+        w_down_grad,
+        gain_late,
         gain_early[0],
         gain_early[1],
         gain_early[2],

time: 1820 us -> 1340 us (0.74)
  Pallas kernels: 46.7 us -> 904 us
  waiting for transfers between devices: 719 us -> 23.3 us
  matrix products: 433 us -> 130 us
  starting transfers between devices: 199 us -> 18.6 us
  local copies, waits for them, and re-layouts: 204 us -> 78.8 us
  other arithmetic: 136 us -> 83.2 us
    pallas_call x2 -> x9, Pallas kernels: 16.3 us -> 878 us  [the longest x4 485 us: plane_gather(): pl.pallas_call(functools.partial(gather_kernel, (len(weights), len(extras...]
    ppermute x62 -> x1, waiting for transfers between devices: 348 us -> 0.01 us  [backward(): lax.ppermute(jnp.where(odd, low, high), 'seq', [(i, i ^ 1) for i in range...]
    reduce_scatter x8 -> x5, waiting for transfers between devices: 305 us -> 0.05 us  [scatter_rows(): lax.psum_scatter(partial.astype(jnp.bfloat16), 'fsdp', scatter_dimension=...]
    ppermute x62 -> x1, starting transfers between devices: 178 us -> 1.07 us  [backward(): lax.ppermute(jnp.where(odd, low, high), 'seq', [(i, i ^ 1) for i in range...]
    dot_general x10 -> x0, matrix products: 163 us -> none  [dot_back(): lax.dot_general(left_side, right_side, (((1,), (1,)), ((), ())), preferre...]
    dot_general x10 -> x1, matrix products: 137 us -> 17.2 us  [final_dot(): return jnp.dot(left_side, right_side, preferred_element_type=jnp.float32)]
    slice x7 -> x1, local copies, waits for them, and re-layouts: 106 us -> 0.19 us  [forward(): rows[..., HEAD_SIZE * i:HEAD_SIZE * (i + 1)]]
    all_gather x8 -> x5, waiting for transfers between devices: 55.9 us -> 0.05 us  [gather_rows(): return lax.all_gather(rows, 'fsdp', axis=0, tiled=True)]
  transfers between devices with their start and end apart: 84 -> 16, of which waited for: 33 -> 1; matrix products, arithmetic and copies ran while one was open for 39% -> 17% of each run, Pallas kernels for 3% -> 51%
where the time goes in v2:
time: 1340 us; the launch traced here: 1330 us
  Pallas kernels  904 us (67%)
  matrix products  130 us (10%)
  other arithmetic  83.2 us (6%)
  blocking collectives  79.9 us (6%)
  local copies, waits for them, and re-layouts  78.8 us (6%)
  waiting for transfers between devices  23.3 us (2%)
  starting transfers between devices  18.6 us (1%)
  between operations  15.5 us (1%)
    pallas_call x4, Pallas kernels, plane_gather(): pl.pallas_call(functools.partial(gather_kernel, (len(weights), len(extras...  485 us
    pallas_call x4, Pallas kernels, plane_scatter(): pl.pallas_call(functools.partial(scatter_kernel, (len(parts), len(weights...  377 us
    dot_general x5, matrix products, dot_rows(): lax.dot_general(left_side, right_side, (((0,), (0,)), ((), ())), preferre...  112 us
    psum x1, blocking collectives, on_device(): gain_late = lax.psum(grad_gain_one, ('seq', 'fsdp'))  47.3 us
  transfers between devices with their start and end apart: 16, of which 1 were waited for; matrix products, arithmetic and copies ran while one was open for 17% of the time, Pallas kernels for 51%

profile of v2, /device:TPU:0, one launch (start us, length us, event | category | flops | bytes accessed | tf_op | source)
XLA Modules:
  0.0 1333.2 jit_solution(15905263930744148787)
XLA Ops:
  11.2 6.5 constant_dynamic-slice_fusion.1
  20.2 4.2 concatenate.26
  27.7 12.4 all_gather.19
  45.6 99.6 %gather_normed.1 = bf16[2,1920,2304]{2,1,0:T(8,128)(2,1)} custom-call(bf16[2,240,2304]{2,1,0:T(8,128)(2,1)} %fusion.8.refs_0_), custom_call_target="tpu_custom_call" | custom-call | bytes 270000000 | tf_op jit(solution)/shard_map/gather_normed/pallas_call | solution.py:317
  149.0 3.1 select_maximum_fusion.low_ref
  152.0 3.6 all-to-all-start
  158.0 17.2 %fusion.20 = f32[2,1920,768]{2,1,0:T(8,128)S(1)} fusion(bf16[2,1920,2304]{2,1,0:T(8,128)(2,1)} %gather_normed.1, bf16[2304,768]{1,0:T(8,128)(2,1)S(1)} %slice_dynamic-update-slice_fusion.1), kind=kOutput, calls=%fused_computation.50 | convolution fusion | flops 13589544960 | bytes 33030144 | tf_op jit(solution)/shard_map/dot_general | solution.py:66
  175.9 10.1 fusion.34
  188.5 15.9 %attend.1 = (bf16[2,1920,256]{2,1,0:T(8,128)(2,1)S(1)}, f32[2,1920,1]{2,1,0:T(8,128)S(1)}) custom-call(bf16[2,1920,256]{2,1,0:T(8,128)(2,1)S(1)} %fusion.18.q_ref, bf16[2,1920,256]{2,1,0:T(8,128)(2,1)S(1)} %pad_maximum_fusion.1.k_ref, bf16[2,1920,256]{2,1,0:T(8,128)(2,1)S(1)} %slice.111.v_ref, s32[2,1920,1]{2,1,0:T(8,128)S(1)} %copy-done.5), custom_call_target="tpu_custom_call" | custom-call | flops 6039797760 | bytes 9830400 | tf_op jit(solution)/shard_map/attend/pallas_call | solution.py:682
  208.1 85.0 %scatter_mixed.1 = f32[2,240,2304]{2,1,0:T(8,128)} custom-call(bf16[2,1920,256]{2,1,0:T(8,128)(2,1)} %copy-done.3, bf16[256,2304]{1,0:T(8,128)(2,1)} %bitcast.122), custom_call_target="tpu_custom_call" | custom-call | flops 4529848320 | bytes 270000000 | tf_op jit(solution)/shard_map/scatter_mixed/pallas_call | solution.py:459
  293.1 2.8 multiply_reduce_fusion.6
  296.6 3.1 multiply_reduce_fusion.5
  299.7 4.5 multiply_convert_fusion.refs_0_
  304.2 144.8 %gather_ffn_in.1 = (bf16[2,1920,2304]{2,1,0:T(8,128)(2,1)}, bf16[2,1920,1152]{2,1,0:T(8,128)(2,1)}, bf16[2,1920,1152]{2,1,0:T(8,128)(2,1)}, bf16[2,1920,1152]{2,1,0:T(8,128)(2,1)}) custom-call(bf16[2,240,2304]{2,1,0:T(8,128)(2,1)} %multiply_convert_fusion.refs_0_, bf16[2304,1152]{1,0:T(8,128)(2,1)} %all-gather.10.cloned.1.call-done.refs_1_.refs_2_, ...), custom_call_target="tpu_custom_call" | custom-call | flops 40768634880 | bytes 270000000 | tf_op jit(solution)/shard_map/gather_ffn_in/pallas_call | solution.py:317
  449.1 92.9 %scatter_down.1 = f32[2,240,2304]{2,1,0:T(8,128)} custom-call(bf16[2,1920,1152]{2,1,0:T(8,128)(2,1)} %get-tuple-element.28.refs_0_, bf16[1152,2304]{1,0:T(8,128)(2,1)} %all-gather.14.cloned.1.call-done.refs_1_), custom_call_target="tpu_custom_call" | custom-call | flops 20384317440 | bytes 270000000 | tf_op jit(solution)/shard_map/scatter_down/pallas_call | solution.py:459
  542.0 2.8 multiply_reduce_fusion.4
  547.5 6.3 fusion.11
  553.7 133.1 %gather_grad_down.1 = (bf16[2,1920,2304]{2,1,0:T(8,128)(2,1)}, bf16[2,1920,1152]{2,1,0:T(8,128)(2,1)}, bf16[2,1920,1152]{2,1,0:T(8,128)(2,1)}) custom-call(bf16[2,240,2304]{2,1,0:T(8,128)(2,1)} %get-tuple-element.171.refs_0_, bf16[1152,2304]{1,0:T(8,128)(2,1)} %all-gather.14.cloned.1.call-done.refs_1_, bf16[2,1920,1152]{2,1,0:T(8,128)(2,1)} %get-tuple-element.29.refs_2_, ...), custom_call_target="tpu_custom_call" | custom-call | flops 20384317440 | bytes 270000000 | tf_op jit(solution)/shard_map/gather_grad_down/pallas_call | solution.py:317
  686.8 28.2 %fusion.2 = bf16[1152,2304]{1,0:T(8,128)(2,1)} fusion(bf16[2,1920,1152]{2,1,0:T(8,128)(2,1)} %get-tuple-element.28.refs_0_, bf16[2,1920,2304]{2,1,0:T(8,128)(2,1)} %get-tuple-element.40), kind=kOutput, calls=%fused_computation.5 | convolution fusion | flops 20386971648 | bytes 31850496 | tf_op jit(solution)/shard_map/dot_general | solution.py:77
  715.1 30.3 %fusion.1 = bf16[2304,1152]{1,0:T(8,128)(2,1)} fusion(bf16[2,1920,2304]{2,1,0:T(8,128)(2,1)} %get-tuple-element.39, bf16[2,1920,1152]{2,1,0:T(8,128)(2,1)} %get-tuple-element.32.refs_1_), kind=kOutput, calls=%fused_computation.4 | convolution fusion | flops 20386971648 | bytes 31850496 | tf_op jit(solution)/shard_map/dot_general | solution.py:77
  745.5 30.5 %fusion = bf16[2304,1152]{1,0:T(8,128)(2,1)} fusion(bf16[2,1920,2304]{2,1,0:T(8,128)(2,1)} %get-tuple-element.39, bf16[2,1920,1152]{2,1,0:T(8,128)(2,1)} %get-tuple-element.31.refs_0_), kind=kOutput, calls=%fused_computation.3 | convolution fusion | flops 20386971648 | bytes 31850496 | tf_op jit(solution)/shard_map/dot_general | solution.py:77
  776.1 106.6 %scatter_grad_ffn_in.1 = f32[2,240,2304]{2,1,0:T(8,128)} custom-call(bf16[2,1920,1152]{2,1,0:T(8,128)(2,1)} %get-tuple-element.31.refs_0_, bf16[2,1920,1152]{2,1,0:T(8,128)(2,1)} %get-tuple-element.32.refs_1_, bf16[2304,1152]{1,0:T(8,128)(2,1)} %all-gather.10.cloned.1.call-done.refs_1_.refs_2_, bf16[2304,1152]{1,0:T(8,128)(2,1)} %all-gather.12.cloned.1.call-done.refs_2_.refs_3_), custom_call_target="tpu_custom_call" | custom-call | flops 40768634880 | bytes 270000000 | tf_op jit(solution)/shard_map/scatter_grad_ffn_in/pallas_call | solution.py:459
  882.8 4.8 multiply_reduce_fusion
  887.7 6.6 multiply_reduce_fusion.1
  894.4 4.5 fusion.12.refs_0_
  898.9 107.2 %gather_grad_mixed.1 = (bf16[2,1920,2304]{2,1,0:T(8,128)(2,1)}, bf16[2,1920,256]{2,1,0:T(8,128)(2,1)}) custom-call(bf16[2,240,2304]{2,1,0:T(8,128)(2,1)} %fusion.12.refs_0_, bf16[256,2304]{1,0:T(8,128)(2,1)} %bitcast.123), custom_call_target="tpu_custom_call" | custom-call | flops 4529848320 | bytes 270000000 | tf_op jit(solution)/shard_map/gather_grad_mixed/pallas_call | solution.py:317
  1006.1 26.4 %attend_back.1 = (bf16[2,1920,256]{2,1,0:T(8,128)(2,1)S(1)}, bf16[2,1920,256]{2,1,0:T(8,128)(2,1)S(1)}, bf16[2,1920,256]{2,1,0:T(8,128)(2,1)S(1)}) custom-call(bf16[2,1920,256]{2,1,0:T(8,128)(2,1)} %copy-done.8, bf16[2,1920,256]{2,1,0:T(8,128)(2,1)} %copy-done.7, bf16[2,1920,256]{2,1,0:T(8,128)(2,1)} %copy-done.6, ...), custom_call_target="tpu_custom_call" | custom-call | flops 15099494400 | bytes 23592960 | tf_op jit(solution)/shard_map/attend_back/pallas_call | solution.py:706
  1036.3 9.0 fusion.19
  1046.7 20.2 %all_to_all.60 = bf16[256,8,288]{0,2,1:T(8,128)(2,1)S(1)} all-to-all(bf16[256,8,288]{0,2,1:T(8,128)(2,1)} %bitcast.118), channel_id=1, replica_groups=mesh['seq'=8,'fsdp'=4] {'seq'}, dimensions={1} | all-to-all | bytes 2359296 | tf_op jit(solution)/shard_map/all_to_all | solution.py:133
  1072.1 14.4 %fusion.7 = bf16[2304,512]{1,0:T(8,128)(2,1)} fusion(bf16[2,1920,2304]{2,1,0:T(8,128)(2,1)} %gather_normed.1, bf16[2,1920,256]{2,1,0:T(8,128)(2,1)S(1)} %add_convert_fusion.1, bf16[2,1920,256]{2,1,0:T(8,128)(2,1)S(1)} %copy-done.10), kind=kOutput, calls=%fused_computation.23 | convolution fusion | flops 9068740608 | bytes 23986176 | tf_op jit(solution)/shard_map/dot_general | solution.py:77
  1086.5 6.7 copy.233
  1093.2 4.4 all-to-all-start.4
  1097.7 3.8 pad_maximum_fusion.refs_0_
  1104.1 23.0 %all-to-all-done.4 = bf16[1,2,144,2304]{2,1,0,3:T(2,128)(2,1)} async-done(((bf16[1,2,144,2304]{2,1,0,3:T(2,128)(2,1)}), bf16[1,2,144,2304]{2,1,0,3:T(2,128)(2,1)}, u32[]{:S(2)}, u32[]{:S(2)}) %all-to-all-start.4) | async-done | bytes 1327136 | tf_op jit(solution)/shard_map/all_to_all | solution.py:133
  1127.1 4.3 all-to-all-start.3
  1131.4 92.8 %scatter_grad_normed.1 = f32[2,240,2304]{2,1,0:T(8,128)} custom-call(bf16[2,1920,512]{2,1,0:T(8,128)(2,1)} %pad_maximum_fusion.refs_0_, bf16[2304,512]{1,0:T(8,128)(2,1)} %all-gather.6.cloned.1.call-done.refs_1_), custom_call_target="tpu_custom_call" | custom-call | flops 9059696640 | bytes 270000000 | tf_op jit(solution)/shard_map/scatter_grad_normed/pallas_call | solution.py:459
  1224.3 3.6 fusion.9
  1230.5 4.3 all-to-all-start.2
  1234.8 6.9 fusion.14
  1241.7 47.3 %all-reduce = (f32[2304]{0:T(1024)}, f32[3,2304]{1,0:T(4,128)S(1)}) all-reduce(f32[2304]{0:T(1024)S(1)} %get-tuple-element.138, f32[3,2304]{1,0:T(4,128)S(1)} %pad_maximum_fusion.3), channel_id=1, replica_groups=mesh['seq'=8,'fsdp'=4] {'seq','fsdp'}, use_global_device_ids=true, to_apply=%region_17.18 | all-reduce | flops 9216 | bytes 73728 | tf_op jit(solution)/shard_map/psum | solution.py:1075
  1295.2 5.6 copy.234
  1300.8 3.8 reshape.378
  1304.6 4.5 copy.235
  1309.0 3.6 copy.240
  1312.6 3.1 bitcast_convert_fusion
  1315.8 3.6 copy.239
  1319.3 3.1 bitcast_convert_fusion.1
  1322.5 3.4 copy.238
  (182 shorter events, 53.5 us)
Async XLA Ops:
  7.2 138.1 %all-gather.6.cloned.1.call-start = ((), (), s32[]{:S(2)}) async-start(), calls=%async_computation.10 | async-start | bytes 2949120 | tf_op jit(solution)/shard_map/all_gather | solution.py:122
  10.3 141.7 %all-gather.8.cloned.1.call-start = ((), (), s32[]{:S(2)}) async-start(), calls=%async_computation.11 | async-start | bytes 1474560 | tf_op jit(solution)/shard_map/all_gather | solution.py:122
  11.1 293.1 %all-gather.12.cloned.1.call-start = ((), (), s32[]{:S(2)}) async-start(), calls=%async_computation.13 | async-start | bytes 6635520 | tf_op jit(solution)/shard_map/all_gather | solution.py:122
  20.1 284.1 %all-gather.10.cloned.1.call-start = ((), (), s32[]{:S(2)}) async-start(), calls=%async_computation.12 | async-start | bytes 6635520 | tf_op jit(solution)/shard_map/all_gather | solution.py:122
  20.2 6.8 copy-start.14
  24.4 424.7 %all-gather.14.cloned.1.call-start = ((), (), s32[]{:S(2)}) async-start(), calls=%async_computation.14 | async-start | bytes 6635520 | tf_op jit(solution)/shard_map/all_gather | solution.py:122
  26.9 16.7 %copy-start.27 = (f32[2304]{0:T(1024)S(1)}, f32[2304]{0:T(1024)}, u32[]{:S(2)}) copy-start(f32[2304]{0:T(1024)} %param.23) | copy-start | bytes 27652
  27.5 12.6 copy-start.37
  27.5 18.1 %copy-start.33 = (f32[2,240]{1,0:T(2,128)}, f32[2,240]{1,0:T(2,128)S(1)}, u32[]{:S(2)}) copy-start(f32[2,240]{1,0:T(2,128)S(1)} %fusion.42) | copy-start | bytes 5764
  145.3 10.4 copy-start.21
  147.8 7.9 collective-permute-start
  152.0 55.0 %all-to-all-start = ((bf16[8,32,2304]{2,1,0:T(8,128)(2,1)}), bf16[8,32,2304]{2,1,0:T(8,128)(2,1)S(1)}, u32[]{:S(2)}, u32[]{:S(2)}) async-start(bf16[8,32,2304]{2,1,0:T(8,128)(2,1)} %bitcast.121), calls=%async_computation | async-start | bytes 2359296 | tf_op jit(solution)/shard_map/all_to_all | solution.py:133
  155.6 930.9 %reduce-scatter.14.cloned.1.call-start = ((), (), s32[]{:S(2)}) async-start(), calls=%async_computation.19 | async-start | bytes 6635520 | tf_op jit(solution)/shard_map/reduce_scatter | solution.py:126
  175.9 10.8 copy-start.6
  188.5 15.9 %copy-start.8 = (bf16[2,1920,256]{2,1,0:T(8,128)(2,1)}, bf16[2,1920,256]{2,1,0:T(8,128)(2,1)S(1)}, u32[]{:S(2)}) copy-start(bf16[2,1920,256]{2,1,0:T(8,128)(2,1)S(1)} %fusion.18.q_ref) | copy-start | bytes 5898244
  208.1 88.4 %copy-start.15 = (bf16[2,1,240,2304]{3,2,1,0:T(8,128)(2,1)S(1)}, bf16[2,1,240,2304]{3,2,1,0:T(8,128)(2,1)}, u32[]{:S(2)}) copy-start(bf16[2,1,240,2304]{3,2,1,0:T(8,128)(2,1)} %param.14) | copy-start | bytes 6635524
  208.1 88.4 %copy-start.25 = (f32[2304]{0:T(1024)S(1)}, f32[2304]{0:T(1024)}, u32[]{:S(2)}) copy-start(f32[2304]{0:T(1024)} %param.24) | copy-start | bytes 27652
  299.7 149.3 %copy-start.41 = (f32[2,240]{1,0:T(2,128)}, f32[2,240]{1,0:T(2,128)S(1)}, u32[]{:S(2)}) copy-start(f32[2,240]{1,0:T(2,128)S(1)} %get-tuple-element.149) | copy-start | bytes 5764
  299.7 149.3 %copy-start.31 = (f32[2,240]{1,0:T(2,128)}, f32[2,240]{1,0:T(2,128)S(1)}, u32[]{:S(2)}) copy-start(f32[2,240]{1,0:T(2,128)S(1)} %fusion.44) | copy-start | bytes 5764
  449.1 95.7 %copy-start.18 = (bf16[2,1,240,2304]{3,2,1,0:T(8,128)(2,1)S(1)}, bf16[2,1,240,2304]{3,2,1,0:T(8,128)(2,1)}, u32[]{:S(2)}) copy-start(bf16[2,1,240,2304]{3,2,1,0:T(8,128)(2,1)} %param.27) | copy-start | bytes 6635524
  449.1 95.7 %copy-start.30 = (f32[2304]{0:T(1024)S(1)}, f32[2304]{0:T(1024)}, u32[]{:S(2)}) copy-start(f32[2304]{0:T(1024)} %param.26) | copy-start | bytes 27652
  542.0 3.6 copy-start.17
  715.1 386.4 %reduce-scatter.12.cloned.1.call-start = ((), (), s32[]{:S(2)}) async-start(), calls=%async_computation.18 | async-start | bytes 6635520 | tf_op jit(solution)/shard_map/reduce_scatter | solution.py:126
  745.5 482.4 %reduce-scatter.10.cloned.1.call-start = ((), (), s32[]{:S(2)}) async-start(), calls=%async_computation.17 | async-start | bytes 6635520 | tf_op jit(solution)/shard_map/reduce_scatter | solution.py:126
  776.1 106.7 %copy-start.24 = (f32[2304]{0:T(1024)S(1)}, f32[2304]{0:T(1024)}, u32[]{:S(2)}) copy-start(f32[2304]{0:T(1024)} %param.25) | copy-start | bytes 27652
  776.1 106.7 %copy-start.32 = (f32[2,240]{1,0:T(2,128)S(1)}, f32[2,240]{1,0:T(2,128)}, u32[]{:S(2)}) copy-start(f32[2,240]{1,0:T(2,128)} %copy-done.31) | copy-start | bytes 5764
  776.1 513.6 %reduce-scatter.8.cloned.1.call-start = ((), (), s32[]{:S(2)}) async-start(), calls=%async_computation.16 | async-start | bytes 1474560 | tf_op jit(solution)/shard_map/reduce_scatter | solution.py:126
  882.8 4.9 copy-start.42
  882.8 4.9 copy-start.19
  882.8 4.9 copy-start.26
  882.8 4.9 copy-start.36
  882.8 11.5 slice-start
  887.7 6.6 copy-start.40
  887.7 6.6 slice-start.1
  1032.5 3.8 copy-start.4
  1035.2 33.1 %collective-permute-start.1 = (bf16[2,1920,256]{2,1,0:T(8,128)(2,1)}, bf16[2,1920,256]{2,1,0:T(8,128)(2,1)}, u32[]{:S(2)}, u32[]{:S(2)}) collective-permute-start(bf16[2,1920,256]{2,1,0:T(8,128)(2,1)} %broadcast_select_fusion), channel_id=1, source_target_pairs={{0,4},{4,0},{8,12},{12,8},{16,20},{20,16},{24,28},{28,24},{1,5},{5... | collective-permute-start | bytes 5898248 | tf_op jit(solution)/shard_map/ppermute | solution.py:792
  1068.1 223.4 %reduce-scatter.6.cloned.1.call-start = ((), (), s32[]{:S(2)}) async-start(), calls=%async_computation.15 | async-start | bytes 2949120 | tf_op jit(solution)/shard_map/reduce_scatter | solution.py:126
  1068.4 3.7 copy-start.10
  1086.5 11.1 copy-start.29
  1086.5 11.2 copy-start.11
  1093.2 33.9 %all-to-all-start.4 = ((bf16[1,2,144,2304]{2,1,0,3:T(2,128)(2,1)}), bf16[1,2,144,2304]{2,1,0,3:T(2,128)(2,1)}, u32[]{:S(2)}, u32[]{:S(2)}) async-start(bf16[1,2,144,2304]{2,1,0,3:T(2,128)(2,1)} %copy.233), calls=%async_computation.9 | async-start | bytes 4718592 | tf_op jit(solution)/shard_map/all_to_all | solution.py:133
  1127.1 103.4 %all-to-all-start.3 = ((bf16[576,8,144]{0,2,1:T(8,128)(2,1)}), bf16[576,8,144]{0,2,1:T(8,128)(2,1)}, u32[]{:S(2)}, u32[]{:S(2)}) async-start(bf16[576,8,144]{0,2,1:T(8,128)(2,1)} %bitcast.32), calls=%async_computation.7 | async-start | bytes 2949120 | tf_op jit(solution)/shard_map/all_to_all | solution.py:133
  1131.4 92.9 %copy-start.16 = (bf16[2,1,240,2304]{3,2,1,0:T(8,128)(2,1)S(1)}, bf16[2,1,240,2304]{3,2,1,0:T(8,128)(2,1)}, u32[]{:S(2)}) copy-start(bf16[2,1,240,2304]{3,2,1,0:T(8,128)(2,1)} %param.14) | copy-start | bytes 6635524
  1131.4 92.9 %copy-start.28 = (f32[2304]{0:T(1024)S(1)}, f32[2304]{0:T(1024)}, u32[]{:S(2)}) copy-start(f32[2304]{0:T(1024)} %param.23) | copy-start | bytes 27652
  1131.4 92.9 %copy-start.34 = (f32[2,240]{1,0:T(2,128)S(1)}, f32[2,240]{1,0:T(2,128)}, u32[]{:S(2)}) copy-start(f32[2,240]{1,0:T(2,128)} %copy-done.33) | copy-start | bytes 5764
  1224.3 3.6 copy-start.38
  1230.5 88.8 %all-to-all-start.2 = ((bf16[576,8,144]{0,2,1:T(8,128)(2,1)}), bf16[576,8,144]{0,2,1:T(8,128)(2,1)}, u32[]{:S(2)}, u32[]{:S(2)}) async-start(bf16[576,8,144]{0,2,1:T(8,128)(2,1)} %bitcast.115), calls=%async_computation.5 | async-start | bytes 2949120 | tf_op jit(solution)/shard_map/all_to_all | solution.py:133
  1315.8 10.1 copy-start.1
  (15 other events, 29.8 us)
Sparse Core Ops, SparseCore 0:
  10.4 53.1 all-gather.5
  65.8 29.2 all-gather.7
  96.6 98.2 all-gather.11
  196.9 97.4 all-gather.9
  295.9 97.4 all-gather.13
  715.2 95.4 reduce-scatter.13
  813.1 95.3 reduce-scatter.11
  910.8 95.3 reduce-scatter.9
  1068.2 28.6 reduce-scatter.7
  1099.7 46.7 reduce-scatter.5

commit v3 on v2

--- a/solution.py
+++ b/solution.py
@@ -123,10 +123,9 @@
 
 
 def scatter_rows(partial):
-    summed = lax.psum_scatter(
+    return lax.psum_scatter(
         partial.astype(jnp.bfloat16), "fsdp", scatter_dimension=0, tiled=True
     )
-    return summed.astype(jnp.float32)
 
 
 def swap_parts(value, split_axis, concat_axis):
@@ -153,24 +152,74 @@
     pl.semaphore_wait(barrier, len(neighbours))
 
 
-def gather_kernel(counts, rows, compute, *refs):
-    weight_count, extra_count, out_count = counts
+BRAID = 384
+
+
+def braid_width(arrays):
+    return sum(array.shape[-1] for array in arrays)
+
+
+def copies_into(sources, target, sem):
+    if len(sources) == 1:
+        return [pltpu.make_async_copy(sources[0], target, sem.at[0])]
+    groups = sources[0].shape[-1] // BRAID
+    copies = []
+    for group in range(groups):
+        for part, source in enumerate(sources):
+            at = group * len(sources) + part
+            copies.append(
+                pltpu.make_async_copy(
+                    source.at[:, pl.ds(group * BRAID, BRAID)],
+                    target.at[:, pl.ds(at * BRAID, BRAID)],
+                    sem.at[at],
+                )
+            )
+    return copies
+
+
+def copy_count(arrays):
+    return 1 if len(arrays) == 1 else braid_width(arrays) // BRAID
+
+
+def unit_rows(place, rows):
+    return pl.ds(pl.multiple_of((place // 2) * (2 * rows), 16), 2 * rows)
+
+
+class Job:
+    def __init__(
+        self, compute, weights=(), extras=(), outs=(), sums=(), side=(), tables=(), spare=None, flops=0
+    ):
+        self.compute, self.flops, self.spare = compute, flops, spare
+        self.tables = list(tables)
+        self.weights, self.extras, self.outs = list(weights), list(extras), list(outs)
+        self.sums, self.side = list(sums), list(side)
+
+
+def gather_kernel(job, rows, *refs):
     refs = list(refs)
     take = lambda n: [refs.pop(0) for _ in range(n)]
-    (local_ref,), weight_refs, extra_refs = take(1), take(weight_count), take(extra_count)
-    (whole_ref,), out_refs = take(1), take(out_count)
-    send_sem, recv_sem, own_sem = take(3)
-    if compute is not None:
-        (x_buf,), weight_bufs, extra_bufs, out_bufs = (
-            take(1),
-            take(weight_count),
-            take(extra_count),
-            take(out_count),
-        )
-        weight_sem, load_sem, store_sem = take(3)
+    (local_ref,) = take(1)
+    weight_refs, extra_refs, side_refs = (
+        take(len(job.weights)),
+        take(len(job.extras)),
+        take(len(job.side)),
+    )
+    table_refs = take(len(job.tables))
+    (whole_ref,), out_refs, final_refs = take(1), take(len(job.outs)), take(len(job.sums))
+    made_refs = take(len(job.spare[1]) if job.spare else 0)
+    send_sem, recv_sem, own_sem, x_buf = take(4)
+    weight_bufs = take(1 if job.weights else 0)
+    extra_bufs, side_bufs, out_bufs = (
+        take(len(job.extras)),
+        take(len(job.side)),
+        take(len(job.outs)),
+    )
+    sum_bufs, final_bufs = take(len(job.sums)), take(len(job.sums))
+    weight_sem, load_sem, side_sem, store_sem, final_sem = take(5)
 
     me, other_core, along_x, along_y = plane_places()
     across = along_x + along_y - me
+    core = me % 2
 
     def piece(batch, place):
         return whole_ref.at[batch, pl.ds(pl.multiple_of(place * rows, 16), rows)]
@@ -205,7 +254,7 @@
         forward(13, 1, across, other_core),
     ]
     greet((other_core, along_x, along_y))
-    for slot in (0, 2, 6, 7, 1, 3):
+    for slot in (0, 2, 1, 3, 6, 7):
         moves[slot].start()
     owns = [
         pltpu.make_async_copy(local_ref.at[batch], piece(batch, me), own_sem.at[batch])
@@ -213,24 +262,33 @@
     ]
     for own in owns:
         own.start()
-    if compute is not None:
-        fetches = [
-            pltpu.make_async_copy(ref, buf, weight_sem.at[i])
-            for i, (ref, buf) in enumerate(zip(weight_refs, weight_bufs))
-        ]
-        for fetch in fetches:
-            fetch.start()
+    fetches = copies_into(weight_refs, weight_bufs[0], weight_sem) if job.weights else []
+    for fetch in fetches:
+        fetch.start()
+    if job.spare:
+        job.spare[0](table_refs, made_refs)
     stores = []
-
-    def unit(place, batch):
-        if compute is None:
+    done = {"side": 0}
+
+    def own_half(which):
+        return x_buf.at[pl.ds(pl.multiple_of(which * rows, 16), rows)]
+
+    def unit(place, batch, own=False):
+        if job.compute is None:
             return
-        span = pl.ds(pl.multiple_of((place // 2) * (2 * rows), 16), 2 * rows)
-        loads = [
-            pltpu.make_async_copy(ref.at[batch, span], buf, load_sem.at[i])
-            for i, (ref, buf) in enumerate(
-                zip([whole_ref] + extra_refs, [x_buf] + extra_bufs)
-            )
+        span = unit_rows(place, rows)
+        if own:
+            loads = [
+                pltpu.make_async_copy(local_ref.at[batch], own_half(core), load_sem.at[0]),
+                pltpu.make_async_copy(
+                    piece(batch, other_core), own_half(1 - core), load_sem.at[1]
+                ),
+            ]
+        else:
+            loads = [pltpu.make_async_copy(whole_ref.at[batch, span], x_buf, load_sem.at[0])]
+        loads += [
+            pltpu.make_async_copy(ref.at[batch, span], buf, load_sem.at[2 + i])
+            for i, (ref, buf) in enumerate(zip(extra_refs, extra_bufs))
         ]
         for load in loads:
             load.start()
@@ -244,7 +302,9 @@
         for load in loads:
             load.wait()
         slot = step % 2
-        compute(x_buf, weight_bufs, extra_bufs, [buf.at[slot] for buf in out_bufs])
+        job.compute(
+            x_buf, weight_bufs, extra_bufs, [buf.at[slot] for buf in out_bufs], sum_bufs, step == 0
+        )
         stores.append(
             [
                 pltpu.make_async_copy(buf.at[slot], ref.at[batch, span], store_sem.at[slot, i])
@@ -254,28 +314,41 @@
         for store in stores[-1]:
             store.start()
 
+    def side(count):
+        if not job.side:
+            return
+        for _ in range(count):
+            chunk = done["side"]
+            done["side"] += 1
+            run_side(chunk, rows, side_refs, side_bufs, sum_bufs[0], side_sem)
+
     for batch in range(2):
-        owns[batch].wait()
         moves[6 + batch].wait_recv()
-        unit(me, batch)
+        unit(me, batch, own=True)
+        side(1)
     moves[0].wait_recv()
     moves[4].start()
     moves[8].start()
     moves[2].wait_recv()
     moves[5].start()
     moves[10].start()
+    side(2)
     moves[8].wait_recv()
     unit(along_x, 0)
     moves[10].wait_recv()
     unit(along_y, 1)
+    side(1)
     moves[1].wait_recv()
     moves[9].start()
     moves[3].wait_recv()
     moves[11].start()
+    side(3)
     moves[9].wait_recv()
     unit(along_x, 1)
     moves[11].wait_recv()
     unit(along_y, 0)
+    if job.side:
+        finish_sums(sum_bufs, final_bufs, final_refs, final_sem)
     moves[4].wait_recv()
     moves[12].start()
     moves[5].wait_recv()
@@ -284,62 +357,107 @@
     unit(across, 0)
     moves[13].wait_recv()
     unit(across, 1)
+    if not job.side:
+        finish_sums(sum_bufs, final_bufs, final_refs, final_sem)
     for move in moves:
         move.wait_send()
+    for own in owns:
+        own.wait()
     for group in stores[-2:]:
         for store in group:
             store.wait()
 
 
-def plane_gather(local, ident, name, weights=(), extras=(), outs=(), compute=None, flops=0):
+def run_side(chunk, rows, refs, bufs, total, sem):
+    span = pl.ds((chunk % 4) * 2 * rows, 2 * rows)
+    loads = [
+        pltpu.make_async_copy(ref.at[chunk // 4, span], buf, sem.at[i])
+        for i, (ref, buf) in enumerate(zip(refs, bufs))
+    ]
+    for load in loads:
+        load.start()
+    for load in loads:
+        load.wait()
+    add_outer(bufs[0], bufs[1], total, chunk == 0)
+
+
+def finish_sums(sum_bufs, final_bufs, final_refs, sem):
+    for i, (total, buf, ref) in enumerate(zip(sum_bufs, final_bufs, final_refs)):
+        copies = []
+        for block in range(total.shape[0] // BRAID):
+            slot = block % 2
+            span = pl.ds(block * BRAID, BRAID)
+            if block >= 2:
+                copies[block - 2].wait()
+            buf[slot] = total[span, :].astype(buf.dtype)
+            copies.append(pltpu.make_async_copy(buf.at[slot], ref.at[span], sem.at[i, slot]))
+            copies[-1].start()
+        for copy in copies[-2:]:
+            copy.wait()
+
+
+def plane_gather(local, ident, name, job=None):
+    job = job or Job(None)
     batches, rows, width = local.shape
     length = rows * lax.axis_size("seq")
-    whole = jax.ShapeDtypeStruct((batches, length, width), local.dtype)
-    scratch = [
-        pltpu.SemaphoreType.DMA((14,)),
-        pltpu.SemaphoreType.DMA((14,)),
-        pltpu.SemaphoreType.DMA((2,)),
+    semaphores = pltpu.SemaphoreType.DMA
+    scratch = [semaphores((14,)), semaphores((14,)), semaphores((2,))]
+    scratch += [pltpu.VMEM((2 * rows if job.compute else 8, width), local.dtype)]
+    if job.weights:
+        depth = job.weights[0].shape[0]
+        scratch += [pltpu.VMEM((depth, braid_width(job.weights)), job.weights[0].dtype)]
+    for arrays in (job.extras, job.side):
+        scratch += [pltpu.VMEM((2 * rows, array.shape[2]), array.dtype) for array in arrays]
+    scratch += [pltpu.VMEM((2, 2 * rows, wide), kind) for wide, kind in job.outs]
+    scratch += [pltpu.VMEM(shape, jnp.float32) for shape in job.sums]
+    scratch += [pltpu.VMEM((2, BRAID, shape[1]), jnp.bfloat16) for shape in job.sums]
+    scratch += [
+        semaphores((copy_count(job.weights) if job.weights else 1,)),
+        semaphores((2 + len(job.extras),)),
+        semaphores((max(1, len(job.side)),)),
+        semaphores((2, max(1, len(job.outs)))),
+        semaphores((max(1, len(job.sums)), 2)),
     ]
-    if compute is not None:
-        scratch += [pltpu.VMEM((2 * rows, width), local.dtype)]
-        scratch += [pltpu.VMEM(weight.shape, weight.dtype) for weight in weights]
-        scratch += [pltpu.VMEM((2 * rows, extra.shape[2]), extra.dtype) for extra in extras]
-        scratch += [pltpu.VMEM((2, 2 * rows, wide), kind) for wide, kind in outs]
-        scratch += [
-            pltpu.SemaphoreType.DMA((len(weights),)),
-            pltpu.SemaphoreType.DMA((1 + len(extras),)),
-            pltpu.SemaphoreType.DMA((2, len(outs))),
-        ]
     any_space = pl.BlockSpec(memory_space=pl.ANY)
-    out_shape = [whole] + [
-        jax.ShapeDtypeStruct((batches, length, wide), kind) for wide, kind in outs
-    ]
+    out_shape = [jax.ShapeDtypeStruct((batches, length, width), local.dtype)]
+    out_shape += [jax.ShapeDtypeStruct((batches, length, wide), kind) for wide, kind in job.outs]
+    out_shape += [jax.ShapeDtypeStruct(shape, jnp.bfloat16) for shape in job.sums]
+    inputs = [local, *job.weights, *job.extras, *job.side]
+    in_specs = [any_space] * len(inputs)
+    in_specs += [pl.BlockSpec(memory_space=pltpu.VMEM)] * len(job.tables)
+    out_specs = [any_space] * len(out_shape)
+    if job.spare:
+        out_shape += job.spare[1]
+        out_specs += [pl.BlockSpec(memory_space=pltpu.VMEM)] * len(job.spare[1])
     return pl.pallas_call(
-        functools.partial(
-            gather_kernel, (len(weights), len(extras), len(outs)), rows, compute
-        ),
-        in_specs=[any_space] * (1 + len(weights) + len(extras)),
-        out_specs=[any_space] * len(out_shape),
+        functools.partial(gather_kernel, job, rows),
+        in_specs=in_specs,
+        out_specs=out_specs,
         out_shape=out_shape,
         scratch_shapes=scratch,
         compiler_params=pltpu.CompilerParams(
             collective_id=ident, has_side_effects=True, vmem_limit_bytes=VMEM_LIMIT
         ),
         cost_estimate=pl.CostEstimate(
-            flops=flops, bytes_accessed=SPAN_BYTES, transcendentals=0
+            flops=job.flops, bytes_accessed=SPAN_BYTES, transcendentals=0
         ),
         name=name,
-    )(local, *weights, *extras)
-
-
-def scatter_kernel(counts, rows, compute, *refs):
-    part_count, weight_count = counts
+    )(*inputs, *job.tables)
+
+
+def scatter_kernel(job, rows, *refs):
     refs = list(refs)
     take = lambda n: [refs.pop(0) for _ in range(n)]
-    part_refs, weight_refs, (out_ref,) = take(part_count), take(weight_count), take(1)
-    part_bufs, weight_bufs = take(part_count), take(weight_count)
-    sums, from_core, from_link, out_buf = take(4)
-    weight_sem, load_sem, out_sem, core_send, core_recv, link_send, link_recv = take(7)
+    part_refs, weight_refs, side_refs = (
+        take(len(job.extras)),
+        take(len(job.weights)),
+        take(len(job.side)),
+    )
+    (out_ref,), final_refs = take(1), take(len(job.sums))
+    part_buf, weight_buf, sums, held, from_core, from_link, out_buf = take(7)
+    side_bufs, sum_bufs, final_bufs = take(len(job.side)), take(len(job.sums)), take(len(job.sums))
+    weight_sem, load_sem, side_sem, final_sem, out_sem = take(5)
+    core_send, core_recv, link_send, link_recv, credit = take(5)
 
     me, other_core, along_x, along_y = plane_places()
     across = along_x + along_y - me
@@ -361,23 +479,18 @@
 
     def load(step):
         place, batch = units[step]
-        span = pl.ds(pl.multiple_of((place // 2) * (2 * rows), 16), 2 * rows)
-        return [
-            pltpu.make_async_copy(ref.at[batch, span], buf.at[step % 2], load_sem.at[step % 2, i])
-            for i, (ref, buf) in enumerate(zip(part_refs, part_bufs))
-        ]
+        span = unit_rows(place, rows)
+        sources = [ref.at[batch, span] for ref in part_refs]
+        return copies_into(sources, part_buf.at[step % 2], load_sem.at[step % 2])
 
     loads = [load(step) for step in range(8)]
-    fetches = [
-        pltpu.make_async_copy(ref, buf, weight_sem.at[i])
-        for i, (ref, buf) in enumerate(zip(weight_refs, weight_bufs))
-    ]
+    fetches = copies_into(weight_refs, weight_buf, weight_sem)
     for copy in loads[0] + fetches:
         copy.start()
     gives = [
         pltpu.make_async_remote_copy(
-            src_ref=sums.at[step, given],
-            dst_ref=from_core.at[step],
+            src_ref=sums.at[step % 2, given],
+            dst_ref=from_core.at[step % 4],
             send_sem=core_send.at[step],
             recv_sem=core_recv.at[step],
             device_id={"seq": other_core},
@@ -387,7 +500,7 @@
     ]
     sends = [
         pltpu.make_async_remote_copy(
-            src_ref=sums.at[step, kept],
+            src_ref=held.at[step],
             dst_ref=from_link.at[step],
             send_sem=link_send.at[step],
             recv_sem=link_recv.at[step],
@@ -397,25 +510,34 @@
         for step in range(6)
     ]
     greet((other_core, along_x, along_y))
-    outs = []
 
     def finish(step):
         gives[step].wait_recv()
-        total = sums[step, kept].astype(jnp.float32) + from_core[step].astype(jnp.float32)
+        total = sums[step % 2, kept].astype(jnp.float32)
+        total = total + from_core[step % 4].astype(jnp.float32)
+        if step < 4:
+            pl.semaphore_signal(credit, inc=1, device_id={"seq": other_core}, device_id_type=MESH)
         for arrived in added.get(step, ()):
             sends[arrived].wait_recv()
             total = total + from_link[arrived].astype(jnp.float32)
         if step < 6:
-            sums[step, kept] = total.astype(jnp.bfloat16)
+            held[step] = total.astype(jnp.bfloat16)
             sends[step].start()
         else:
-            out_buf[step - 6] = total
-            outs.append(
-                pltpu.make_async_copy(
-                    out_buf.at[step - 6], out_ref.at[step - 6], out_sem.at[step - 6]
-                )
-            )
-            outs[-1].start()
+            out = pltpu.make_async_copy(out_buf, out_ref.at[step - 6], out_sem.at[step - 6])
+            out_buf[...] = total
+            out.start()
+            out.wait()
+
+    done = {"side": 0}
+
+    def side(count):
+        if not job.side:
+            return
+        for _ in range(count):
+            chunk = done["side"]
+            done["side"] += 1
+            run_side(chunk, rows, side_refs, side_bufs, sum_bufs[0], side_sem)
 
     for step in range(8):
         for copy in loads[step]:
@@ -426,60 +548,150 @@
         if step < 7:
             for copy in loads[step + 1]:
                 copy.start()
-        compute([buf.at[step % 2] for buf in part_bufs], weight_bufs, sums.at[step])
+        if step >= 2:
+            gives[step - 2].wait_send()
+        job.compute(part_buf.at[step % 2], weight_buf, sums.at[step % 2])
+        if step >= 4:
+            pl.semaphore_wait(credit, 1)
         gives[step].start()
         if step >= 1:
             finish(step - 1)
+        side((0, 0, 1, 1, 1, 1, 2, 2)[step])
+    if job.side:
+        finish_sums(sum_bufs, final_bufs, final_refs, final_sem)
     finish(7)
-    for move in gives + sends:
+    for move in gives[6:] + sends:
         move.wait_send()
-    for out in outs:
-        out.wait()
-
-
-def plane_scatter(parts, weights, compute, width, ident, name, flops):
+
+
+def plane_scatter(parts, width, ident, name, job):
+    job.extras = list(parts)
     batches, length = parts[0].shape[:2]
     rows = length // lax.axis_size("seq")
     any_space = pl.BlockSpec(memory_space=pl.ANY)
-    scratch = [pltpu.VMEM((2, 2 * rows, part.shape[2]), part.dtype) for part in parts]
-    scratch += [pltpu.VMEM(weight.shape, weight.dtype) for weight in weights]
+    semaphores = pltpu.SemaphoreType.DMA
+    weights = job.weights
+    scratch = [
+        pltpu.VMEM((2, 2 * rows, braid_width(parts)), parts[0].dtype),
+        pltpu.VMEM((weights[0].shape[0], braid_width(weights)), weights[0].dtype),
+        pltpu.VMEM((2, 2 * rows, width), jnp.bfloat16),
+        pltpu.VMEM((6, rows, width), jnp.bfloat16),
+        pltpu.VMEM((4, rows, width), jnp.bfloat16),
+        pltpu.VMEM((6, rows, width), jnp.bfloat16),
+        pltpu.VMEM((rows, width), jnp.float32),
+    ]
+    scratch += [pltpu.VMEM((2 * rows, array.shape[2]), array.dtype) for array in job.side]
+    scratch += [pltpu.VMEM(shape, jnp.float32) for shape in job.sums]
+    scratch += [pltpu.VMEM((2, BRAID, shape[1]), jnp.bfloat16) for shape in job.sums]
     scratch += [
-        pltpu.VMEM((8, 2 * rows, width), jnp.bfloat16),
-        pltpu.VMEM((8, rows, width), jnp.bfloat16),
-        pltpu.VMEM((6, rows, width), jnp.bfloat16),
-        pltpu.VMEM((2, rows, width), jnp.float32),
-        pltpu.SemaphoreType.DMA((len(weights),)),
-        pltpu.SemaphoreType.DMA((2, len(parts))),
-        pltpu.SemaphoreType.DMA((2,)),
-        pltpu.SemaphoreType.DMA((8,)),
-        pltpu.SemaphoreType.DMA((8,)),
-        pltpu.SemaphoreType.DMA((6,)),
-        pltpu.SemaphoreType.DMA((6,)),
+        semaphores((copy_count(weights),)),
+        semaphores((2, copy_count(parts))),
+        semaphores((max(1, len(job.side)),)),
+        semaphores((max(1, len(job.sums)), 2)),
+        semaphores((2,)),
+        semaphores((8,)),
+        semaphores((8,)),
+        semaphores((6,)),
+        semaphores((6,)),
+        pltpu.SemaphoreType.REGULAR,
     ]
+    out_shape = [jax.ShapeDtypeStruct((batches, rows, width), jnp.float32)]
+    out_shape += [jax.ShapeDtypeStruct(shape, jnp.bfloat16) for shape in job.sums]
+    inputs = [*parts, *weights, *job.side]
     return pl.pallas_call(
-        functools.partial(scatter_kernel, (len(parts), len(weights)), rows, compute),
-        in_specs=[any_space] * (len(parts) + len(weights)),
-        out_specs=any_space,
-        out_shape=jax.ShapeDtypeStruct((batches, rows, width), jnp.float32),
+        functools.partial(scatter_kernel, job, rows),
+        in_specs=[any_space] * len(inputs),
+        out_specs=[any_space] * len(out_shape),
+        out_shape=out_shape,
         scratch_shapes=scratch,
         compiler_params=pltpu.CompilerParams(
             collective_id=ident, has_side_effects=True, vmem_limit_bytes=VMEM_LIMIT
         ),
         cost_estimate=pl.CostEstimate(
-            flops=flops, bytes_accessed=SPAN_BYTES, transcendentals=0
+            flops=job.flops, bytes_accessed=SPAN_BYTES, transcendentals=0
         ),
         name=name,
-    )(*parts, *weights)
-
-
-TILE = 384
-
-
-def tiles(width, body):
-    tile = TILE if width % TILE == 0 else 128
-
+    )(*inputs)
+
+
+def small_sum_kernel(over_layers, value_ref, out_ref, plane_buf, layer_buf, *sems):
+    plane_send, plane_recv, layer_send, layer_recv = sems
+    neighbours = plane_places()[1:]
+    layer, layers = lax.axis_index("fsdp"), lax.axis_size("fsdp")
+    others = [lax.rem(layer + hop, layers) for hop in range(1, layers)] if over_layers else []
+    barrier = pltpu.get_barrier_semaphore()
+    for neighbour in neighbours:
+        pl.semaphore_signal(barrier, inc=1, device_id={"seq": neighbour}, device_id_type=MESH)
+    for other in others:
+        pl.semaphore_signal(barrier, inc=1, device_id={"fsdp": other}, device_id_type=MESH)
+    pl.semaphore_wait(barrier, len(neighbours) + len(others))
+    out_ref[...] = value_ref[...]
+    copies = []
+    for turn, neighbour in enumerate(neighbours):
+        plane_buf[turn, 0] = out_ref[...]
+        copies.append(
+            pltpu.make_async_remote_copy(
+                src_ref=plane_buf.at[turn, 0],
+                dst_ref=plane_buf.at[turn, 1],
+                send_sem=plane_send.at[turn],
+                recv_sem=plane_recv.at[turn],
+                device_id={"seq": neighbour},
+                device_id_type=MESH,
+            )
+        )
+        copies[-1].start()
+        copies[-1].wait_recv()
+        out_ref[...] = plane_buf[turn, 0] + plane_buf[turn, 1]
+    if over_layers:
+        layer_buf[layer] = out_ref[...]
+        layer_copies = [
+            pltpu.make_async_remote_copy(
+                src_ref=layer_buf.at[layer],
+                dst_ref=layer_buf.at[layer],
+                send_sem=layer_send.at[hop],
+                recv_sem=layer_recv.at[hop],
+                device_id={"fsdp": other},
+                device_id_type=MESH,
+            )
+            for hop, other in enumerate(others)
+        ]
+        for copy in layer_copies:
+            copy.start()
+        for copy in layer_copies:
+            copy.wait_recv()
+        total = layer_buf[0]
+        for index in range(1, layers):
+            total = total + layer_buf[index]
+        out_ref[...] = total
+        copies += layer_copies
+    for copy in copies:
+        copy.wait_send()
+
+
+def small_sum(value, over_layers, ident, name):
+    layers = lax.axis_size("fsdp")
+    semaphores = pltpu.SemaphoreType.DMA
+    return pl.pallas_call(
+        functools.partial(small_sum_kernel, over_layers),
+        in_specs=[pl.BlockSpec(memory_space=pltpu.VMEM)],
+        out_specs=pl.BlockSpec(memory_space=pltpu.VMEM),
+        out_shape=jax.ShapeDtypeStruct(value.shape, jnp.float32),
+        scratch_shapes=[
+            pltpu.VMEM((3, 2) + value.shape, jnp.float32),
+            pltpu.VMEM((layers,) + value.shape, jnp.float32),
+            semaphores((3,)),
+            semaphores((3,)),
+            semaphores((layers,)),
+            semaphores((layers,)),
+        ],
+        compiler_params=pltpu.CompilerParams(collective_id=ident, has_side_effects=True),
+        name=name,
+    )(value)
+
+
+def tiles(width, tile, body):
     def step(index, carry):
-        body(pl.ds(pl.multiple_of(index * tile, tile), tile))
+        body(pl.ds(pl.multiple_of(index * tile, 128), tile))
         return carry
 
     lax.fori_loop(0, width // tile, step, 0)
@@ -497,55 +709,65 @@
     return gate * half, slope
 
 
-def hidden_compute(x_buf, weights, extras, outs):
-    gate_w, up_w = weights
+def add_outer(left, right, total, first):
+    def body(span):
+        outer = lax.dot_general(
+            left[:, span], right[...], (((0,), (0,)), ((), ())), preferred_element_type=jnp.float32
+        )
+        total[span, :] = outer if first else total[span, :] + outer
+
+    tiles(left.shape[1], BRAID, body)
+
+
+def hidden_compute(x_buf, weights, extras, outs, sums, first):
     gate_out, up_out, hidden_out = outs
-
-    def body(span):
-        gate = final_dot(x_buf[...], gate_w[:, span])
-        up = final_dot(x_buf[...], up_w[:, span])
+    (weight,) = weights
+
+    def step(index, carry):
+        both = pl.ds(pl.multiple_of(index * 2 * BRAID, 128), 2 * BRAID)
+        span = pl.ds(pl.multiple_of(index * BRAID, 128), BRAID)
+        product = final_dot(x_buf[...], weight[:, both])
+        gate, up = product[:, :BRAID], product[:, BRAID:]
         gate_out[:, span] = gate.astype(gate_out.dtype)
         up_out[:, span] = up.astype(up_out.dtype)
         hidden_out[:, span] = (gelu_parts(gate)[0] * up).astype(hidden_out.dtype)
-
-    tiles(gate_w.shape[1], body)
-
-
-def hidden_back_compute(x_buf, weights, extras, outs):
+        return carry
+
+    lax.fori_loop(0, weight.shape[1] // (2 * BRAID), step, 0)
+
+
+def hidden_back_compute(x_buf, weights, extras, outs, sums, first):
     (down_w,) = weights
-    gate_in, up_in = extras
+    gate_in, up_in, hidden_in = extras
     gate_out, up_out = outs
-
-    def body(span):
-        grad = dot_back(x_buf[...], down_w[span, :])
+    product = dot_back(x_buf[...], down_w[...])
+    for start in range(0, product.shape[1], BRAID):
+        span = slice(start, start + BRAID)
+        grad = product[:, span]
         value, slope = gelu_parts(gate_in[:, span].astype(jnp.float32))
         gate_out[:, span] = (grad * up_in[:, span].astype(jnp.float32) * slope).astype(
             gate_out.dtype
         )
         up_out[:, span] = (grad * value).astype(up_out.dtype)
-
-    tiles(down_w.shape[0], body)
-
-
-def rows_compute(parts, weights, out):
+    add_outer(hidden_in, x_buf, sums[0], first)
+
+
+def head_back_compute(x_buf, weights, extras, outs, sums, first):
+    outs[0][...] = dot_back(x_buf[...], weights[0][...]).astype(outs[0].dtype)
+
+
+def rows_compute(part, weight, out):
     def body(span):
-        out[:, span] = final_dot(parts[0][...], weights[0][:, span]).astype(out.dtype)
-
-    tiles(weights[0].shape[1], body)
-
-
-def back_compute(parts, weights, out):
+        out[:, span] = final_dot(part[...], weight[:, span]).astype(out.dtype)
+
+    tiles(weight.shape[1], 2 * BRAID, body)
+
+
+def back_compute(part, weight, out):
     def body(span):
-        total = dot_back(parts[0][...], weights[0][span, :])
-        for part, weight in zip(parts[1:], weights[1:]):
-            total = total + dot_back(part[...], weight[span, :])
-        out[:, span] = total.astype(out.dtype)
-
-    tiles(weights[0].shape[0], body)
-
-
-def head_back_compute(x_buf, weights, extras, outs):
-    outs[0][...] = dot_back(x_buf[...], weights[0][...]).astype(outs[0].dtype)
+        out[:, span] = dot_back(part[...], weight[span, :]).astype(out.dtype)
+
+    tiles(weight.shape[0], 2 * BRAID, body)
 
 
 def score_parts(query, key, low_bound, row_start, col_start):
@@ -603,9 +825,7 @@
     log_ref,
     cos_ref,
     sin_ref,
-    dq_ref,
-    low_out_ref,
-    high_out_ref,
+    grad_ref,
     dk_ref,
     dv_ref,
 ):
@@ -633,7 +853,8 @@
         grad_score = (prob * (grad_prob - delta) * (1.0 - bent * bent)).astype(jnp.bfloat16)
         dq = jnp.dot(grad_score, key, preferred_element_type=jnp.float32)
         dq = dq * (1.0 / math.sqrt(HEAD_SIZE))
-        dq_ref[...] = turn_back(dq, cos_ref[own, :], sin_ref[own, :]).astype(jnp.bfloat16)
+        dq = turn_back(dq, cos_ref[own, :], sin_ref[own, :])
+        grad_ref[own, :HEAD_SIZE] = dq.astype(jnp.bfloat16)
         across = (((0,), (0,)), ((), ()))
         dk_ref[span, :] += lax.dot_general(
             grad_score, query, across, preferred_element_type=jnp.float32
@@ -650,12 +871,9 @@
 
     @pl.when(index == steps - 1)
     def _():
-        half = HEAD_SIZE // 2
         dk = turn_back(dk_ref[...], cos_ref[...], sin_ref[...])
-        for part, out_ref in enumerate((low_out_ref, high_out_ref)):
-            lanes = slice(part * half, (part + 1) * half)
-            out_ref[:, :half] = dk[:, lanes].astype(jnp.bfloat16)
-            out_ref[:, half:] = dv_ref[:, lanes].astype(jnp.bfloat16)
+        grad_ref[:, HEAD_SIZE : 2 * HEAD_SIZE] = dk.astype(jnp.bfloat16)
+        grad_ref[:, 2 * HEAD_SIZE :] = dv_ref[...].astype(jnp.bfloat16)
 
 
 def block_shape(length):
@@ -672,6 +890,68 @@
     rows = pl.BlockSpec((None, block, HEAD_SIZE), lambda m, i: (m, i, 0))
     line = pl.BlockSpec((None, block, 1), lambda m, i: (m, i, 0))
     return whole, half, rows, line
+
+
+def project_kernel(x_ref, w_ref, cos_ref, sin_ref, q_ref, k_ref, v_ref):
+    product = final_dot(x_ref[...], w_ref[...])
+    cosine, sine = cos_ref[...], sin_ref[...]
+    query, key = product[:, :HEAD_SIZE], product[:, HEAD_SIZE : 2 * HEAD_SIZE]
+    query = rotate(query, cosine, sine, 1.0) * (1.0 / math.sqrt(HEAD_SIZE))
+    q_ref[...] = query.astype(jnp.bfloat16)
+    k_ref[...] = rotate(key, cosine, sine, 1.0).astype(jnp.bfloat16)
+    v_ref[...] = product[:, 2 * HEAD_SIZE :].astype(jnp.bfloat16)
+
+
+def project(whole, weight, cosine, sine):
+    batches, length, width = whole.shape
+    block = block_shape(length)[0]
+    _, _, rows, _ = attend_specs(length, block)
+    half = pl.BlockSpec((None, block, HEAD_SIZE // 2), lambda m, i: (m, i, 0))
+    return pl.pallas_call(
+        project_kernel,
+        grid=(batches, length // block),
+        in_specs=[
+            pl.BlockSpec((None, block, width), lambda m, i: (m, i, 0)),
+            pl.BlockSpec(weight.shape, lambda m, i: (0, 0)),
+            half,
+            half,
+        ],
+        out_specs=[rows] * 3,
+        out_shape=[jax.ShapeDtypeStruct((batches, length, HEAD_SIZE), jnp.bfloat16)] * 3,
+        compiler_params=pltpu.CompilerParams(vmem_limit_bytes=40 * 2**20),
+        cost_estimate=pl.CostEstimate(
+            flops=6 * batches * length * width * HEAD_SIZE,
+            bytes_accessed=2 * batches * length * width,
+            transcendentals=0,
+        ),
+        name="project",
+    )(whole, weight, cosine, sine)
+
+
+def token_tables(tables, made):
+    counts_ref, frequency_ref = tables
+    cos_ref, sin_ref, low_ref = made
+    batches, length, _ = cos_ref.shape
+    block = block_shape(length)[0]
+    for batch in range(batches):
+
+        def step(index, carry, batch=batch):
+            span = pl.ds(pl.multiple_of(index * block, 16), block)
+            place = index * block + lax.broadcasted_iota(jnp.int32, (block, HEAD_SIZE // 2), 0)
+            place = place.astype(jnp.float32)
+            start = jnp.zeros_like(place)
+            for number in range(1, DOCUMENTS):
+                row = batch * (DOCUMENTS - 1) + number - 1
+                count = counts_ref[row : row + 1, :]
+                start = jnp.where(place >= count, count, start)
+            phase_angle = (place - start) * frequency_ref[...]
+            cos_ref[batch, span, :] = jnp.cos(phase_angle)
+            sin_ref[batch, span, :] = jnp.sin(phase_angle)
+            low = jnp.maximum(start, place - (WIN - 1))
+            low_ref[batch, span, :] = low[:, :1].astype(jnp.int32)
+            return carry
+
+        lax.fori_loop(0, length // block, step, 0)
 
 
 def attend(query, key, value, low_bound):
@@ -707,8 +987,8 @@
         functools.partial(attend_back_kernel, block, reach),
         grid=(batches, length // block),
         in_specs=[rows, whole, whole, rows, line, line, half, half],
-        out_specs=[rows, whole, whole],
-        out_shape=[jax.ShapeDtypeStruct((batches, length, HEAD_SIZE), jnp.bfloat16)] * 3,
+        out_specs=pl.BlockSpec((None, length, 3 * HEAD_SIZE), lambda m, i: (m, 0, 0)),
+        out_shape=jax.ShapeDtypeStruct((batches, length, 3 * HEAD_SIZE), jnp.bfloat16),
         scratch_shapes=[pltpu.VMEM((length, HEAD_SIZE), jnp.float32)] * 2,
         compiler_params=pltpu.CompilerParams(vmem_limit_bytes=48 * 2**20),
         cost_estimate=pl.CostEstimate(
@@ -750,68 +1030,94 @@
         part = gather_rows(part.reshape(here * depth, -1))
         self.out_rows = swap_parts(part, 0, 0)
 
-    def forward(self, normed, seg_whole):
-        batches, length = seg_whole.shape
-        (whole,) = plane_gather(normed, 0, "gather_normed")
-        starts = doc_starts(seg_whole)
-        places = jnp.arange(length, dtype=jnp.int32)
-        low_bound = jnp.maximum(starts, places - (WIN - 1))[..., None]
-        cosine, sine = angles(places - starts, HEAD_SIZE)
-        rows = final_dot(whole, self.weights)
-        query, key, value = (rows[..., HEAD_SIZE * i : HEAD_SIZE * (i + 1)] for i in range(3))
-        query = rotate(query, cosine, sine, 1.0) * (1.0 / math.sqrt(HEAD_SIZE))
-        query = query.astype(jnp.bfloat16)
-        key = rotate(key, cosine, sine, 1.0).astype(jnp.bfloat16)
-        value = value.astype(jnp.bfloat16)
+    def forward(self, normed, segments):
+        batches, rows, width = normed.shape
+        length = rows * lax.axis_size("seq")
+        half = HEAD_SIZE // 2
+        counts = [
+            jnp.sum((segments[batch] < number).astype(jnp.float32))
+            for batch in range(batches)
+            for number in range(1, DOCUMENTS)
+        ]
+        counts += [jnp.zeros(())] * (8 - len(counts))
+        counts = jnp.broadcast_to(jnp.stack(counts)[:, None], (8, half))
+        counts = small_sum(counts, False, 8, "sum_counts")
+        frequency = 10000.0 ** (-jnp.arange(half, dtype=jnp.float32) * 2.0 / HEAD_SIZE)
+        table = jax.ShapeDtypeStruct((batches, length, half), jnp.float32)
+        bound = jax.ShapeDtypeStruct((batches, length, 1), jnp.int32)
+        whole, cosine, sine, low_bound = plane_gather(
+            normed,
+            0,
+            "gather_normed",
+            Job(
+                None,
+                tables=[counts, frequency[None]],
+                spare=(token_tables, [table, table, bound]),
+            ),
+        )
+        query, key, value = project(whole, self.weights, cosine, sine)
         attended, log_total = attend(query, key, value, low_bound)
-        width = normed.shape[-1]
-        flops = 2 * batches * length * HEAD_SIZE * width
-        mixed = plane_scatter(
-            [attended], [self.out_rows], rows_compute, width, 1, "scatter_mixed", flops
-        )
+        job = Job(
+            rows_compute, weights=[self.out_rows], flops=2 * batches * length * HEAD_SIZE * width
+        )
+        (mixed,) = plane_scatter([attended], width, 1, "scatter_mixed", job)
         return mixed, (whole, query, key, value, low_bound, log_total, cosine, sine, attended)
 
-    def backward(self, grad_mixed_b, saved):
+    def backward(self, grad_mixed_b, saved, side, meanwhile):
         whole, query, key, value, low_bound, log_total, cosine, sine, attended = saved
         batches, length = key.shape[:2]
         width = grad_mixed_b.shape[-1]
-        count = lax.axis_size("seq")
-        grad_whole, grad_att = plane_gather(
-            grad_mixed_b,
-            2,
-            "gather_grad_mixed",
+        job = Job(
+            head_back_compute,
             weights=[self.out_rows],
             outs=[(HEAD_SIZE, jnp.bfloat16)],
-            compute=head_back_compute,
-            flops=2 * batches * length * HEAD_SIZE * width,
-        )
-        dq, low, high = attend_back(
+            side=side,
+            sums=[(side[0].shape[2], side[1].shape[2])],
+            flops=2 * batches * length * (HEAD_SIZE * width + side[0].shape[2] * side[1].shape[2]),
+        )
+        grad_whole, grad_att, side_sum = plane_gather(grad_mixed_b, 2, "gather_grad_mixed", job)
+        grad_att, meanwhile = lax.optimization_barrier((grad_att, scatter_rows(meanwhile)))
+        grads = attend_back(
             query, key, value, grad_att, low_bound, log_total, cosine, sine
         )
+        self.record = (whole, grads, attended, grad_whole)
+        job = Job(
+            back_compute, weights=[self.weights], flops=6 * batches * length * HEAD_SIZE * width
+        )
+        (grad_normed,) = plane_scatter([grads], width, 3, "scatter_grad_normed", job)
+        return grad_normed, side_sum, meanwhile
+
+    def weight_grads(self):
+        half = HEAD_SIZE // 2
+        count = lax.axis_size("seq")
+        layers = lax.axis_size("fsdp")
+        whole, grads, attended, grad_whole = self.record
+        joined = dot_rows(whole, grads).astype(jnp.bfloat16)
+        k_low, k_high, v_low, v_high = (
+            joined[:, HEAD_SIZE + half * i : HEAD_SIZE + half * (i + 1)] for i in range(4)
+        )
+        low = jnp.concatenate([k_low, v_low], axis=1)
+        high = jnp.concatenate([k_high, v_high], axis=1)
         odd = lax.axis_index("seq") % 2 == 1
         came = lax.ppermute(
             jnp.where(odd, low, high), "seq", [(i, i ^ 1) for i in range(count)]
         )
         kept = jnp.where(odd, high, low)
-        dkv = (kept.astype(jnp.float32) + came.astype(jnp.float32)).astype(jnp.bfloat16)
-        grads = jnp.concatenate([dq, dkv], axis=-1)
-        self.record = (whole, grads, attended, grad_whole)
-        flops = 4 * batches * length * HEAD_SIZE * width
-        return plane_scatter(
-            [grads], [self.joined], back_compute, width, 3, "scatter_grad_normed", flops
-        )
-
-    def weight_grads(self):
-        half = HEAD_SIZE // 2
-        whole, grads, attended, grad_whole = self.record
+        kept = (kept.astype(jnp.float32) + came.astype(jnp.float32)).astype(jnp.bfloat16)
+        joined = scatter_rows(jnp.concatenate([joined[:, :HEAD_SIZE], kept], axis=1))
+
+        width = grad_whole.shape[-1]
         out = dot_rows(attended, grad_whole).astype(jnp.bfloat16)
-        out = scatter_rows(swap_parts(out, 1, 0))
-        joined = scatter_rows(dot_rows(whole, grads))
+        out = scatter_rows(swap_parts(out, 0, 0))
+        here = QUERY_HEADS // layers
+        out = swap_parts(out.reshape(1, here, HEAD_SIZE // count, width), 3, 0)
+        out = out.transpose(1, 0, 2, 3).reshape(here * HEAD_SIZE, -1)
+        joined = joined.astype(jnp.float32)
         return (
             joined[:, :HEAD_SIZE],
             joined[:, HEAD_SIZE : HEAD_SIZE + half],
             joined[:, HEAD_SIZE + half :],
-            out,
+            out.astype(jnp.float32),
         )
 
 
@@ -820,7 +1126,8 @@
         self.weights = fetch_attention(w_query, key_weight, value_weight, w_out)
         self.records = []
 
-    def forward(self, normed, seg_whole):
+    def forward(self, normed, segments):
+        seg_whole = lax.all_gather(segments, "seq", axis=1, tiled=True)
         done = [self.forward_one(*pair) for pair in zip(normed, seg_whole)]
         return jnp.stack([mixed for mixed, _ in done]), [saved for _, saved in done]
 
@@ -866,8 +1173,9 @@
         log_total = peak + jnp.log(total)
         return mixed, (normed, query, pair, allowed, log_total, cosine, sine, attended)
 
-    def backward(self, grad_mixed_b, saved):
-        return jnp.stack([self.backward_one(*pair) for pair in zip(grad_mixed_b, saved)])
+    def backward(self, grad_mixed_b, saved, side, meanwhile):
+        grads = [self.backward_one(*pair) for pair in zip(grad_mixed_b, saved)]
+        return jnp.stack(grads), dot_rows(*side), scatter_rows(meanwhile)
 
     def backward_one(self, grad_mixed_b, saved):
         normed, query, pair, allowed, log_total, cosine, sine, attended = saved
@@ -943,19 +1251,17 @@
         hidden_width, width = self.down.shape
         if self.by_kernel:
             rows = ffn_in.shape[0] * ffn_in.shape[1] * lax.axis_size("seq")
-            whole, gate_proj, up_proj, hidden = plane_gather(
-                ffn_in,
-                4,
-                "gather_ffn_in",
+            job = Job(
+                hidden_compute,
                 weights=[self.gate, self.up],
                 outs=[(hidden_width, jnp.bfloat16)] * 3,
-                compute=hidden_compute,
                 flops=4 * rows * width * hidden_width,
             )
-            flops = 2 * rows * width * hidden_width
-            down_proj = plane_scatter(
-                [hidden], [self.down], rows_compute, width, 5, "scatter_down", flops
+            whole, gate_proj, up_proj, hidden = plane_gather(ffn_in, 4, "gather_ffn_in", job)
+            job = Job(
+                rows_compute, weights=[self.down], flops=2 * rows * width * hidden_width
             )
+            (down_proj,) = plane_scatter([hidden], width, 5, "scatter_down", job)
         else:
             whole = lax.all_gather(ffn_in, "seq", axis=1, tiled=True)
             gate_proj = final_dot(whole, self.gate)
@@ -974,24 +1280,26 @@
         hidden_width, width = self.down.shape
         if self.by_kernel:
             rows = whole.shape[0] * whole.shape[1]
-            grad_whole, grad_gate, grad_up = plane_gather(
-                grad_down_b,
-                6,
-                "gather_grad_down",
+            job = Job(
+                hidden_back_compute,
                 weights=[self.down],
-                extras=[gate_proj, up_proj],
+                extras=[gate_proj, up_proj, hidden],
                 outs=[(hidden_width, jnp.bfloat16)] * 2,
-                compute=hidden_back_compute,
-                flops=2 * rows * width * hidden_width,
+                sums=[(hidden_width, width)],
+                flops=4 * rows * width * hidden_width,
             )
-            grad_ffn_in = plane_scatter(
-                [grad_gate, grad_up],
-                [self.gate, self.up],
+            _, grad_gate, grad_up, self.down_sum = plane_gather(
+                grad_down_b, 6, "gather_grad_down", job
+            )
+            job = Job(
                 back_compute,
-                width,
-                7,
-                "scatter_grad_ffn_in",
-                4 * rows * width * hidden_width,
+                weights=[self.gate, self.up],
+                side=[whole, grad_gate],
+                sums=[(width, hidden_width)],
+                flops=6 * rows * width * hidden_width,
+            )
+            grad_ffn_in, self.gate_sum = plane_scatter(
+                [grad_gate, grad_up], width, 7, "scatter_grad_ffn_in", job
             )
         else:
             grad_whole = lax.all_gather(grad_down_b, "seq", axis=1, tiled=True)
@@ -1002,23 +1310,23 @@
             grad_ffn_in = lax.psum_scatter(
                 partial.astype(jnp.bfloat16), "seq", scatter_dimension=1, tiled=True
             ).astype(jnp.float32)
-        self.record = (whole, hidden, grad_whole, grad_gate, grad_up)
+            self.down_sum = dot_rows(hidden, grad_whole)
+            self.gate_sum = dot_rows(whole, grad_gate)
+        self.up_side = (whole, grad_up)
         return grad_ffn_in
 
-    def weight_grads(self):
-        whole, hidden, grad_whole, grad_gate, grad_up = self.record
+    def weight_grads(self, gate_own, up_own, down_own):
         count = lax.axis_size("seq")
 
-        down = scatter_rows(dot_rows(hidden, grad_whole)).astype(jnp.bfloat16)
+        down = down_own
         here = down.shape[0] // self.run
         down = swap_parts(down.reshape(1, here, self.run, -1), 3, 0)
         down = down.transpose(1, 0, 2, 3).reshape(here * count * self.run, -1)
 
-        def columns(grads):
-            summed = scatter_rows(dot_rows(whole, grads)).astype(jnp.bfloat16)
-            return swap_parts(summed, 1, 1).astype(jnp.float32)
-
-        return columns(grad_gate), columns(grad_up), down.astype(jnp.float32)
+        def columns(own):
+            return swap_parts(own, 1, 1).astype(jnp.float32)
+
+        return columns(gate_own), columns(up_own), down.astype(jnp.float32)
 
 
 def on_device(
@@ -1037,7 +1345,6 @@
     gain_ffn_out,
     cotangent,
 ):
-    seg_whole = lax.all_gather(segments, "seq", axis=2, tiled=True)[:, 0]
     by_kernel = (
         lax.axis_size("seq") == QUERY_HEADS
         and tokens.shape[0] == 2
@@ -1048,7 +1355,7 @@
 
     stream = tokens[:, 0].astype(jnp.float32)
     normed = rms_gain(stream, gain_attn_in).astype(jnp.bfloat16)
-    mixed, attention_saved = attention.forward(normed, seg_whole)
+    mixed, attention_saved = attention.forward(normed, segments[:, 0])
     middle = stream + rms_gain(mixed, gain_attn_out)
     ffn_in = rms_gain(middle, gain_ffn_in).astype(jnp.bfloat16)
     down_proj, ffn_saved = ffn.forward(ffn_in)
@@ -1063,16 +1370,25 @@
     grad_middle = grad_result + grad_middle
     _, pullback = jax.vjp(rms_gain, mixed, gain_attn_out)
     grad_mixed, grad_gain_two = pullback(grad_middle)
-    grad_normed = attention.backward(grad_mixed.astype(jnp.bfloat16), attention_saved)
+    grad_mixed, down_own = lax.optimization_barrier(
+        (grad_mixed.astype(jnp.bfloat16), scatter_rows(ffn.down_sum))
+    )
+    grad_normed, up_sum, gate_own = attention.backward(
+        grad_mixed, attention_saved, ffn.up_side, ffn.gate_sum
+    )
     _, pullback = jax.vjp(rms_gain, stream, gain_attn_in)
     grad_stream, grad_gain_one = pullback(grad_normed)
     grad_stream = grad_middle + grad_stream
 
-    w_gate_grad, w_up_grad, w_down_grad = ffn.weight_grads()
+    w_gate_grad, w_up_grad, w_down_grad = ffn.weight_grads(
+        gate_own, scatter_rows(up_sum), down_own
+    )
     query_grad, key_grad, value_grad, out_grad = attention.weight_grads()
-    gain_early = jnp.stack([grad_gain_two, grad_gain_three, grad_gain_four])
-    gain_early = lax.psum(gain_early, ("seq", "fsdp"))
-    gain_late = lax.psum(grad_gain_one, ("seq", "fsdp"))
+    gains = jnp.stack([grad_gain_one, grad_gain_two, grad_gain_three, grad_gain_four])
+    if by_kernel:
+        gains = small_sum(jnp.pad(gains, ((0, 4), (0, 0))), True, 9, "sum_gains")
+    else:
+        gains = lax.psum(gains, ("seq", "fsdp"))
     return (
         result.astype(jnp.bfloat16)[:, None],
         grad_stream[:, None],
@@ -1083,10 +1399,10 @@
         w_gate_grad,
         w_up_grad,
         w_down_grad,
-        gain_late,
-        gain_early[0],
-        gain_early[1],
-        gain_early[2],
+        gains[0],
+        gains[1],
+        gains[2],
+        gains[3],
     )
 
 

time: 1340 us -> 1160 us (0.87)
  matrix products: 130 us -> 29.1 us
  blocking collectives: 79.9 us -> 21.2 us
  Pallas kernels: 904 us -> 853 us
  waiting for transfers between devices: 23.3 us -> 58.8 us
  other arithmetic: 83.2 us -> 55.9 us
  local copies, waits for them, and re-layouts: 78.8 us -> 99.8 us
    dot_general x5 -> x2, matrix products: 112 us -> 29.1 us  [dot_rows(): lax.dot_general(left_side, right_side, (((0,), (0,)), ((), ())), preferre...]
    pallas_call x8 -> x11, Pallas kernels: 862 us -> 810 us  [the longest x4 392 us: plane_scatter(): pl.pallas_call(functools.partial(scatter_kernel, job, rows), in_specs=[an...]
    psum x1 -> x0, blocking collectives: 47.3 us -> none  [on_device(): gain_late = lax.psum(grad_gain_one, ('seq', 'fsdp'))]
    all_gather x5, waiting for transfers between devices: 0.05 us -> 36.2 us  [gather_rows(): return lax.all_gather(rows, 'fsdp', axis=0, tiled=True)]
    dot_general x1 -> x0, matrix products: 17.2 us -> none  [final_dot(): return jnp.dot(left_side, right_side, preferred_element_type=jnp.float32)]
    unnamed x101 -> x125, local copies, waits for them, and re-layouts: 21.3 us -> 36.6 us
  transfers between devices with their start and end apart: 16 -> 17, of which waited for: 1 -> 2; matrix products, arithmetic and copies ran while one was open for 17% -> 13% of each run, Pallas kernels for 51% -> 57%
where the time goes in v3:
time: 1160 us; the launch traced here: 1150 us
  Pallas kernels  853 us (74%)
  local copies, waits for them, and re-layouts  99.8 us (9%)
  waiting for transfers between devices  58.8 us (5%)
  other arithmetic  55.9 us (5%)
  matrix products  29.1 us (3%)
  blocking collectives  21.2 us (2%)
  starting transfers between devices  20.8 us (2%)
  between operations  15.5 us (1%)
    pallas_call x4, Pallas kernels, plane_scatter(): pl.pallas_call(functools.partial(scatter_kernel, job, rows), in_specs=[an...  392 us
    pallas_call x4, Pallas kernels, plane_gather(): pl.pallas_call(functools.partial(gather_kernel, job, rows), in_specs=in_s...  362 us
    pallas_call x2, Pallas kernels, small_sum(): pl.pallas_call(functools.partial(small_sum_kernel, over_layers), in_specs...  37.7 us
    unnamed x125, local copies, waits for them, and re-layouts  36.6 us
    all_gather x5, waiting for transfers between devices, gather_rows(): return lax.all_gather(rows, 'fsdp', axis=0, tiled=True)  36.2 us
    dot_general x2, matrix products, dot_rows(): lax.dot_general(left_side, right_side, (((0,), (0,)), ((), ())), preferre...  29.1 us
    pallas_call x1, Pallas kernels, attend_back(): pl.pallas_call(functools.partial(attend_back_kernel, block, reach), grid=...  27.3 us
  transfers between devices with their start and end apart: 17, of which 2 were waited for; matrix products, arithmetic and copies ran while one was open for 13% of the time, Pallas kernels for 57%

profile of v3, /device:TPU:0, one launch (start us, length us, event | category | flops | bytes accessed | tf_op | source)
XLA Modules:
  0.0 1154.3 jit_solution(18432950653256306357)
XLA Ops:
  11.2 6.5 constant_dynamic-slice_fusion.1
  17.7 4.0 concatenate.24
  21.8 2.4 concatenate.23
  24.2 2.7 constant_dynamic-slice_fusion
  27.5 36.2 %all-gather.6.cloned.1.call-done = bf16[2304,512]{1,0:T(8,128)(2,1)} async-done(((bf16[576,512]{1,0:T(8,128)(2,1)}), bf16[2304,512]{1,0:T(8,128)(2,1)}) %all-gather.6.cloned.1.call-update) | async-done | bytes 2359312 | tf_op jit(solution)/shard_map/all_gather | solution.py:122
  63.6 2.4 slice.87
  66.6 4.0 stack.42
  71.3 9.0 sum_counts.1.refs_1_
  83.3 82.2 %gather_normed.1 = (bf16[2,1920,2304]{2,1,0:T(8,128)(2,1)}, f32[2,1920,128]{2,1,0:T(8,128)}, f32[2,1920,128]{2,1,0:T(8,128)}, s32[2,1920,1]{2,1,0:T(8,128)}) custom-call(bf16[2,240,2304]{2,1,0:T(8,128)(2,1)} %fusion.4.refs_0_, f32[8,128]{1,0:T(8,128)} %sum_counts.1.refs_1_, f32[1,128]{1,0:T(1,128)} %multiply_power_fusion.refs_2_), custom_call_target="tpu_custom_call" | custom-call | bytes 270000000 | tf_op jit(solution)/shard_map/gather_normed/pallas_call | solution.py:432
  165.5 4.3 all-to-all-start
  173.7 17.4 %project.1 = (bf16[2,1920,256]{2,1,0:T(8,128)(2,1)S(1)}, bf16[2,1920,256]{2,1,0:T(8,128)(2,1)S(1)}, bf16[2,1920,256]{2,1,0:T(8,128)(2,1)S(1)}) custom-call(bf16[2,1920,2304]{2,1,0:T(8,128)(2,1)} %get-tuple-element.38.x_ref, bf16[2304,768]{1,0:T(8,128)(2,1)S(1)} %slice_dynamic-update-slice_fusion.1.w_ref.refs_1_, f32[2,1920,128]{2,1,0:T(8,128)S(1)} %copy-done.5, ...), custom_call_target="tpu_custom_call" | custom-call | flops 13589544960 | bytes 17694720 | tf_op jit(solution)/shard_map/project/pallas_call | solution.py:910
  191.2 15.9 %attend.1 = (bf16[2,1920,256]{2,1,0:T(8,128)(2,1)S(1)}, f32[2,1920,1]{2,1,0:T(8,128)S(1)}) custom-call(bf16[2,1920,256]{2,1,0:T(8,128)(2,1)S(1)} %get-tuple-element.41.q_ref, bf16[2,1920,256]{2,1,0:T(8,128)(2,1)S(1)} %get-tuple-element.42.k_ref, bf16[2,1920,256]{2,1,0:T(8,128)(2,1)S(1)} %get-tuple-element.43.v_ref, s32[2,1920,1]{2,1,0:T(8,128)S(1)} %copy-done.7), custom_call_target="tpu_custom_call" | custom-call | flops 6039797760 | bytes 9830400 | tf_op jit(solution)/shard_map/attend/pallas_call | solution.py:962
  213.5 85.6 %scatter_mixed.1 = f32[2,240,2304]{2,1,0:T(8,128)} custom-call(bf16[2,1920,256]{2,1,0:T(8,128)(2,1)} %copy-done.2, bf16[256,2304]{1,0:T(8,128)(2,1)} %bitcast.13.refs_1_), custom_call_target="tpu_custom_call" | custom-call | flops 4529848320 | bytes 270000000 | tf_op jit(solution)/shard_map/scatter_mixed/pallas_call | solution.py:601
  299.2 3.1 multiply_reduce_fusion.6
  308.5 93.1 %gather_ffn_in.1 = (bf16[2,1920,2304]{2,1,0:T(8,128)(2,1)}, bf16[2,1920,1152]{2,1,0:T(8,128)(2,1)}, bf16[2,1920,1152]{2,1,0:T(8,128)(2,1)}, bf16[2,1920,1152]{2,1,0:T(8,128)(2,1)}) custom-call(bf16[2,240,2304]{2,1,0:T(8,128)(2,1)} %multiply_convert_fusion.refs_0_, bf16[2304,1152]{1,0:T(8,128)(2,1)} %all-gather.10.cloned.1.call-done.refs_1_.refs_2_, ...), custom_call_target="tpu_custom_call" | custom-call | flops 40768634880 | bytes 270000000 | tf_op jit(solution)/shard_map/gather_ffn_in/pallas_call | solution.py:432
  401.7 92.5 %scatter_down.1 = f32[2,240,2304]{2,1,0:T(8,128)} custom-call(bf16[2,1920,1152]{2,1,0:T(8,128)(2,1)} %get-tuple-element.46.refs_0_.refs_4_, bf16[1152,2304]{1,0:T(8,128)(2,1)} %all-gather.14.cloned.1.call-done.refs_1_), custom_call_target="tpu_custom_call" | custom-call | flops 20384317440 | bytes 270000000 | tf_op jit(solution)/shard_map/scatter_down/pallas_call | solution.py:601
  494.3 2.8 multiply_reduce_fusion.4
  499.7 3.5 fusion.7
  503.3 100.9 %gather_grad_down.1 = (bf16[2,1920,2304]{2,1,0:T(8,128)(2,1)}, bf16[2,1920,1152]{2,1,0:T(8,128)(2,1)}, bf16[2,1920,1152]{2,1,0:T(8,128)(2,1)}, bf16[1152,2304]{1,0:T(8,128)(2,1)}) custom-call(bf16[2,240,2304]{2,1,0:T(8,128)(2,1)} %get-tuple-element.178.refs_0_, bf16[1152,2304]{1,0:T(8,128)(2,1)} %all-gather.14.cloned.1.call-done.refs_1_, ...), custom_call_target="tpu_custom_call" | custom-call | flops 40768634880 | bytes 270000000 | tf_op jit(solution)/shard_map/gather_grad_down/pallas_call | solution.py:432
  604.3 119.9 %scatter_grad_ffn_in.1 = (f32[2,240,2304]{2,1,0:T(8,128)}, bf16[2304,1152]{1,0:T(8,128)(2,1)}) custom-call(bf16[2,1920,1152]{2,1,0:T(8,128)(2,1)} %get-tuple-element.49.refs_0_.refs_5_, bf16[2,1920,1152]{2,1,0:T(8,128)(2,1)} %get-tuple-element.50.refs_1_.refs_3_, bf16[2304,1152]{1,0:T(8,128)(2,1)} %all-gather.10.cloned.1.call-done.refs_1_.refs_2_, ...), custom_call_target="tpu_custom_call" | custom-call | flops 61152952320 | bytes 270000000 | tf_op jit(solution)/shard_map/scatter_grad_ffn_in/pallas_call | solution.py:601
  724.9 5.8 multiply_reduce_fusion
  730.8 5.7 multiply_reduce_fusion.1
  740.9 86.3 %gather_grad_mixed.1 = (bf16[2,1920,2304]{2,1,0:T(8,128)(2,1)}, bf16[2,1920,256]{2,1,0:T(8,128)(2,1)}, bf16[2304,1152]{1,0:T(8,128)(2,1)}) custom-call(bf16[2,240,2304]{2,1,0:T(8,128)(2,1)} %fusion.8.refs_0_, bf16[256,2304]{1,0:T(8,128)(2,1)} %bitcast.13.refs_1_, bf16[2,1920,2304]{2,1,0:T(8,128)(2,1)} %get-tuple-element.51.refs_4_.refs_2_, ...), custom_call_target="tpu_custom_call" | custom-call | flops 24914165760 | bytes 270000000 | tf_op jit(solution)/shard_map/gather_grad_mixed/pallas_call | solution.py:432
  827.2 9.3 fusion.14
  836.5 21.2 %all_to_all.65 = bf16[8,32,2304]{2,1,0:T(8,128)(2,1)} all-to-all(bf16[8,32,2304]{2,1,0:T(8,128)(2,1)S(1)} %bitcast.91), channel_id=1, replica_groups=mesh['seq'=8,'fsdp'=4] {'seq'}, dimensions={0} | all-to-all | bytes 2359296 | tf_op jit(solution)/shard_map/all_to_all | solution.py:132
  862.6 27.3 %attend_back.1.refs_0_ = bf16[2,1920,768]{2,1,0:T(8,128)(2,1)} custom-call(bf16[2,1920,256]{2,1,0:T(8,128)(2,1)S(1)} %copy-done.9, bf16[2,1920,256]{2,1,0:T(8,128)(2,1)S(1)} %copy-done.11, bf16[2,1920,256]{2,1,0:T(8,128)(2,1)S(1)} %copy-done.13, bf16[2,1920,256]{2,1,0:T(8,128)(2,1)} %get-tuple-element.57.g_ref, s32[2,1920,1]{2,1,0:T(8,128)} %get-tuple-element.44.low_ref, ...), custom_call_target="tpu_custom_call" | custom-call | flops 15099494400 | bytes 23592960 | tf_op jit(solution)/shard_map/attend_back/pallas_call | solution.py:986
  889.9 19.7 %bitcast_convert_fusion = bf16[2304,768]{1,0:T(8,128)(2,1)S(1)} fusion(bf16[2,1920,2304]{2,1,0:T(8,128)(2,1)} %get-tuple-element.38.x_ref, bf16[2,1920,768]{2,1,0:T(8,128)(2,1)} %attend_back.1.refs_0_), kind=kOutput, calls=%fused_computation.5 | convolution fusion | flops 13591314432 | bytes 27131904 | tf_op jit(solution)/shard_map/dot_general | solution.py:77
  911.9 6.6 copy.118
  918.4 3.6 all-to-all-start.5
  927.2 2.6 copy.116
  929.8 21.6 %all-to-all-done.5 = bf16[1,2,144,2304]{2,1,0,3:T(2,128)(2,1)S(1)} async-done(((bf16[1,2,144,2304]{2,1,0,3:T(2,128)(2,1)}), bf16[1,2,144,2304]{2,1,0,3:T(2,128)(2,1)S(1)}, u32[]{:S(2)}, u32[]{:S(2)}) %all-to-all-start.5) | async-done | bytes 1327136 | tf_op jit(solution)/shard_map/all_to_all | solution.py:132
  952.9 4.5 all-to-all-start.3
  957.4 94.3 %scatter_grad_normed.1 = f32[2,240,2304]{2,1,0:T(8,128)} custom-call(bf16[2,1920,768]{2,1,0:T(8,128)(2,1)} %attend_back.1.refs_0_, bf16[2304,768]{1,0:T(8,128)(2,1)} %copy-done.4), custom_call_target="tpu_custom_call" | custom-call | flops 13589544960 | bytes 270000000 | tf_op jit(solution)/shard_map/scatter_grad_normed/pallas_call | solution.py:601
  1051.7 3.6 fusion.5
  1055.3 3.0 copy.113
  1060.1 3.4 all-to-all-start.2
  1063.5 6.8 fusion.10
  1070.4 2.6 copy.117
  1073.0 4.6 all-to-all-start.4
  1078.3 28.8 %sum_gains.1 = f32[8,2304]{1,0:T(8,128)} custom-call(f32[8,2304]{1,0:T(8,128)} %select_maximum_fusion.value_ref), custom_call_target="tpu_custom_call" | custom-call | tf_op jit(solution)/shard_map/sum_gains/pallas_call | solution.py:674
  1108.8 3.1 bitcast_convert_fusion.2
  1112.0 3.6 copy.124
  1115.6 4.2 copy.119
  1119.7 4.9 reshape.211
  1124.7 4.5 copy.120
  1129.1 3.6 copy.126
  1140.2 3.3 bitcast_convert_fusion.1
  1143.5 3.4 copy.125
  (202 shorter events, 58.5 us)
Async XLA Ops:
  7.2 56.4 %all-gather.6.cloned.1.call-start = ((), (), s32[]{:S(2)}) async-start(), calls=%async_computation.11 | async-start | bytes 2949120 | tf_op jit(solution)/shard_map/all_gather | solution.py:122
  10.3 155.2 %all-gather.8.cloned.1.call-start = ((), (), s32[]{:S(2)}) async-start(), calls=%async_computation.12 | async-start | bytes 1474560 | tf_op jit(solution)/shard_map/all_gather | solution.py:122
  11.1 297.4 %all-gather.12.cloned.1.call-start = ((), (), s32[]{:S(2)}) async-start(), calls=%async_computation.14 | async-start | bytes 6635520 | tf_op jit(solution)/shard_map/all_gather | solution.py:122
  21.7 286.8 %all-gather.10.cloned.1.call-start = ((), (), s32[]{:S(2)}) async-start(), calls=%async_computation.13 | async-start | bytes 6635520 | tf_op jit(solution)/shard_map/all_gather | solution.py:122
  24.2 377.5 %all-gather.14.cloned.1.call-start = ((), (), s32[]{:S(2)}) async-start(), calls=%async_computation.15 | async-start | bytes 6635520 | tf_op jit(solution)/shard_map/all_gather | solution.py:122
  26.9 39.1 %copy-start.53 = (s32[2,1,240]{2,1,0:T(1,128)S(1)}, s32[2,1,240]{2,1,0:T(1,128)}, u32[]{:S(2)}) copy-start(s32[2,1,240]{2,1,0:T(1,128)} %param.15) | copy-start | bytes 5764
  26.9 54.4 %copy-start.34 = (f32[2304]{0:T(1024)S(1)}, f32[2304]{0:T(1024)}, u32[]{:S(2)}) copy-start(f32[2304]{0:T(1024)} %param.23) | copy-start | bytes 27652
  27.5 53.3 %copy-start.47 = (f32[2,240]{1,0:T(2,128)}, f32[2,240]{1,0:T(2,128)S(1)}, u32[]{:S(2)}) copy-start(f32[2,240]{1,0:T(2,128)S(1)} %fusion.12) | copy-start | bytes 5764
  66.0 103.8 %collective-permute-start = (bf16[2304,256]{1,0:T(8,128)(2,1)}, bf16[2304,256]{1,0:T(8,128)(2,1)S(1)}, u32[]{:S(2)}, u32[]{:S(2)}) collective-permute-start(bf16[2304,256]{1,0:T(8,128)(2,1)} %slice.87), channel_id=1, source_target_pairs={{0,4},{4,0},{8,12},{12,8},{16,20},{20,16},{24,28},{28,24},{1,5},{5... | collective-permute-start | bytes 3538952 | tf_op jit(solution)/shard_map/ppermute | solution.py:1019
  83.3 86.6 %copy-start.28 = (bf16[2304,512]{1,0:T(8,128)(2,1)S(1)}, bf16[2304,512]{1,0:T(8,128)(2,1)}, u32[]{:S(2)}) copy-start(bf16[2304,512]{1,0:T(8,128)(2,1)} %all-gather.6.cloned.1.call-done) | copy-start | bytes 7077892
  165.5 48.0 %all-to-all-start = ((bf16[8,32,2304]{2,1,0:T(8,128)(2,1)}), bf16[8,32,2304]{2,1,0:T(8,128)(2,1)}, u32[]{:S(2)}, u32[]{:S(2)}) async-start(bf16[8,32,2304]{2,1,0:T(8,128)(2,1)} %bitcast.98), calls=%async_computation | async-start | bytes 2359296 | tf_op jit(solution)/shard_map/all_to_all | solution.py:132
  169.8 571.1 %reduce-scatter.6.cloned.1.call-start = ((), (), s32[]{:S(2)}) async-start(), calls=%async_computation.16 | async-start | bytes 6635520 | tf_op jit(solution)/shard_map/reduce_scatter | solution.py:126
  170.9 20.2 %copy-start.4 = (bf16[2304,768]{1,0:T(8,128)(2,1)}, bf16[2304,768]{1,0:T(8,128)(2,1)S(1)}, u32[]{:S(2)}) copy-start(bf16[2304,768]{1,0:T(8,128)(2,1)S(1)} %slice_dynamic-update-slice_fusion.1.w_ref.refs_1_) | copy-start | bytes 10616836
  173.7 17.4 %copy-start.7 = (s32[2,1920,1]{2,1,0:T(8,128)S(1)}, s32[2,1920,1]{2,1,0:T(8,128)}, u32[]{:S(2)}) copy-start(s32[2,1920,1]{2,1,0:T(8,128)} %get-tuple-element.44.low_ref) | copy-start | bytes 46084
  213.5 89.3 %copy-start.19 = (bf16[2,1,240,2304]{3,2,1,0:T(8,128)(2,1)S(1)}, bf16[2,1,240,2304]{3,2,1,0:T(8,128)(2,1)}, u32[]{:S(2)}) copy-start(bf16[2,1,240,2304]{3,2,1,0:T(8,128)(2,1)} %param.14) | copy-start | bytes 6635524
  213.5 89.3 %copy-start.32 = (f32[2304]{0:T(1024)S(1)}, f32[2304]{0:T(1024)}, u32[]{:S(2)}) copy-start(f32[2304]{0:T(1024)} %param.24) | copy-start | bytes 27652
  299.1 4.4 copy-start.17
  304.6 97.0 %copy-start.51 = (f32[2,240]{1,0:T(2,128)}, f32[2,240]{1,0:T(2,128)S(1)}, u32[]{:S(2)}) copy-start(f32[2,240]{1,0:T(2,128)S(1)} %get-tuple-element.160) | copy-start | bytes 5764
  304.6 97.0 %copy-start.41 = (f32[2,240]{1,0:T(2,128)}, f32[2,240]{1,0:T(2,128)S(1)}, u32[]{:S(2)}) copy-start(f32[2,240]{1,0:T(2,128)S(1)} %fusion.18) | copy-start | bytes 5764
  401.7 95.4 %copy-start.23 = (bf16[2,1,240,2304]{3,2,1,0:T(8,128)(2,1)S(1)}, bf16[2,1,240,2304]{3,2,1,0:T(8,128)(2,1)}, u32[]{:S(2)}) copy-start(bf16[2,1,240,2304]{3,2,1,0:T(8,128)(2,1)} %param.27) | copy-start | bytes 6635524
  401.7 95.4 %copy-start.38 = (f32[2304]{0:T(1024)S(1)}, f32[2304]{0:T(1024)}, u32[]{:S(2)}) copy-start(f32[2304]{0:T(1024)} %param.26) | copy-start | bytes 27652
  494.3 3.6 copy-start.22
  604.2 254.4 %reduce-scatter.8.cloned.1.call-start = ((), (), s32[]{:S(2)}) async-start(), calls=%async_computation.17 | async-start | bytes 6635520 | tf_op jit(solution)/shard_map/reduce_scatter | solution.py:126
  724.2 6.5 slice-start
  724.2 331.1 %reduce-scatter.12.cloned.1.call-start = ((), (), s32[]{:S(2)}) async-start(), calls=%async_computation.19 | async-start | bytes 1474560 | tf_op jit(solution)/shard_map/reduce_scatter | solution.py:126
  724.9 5.8 copy-start.52
  724.9 5.8 slice-start.1
  724.9 5.8 copy-start.33
  724.9 5.8 copy-start.46
  724.9 13.7 %slice-start.2 = ((s8[4423680]{0:T(1024)(128)(4,1)}), s8[4194304]{0:T(1024)(128)(4,1)S(1)}, s32[]{:S(2)}) async-start(s8[4423680]{0:T(1024)(128)(4,1)} %bitcast.85), calls=%async_computation.23 | async-start | bytes 8388608
  730.7 5.8 copy-start.50
  730.8 7.8 slice-start.3
  740.9 86.3 %copy-start.3 = (bf16[2,1920,256]{2,1,0:T(8,128)(2,1)S(1)}, bf16[2,1920,256]{2,1,0:T(8,128)(2,1)}, u32[]{:S(2)}) copy-start(bf16[2,1920,256]{2,1,0:T(8,128)(2,1)} %copy-done.2) | copy-start | bytes 5898244
  857.8 212.6 %reduce-scatter.14.cloned.1.call-start = ((), (), s32[]{:S(2)}) async-start(), calls=%async_computation.20 | async-start | bytes 6635520 | tf_op jit(solution)/shard_map/reduce_scatter | solution.py:126
  910.1 8.4 copy-start.26
  910.1 8.4 copy-start.27
  911.9 10.3 collective-permute-start.1
  918.4 33.0 %all-to-all-start.5 = ((bf16[1,2,144,2304]{2,1,0,3:T(2,128)(2,1)}), bf16[1,2,144,2304]{2,1,0,3:T(2,128)(2,1)S(1)}, u32[]{:S(2)}, u32[]{:S(2)}) async-start(bf16[1,2,144,2304]{2,1,0,3:T(2,128)(2,1)} %copy.118), calls=%async_computation.10 | async-start | bytes 4718592 | tf_op jit(solution)/shard_map/all_to_all | solution.py:132
  922.1 214.5 %reduce-scatter.10.cloned.1.call-start = ((), (), s32[]{:S(2)}) async-start(), calls=%async_computation.18 | async-start | bytes 2949120 | tf_op jit(solution)/shard_map/reduce_scatter | solution.py:126
  952.9 107.3 %all-to-all-start.3 = ((bf16[576,8,144]{0,2,1:T(8,128)(2,1)}), bf16[576,8,144]{0,2,1:T(8,128)(2,1)}, u32[]{:S(2)}, u32[]{:S(2)}) async-start(bf16[576,8,144]{0,2,1:T(8,128)(2,1)} %bitcast.89), calls=%async_computation.7 | async-start | bytes 2949120 | tf_op jit(solution)/shard_map/all_to_all | solution.py:132
  957.4 94.3 %copy-start.20 = (bf16[2,1,240,2304]{3,2,1,0:T(8,128)(2,1)S(1)}, bf16[2,1,240,2304]{3,2,1,0:T(8,128)(2,1)}, u32[]{:S(2)}) copy-start(bf16[2,1,240,2304]{3,2,1,0:T(8,128)(2,1)} %param.14) | copy-start | bytes 6635524
  957.4 94.3 %copy-start.35 = (f32[2304]{0:T(1024)S(1)}, f32[2304]{0:T(1024)}, u32[]{:S(2)}) copy-start(f32[2304]{0:T(1024)} %param.23) | copy-start | bytes 27652
  957.4 94.3 %copy-start.44 = (f32[2,240]{1,0:T(2,128)S(1)}, f32[2,240]{1,0:T(2,128)}, u32[]{:S(2)}) copy-start(f32[2,240]{1,0:T(2,128)} %copy-done.43) | copy-start | bytes 5764
  1060.1 12.9 %all-to-all-start.2 = ((bf16[8,2,9216]{2,1,0:T(2,128)(2,1)}), bf16[8,2,9216]{2,1,0:T(2,128)(2,1)S(1)}, u32[]{:S(2)}, u32[]{:S(2)}) async-start(bf16[8,2,9216]{2,1,0:T(2,128)(2,1)} %reshape.218), calls=%async_computation.6 | async-start | bytes 589824 | tf_op jit(solution)/shard_map/all_to_all | solution.py:132
  1070.4 7.2 copy-start.39
  1070.4 7.2 copy-start.40
  1073.0 67.2 %all-to-all-start.4 = ((bf16[576,8,144]{0,2,1:T(8,128)(2,1)}), bf16[576,8,144]{0,2,1:T(8,128)(2,1)}, u32[]{:S(2)}, u32[]{:S(2)}) async-start(bf16[576,8,144]{0,2,1:T(8,128)(2,1)} %bitcast.34), calls=%async_computation.9 | async-start | bytes 2949120 | tf_op jit(solution)/shard_map/all_to_all | solution.py:132
  1140.2 6.7 copy-start.1
  (28 other events, 53.4 us)
Sparse Core Ops, SparseCore 0:
  10.4 53.1 all-gather.5
  65.8 29.2 all-gather.7
  96.6 98.2 all-gather.11
  196.9 97.4 all-gather.9
  295.9 97.5 all-gather.13
  604.3 92.2 reduce-scatter.5
  724.3 92.0 reduce-scatter.7
  857.9 25.4 reduce-scatter.11
  885.8 93.5 reduce-scatter.13
  982.2 48.5 reduce-scatter.9

commit v4 on v3

--- a/solution.py
+++ b/solution.py
@@ -145,11 +145,69 @@
     return me, other_core, along_x, along_y
 
 
-def greet(neighbours):
+def greet(neighbours, spread=None):
     barrier = pltpu.get_barrier_semaphore()
     for neighbour in neighbours:
         pl.semaphore_signal(barrier, inc=1, device_id={"seq": neighbour}, device_id_type=MESH)
-    pl.semaphore_wait(barrier, len(neighbours))
+    count = len(neighbours)
+    if spread is not None:
+        count = count + spread.greet(barrier)
+    pl.semaphore_wait(barrier, count)
+
+
+class Spread:
+    def __init__(self, parts_ref, placed_ref, send, recv):
+        self.parts, self.placed, self.send, self.recv = parts_ref, placed_ref, send, recv
+        self.me, self.layer = lax.axis_index("seq"), lax.axis_index("fsdp")
+        layers = lax.axis_size("fsdp")
+        shared = lax.axis_size("seq") // layers
+        self.owner = self.me // shared
+        self.slot = (self.me - self.owner * shared) * layers + self.layer
+        self.targets = [(place, self.owner) for place in range(shared * layers)]
+        self.sources = [
+            (self.layer * shared + part, from_layer)
+            for part in range(shared)
+            for from_layer in range(layers)
+        ]
+
+    def away(self, device):
+        return (device[0] != self.me) | (device[1] != self.layer)
+
+    def greet(self, barrier):
+        for place, layer in self.targets + self.sources:
+
+            @pl.when(self.away((place, layer)))
+            def _(place=place, layer=layer):
+                device = {"seq": place, "fsdp": layer}
+                pl.semaphore_signal(barrier, inc=1, device_id=device, device_id_type=MESH)
+
+        return 2 * len(self.targets) - 2 * (self.owner == self.layer).astype(jnp.int32)
+
+    def copy(self, index, slot, device):
+        return pltpu.make_async_remote_copy(
+            src_ref=self.parts.at[index],
+            dst_ref=self.placed.at[slot],
+            send_sem=self.send.at[index],
+            recv_sem=self.recv.at[slot],
+            device_id={"seq": device[0], "fsdp": device[1]},
+            device_id_type=MESH,
+        )
+
+    def own(self):
+        source, target = self.parts.at[self.me], self.placed.at[self.slot]
+        return pltpu.make_async_copy(source, target, self.send.at[len(self.targets)])
+
+    def begin(self):
+        for index, device in enumerate(self.targets):
+            pl.when(self.away(device))(self.copy(index, self.slot, device).start)
+        pl.when(self.owner == self.layer)(self.own().start)
+
+    def end(self):
+        for index, device in enumerate(self.targets):
+            pl.when(self.away(device))(self.copy(index, self.slot, device).wait_send)
+        for index, device in enumerate(self.sources):
+            pl.when(self.away(device))(self.copy(0, index, device).wait_recv)
+        pl.when(self.owner == self.layer)(self.own().wait)
 
 
 BRAID = 384
@@ -159,9 +217,20 @@
     return sum(array.shape[-1] for array in arrays)
 
 
+def braided(arrays):
+    return len(arrays) == 2 and arrays[0].shape[-1] == arrays[1].shape[-1]
+
+
 def copies_into(sources, target, sem):
-    if len(sources) == 1:
-        return [pltpu.make_async_copy(sources[0], target, sem.at[0])]
+    if not braided(sources):
+        copies, at = [], 0
+        for i, source in enumerate(sources):
+            width = source.shape[-1]
+            copies.append(
+                pltpu.make_async_copy(source, target.at[:, pl.ds(at, width)], sem.at[i])
+            )
+            at += width
+        return copies
     groups = sources[0].shape[-1] // BRAID
     copies = []
     for group in range(groups):
@@ -178,7 +247,7 @@
 
 
 def copy_count(arrays):
-    return 1 if len(arrays) == 1 else braid_width(arrays) // BRAID
+    return braid_width(arrays) // BRAID if braided(arrays) else len(arrays)
 
 
 def unit_rows(place, rows):
@@ -187,8 +256,19 @@
 
 class Job:
     def __init__(
-        self, compute, weights=(), extras=(), outs=(), sums=(), side=(), tables=(), spare=None, flops=0
+        self,
+        compute,
+        weights=(),
+        extras=(),
+        outs=(),
+        sums=(),
+        side=(),
+        tables=(),
+        spare=None,
+        spread=None,
+        flops=0,
     ):
+        self.spread = spread
         self.compute, self.flops, self.spare = compute, flops, spare
         self.tables = list(tables)
         self.weights, self.extras, self.outs = list(weights), list(extras), list(outs)
@@ -268,7 +348,28 @@
     if job.spare:
         job.spare[0](table_refs, made_refs)
     stores = []
-    done = {"side": 0}
+
+    order = [
+        (me, 0),
+        (me, 1),
+        (along_x, 0),
+        (along_y, 1),
+        (along_x, 1),
+        (along_y, 0),
+        (across, 0),
+        (across, 1),
+    ]
+
+    def extra_loads(step):
+        place, batch = order[step]
+        span = unit_rows(place, rows)
+        return [
+            pltpu.make_async_copy(ref.at[batch, span], buf.at[step % 2], load_sem.at[2 + i, step % 2])
+            for i, (ref, buf) in enumerate(zip(extra_refs, extra_bufs))
+        ]
+
+    for load in extra_loads(0):
+        load.start()
 
     def own_half(which):
         return x_buf.at[pl.ds(pl.multiple_of(which * rows, 16), rows)]
@@ -279,20 +380,20 @@
         span = unit_rows(place, rows)
         if own:
             loads = [
-                pltpu.make_async_copy(local_ref.at[batch], own_half(core), load_sem.at[0]),
+                pltpu.make_async_copy(local_ref.at[batch], own_half(core), load_sem.at[0, 0]),
                 pltpu.make_async_copy(
-                    piece(batch, other_core), own_half(1 - core), load_sem.at[1]
+                    piece(batch, other_core), own_half(1 - core), load_sem.at[1, 0]
                 ),
             ]
         else:
-            loads = [pltpu.make_async_copy(whole_ref.at[batch, span], x_buf, load_sem.at[0])]
-        loads += [
-            pltpu.make_async_copy(ref.at[batch, span], buf, load_sem.at[2 + i])
-            for i, (ref, buf) in enumerate(zip(extra_refs, extra_bufs))
-        ]
+            loads = [pltpu.make_async_copy(whole_ref.at[batch, span], x_buf, load_sem.at[0, 0])]
+        step = len(stores)
         for load in loads:
             load.start()
-        step = len(stores)
+        loads += extra_loads(step)
+        if step < 7:
+            for load in extra_loads(step + 1):
+                load.start()
         if step == 0:
             for fetch in fetches:
                 fetch.wait()
@@ -302,9 +403,9 @@
         for load in loads:
             load.wait()
         slot = step % 2
-        job.compute(
-            x_buf, weight_bufs, extra_bufs, [buf.at[slot] for buf in out_bufs], sum_bufs, step == 0
-        )
+        extras = [buf.at[slot] for buf in extra_bufs]
+        outs = [buf.at[slot] for buf in out_bufs]
+        job.compute(x_buf, weight_bufs, extras, outs, sum_bufs, step == 0)
         stores.append(
             [
                 pltpu.make_async_copy(buf.at[slot], ref.at[batch, span], store_sem.at[slot, i])
@@ -314,41 +415,35 @@
         for store in stores[-1]:
             store.start()
 
-    def side(count):
-        if not job.side:
-            return
-        for _ in range(count):
-            chunk = done["side"]
-            done["side"] += 1
-            run_side(chunk, rows, side_refs, side_bufs, sum_bufs[0], side_sem)
+    side = Side(rows, side_refs, side_bufs, sum_bufs, side_sem)
 
     for batch in range(2):
         moves[6 + batch].wait_recv()
         unit(me, batch, own=True)
-        side(1)
+        side.run(1)
     moves[0].wait_recv()
     moves[4].start()
     moves[8].start()
     moves[2].wait_recv()
     moves[5].start()
     moves[10].start()
-    side(2)
+    side.run(2)
     moves[8].wait_recv()
     unit(along_x, 0)
     moves[10].wait_recv()
     unit(along_y, 1)
-    side(1)
+    side.run(1)
     moves[1].wait_recv()
     moves[9].start()
     moves[3].wait_recv()
     moves[11].start()
-    side(3)
+    side.run(3)
     moves[9].wait_recv()
     unit(along_x, 1)
     moves[11].wait_recv()
     unit(along_y, 0)
-    if job.side:
-        finish_sums(sum_bufs, final_bufs, final_refs, final_sem)
+    early = 1 if job.side else 0
+    finish_sums(sum_bufs[:early], final_bufs[:early], final_refs[:early], final_sem)
     moves[4].wait_recv()
     moves[12].start()
     moves[5].wait_recv()
@@ -357,8 +452,7 @@
     unit(across, 0)
     moves[13].wait_recv()
     unit(across, 1)
-    if not job.side:
-        finish_sums(sum_bufs, final_bufs, final_refs, final_sem)
+    finish_sums(sum_bufs[early:], final_bufs[early:], final_refs[early:], final_sem)
     for move in moves:
         move.wait_send()
     for own in owns:
@@ -368,25 +462,40 @@
             store.wait()
 
 
-def run_side(chunk, rows, refs, bufs, total, sem):
-    span = pl.ds((chunk % 4) * 2 * rows, 2 * rows)
-    loads = [
-        pltpu.make_async_copy(ref.at[chunk // 4, span], buf, sem.at[i])
-        for i, (ref, buf) in enumerate(zip(refs, bufs))
-    ]
-    for load in loads:
-        load.start()
-    for load in loads:
-        load.wait()
-    add_outer(bufs[0], bufs[1], total, chunk == 0)
+class Side:
+    def __init__(self, rows, refs, bufs, sums, sem):
+        self.rows, self.refs, self.bufs, self.sums, self.sem = rows, refs, bufs, sums, sem
+        self.block = 0
+        self.start()
+
+    def copies(self):
+        span = pl.ds((self.block % 4) * 2 * self.rows, 2 * self.rows)
+        return [
+            pltpu.make_async_copy(ref.at[self.block // 4, span], buf, self.sem.at[i])
+            for i, (ref, buf) in enumerate(zip(self.refs, self.bufs))
+        ]
+
+    def start(self):
+        if self.refs and self.block < 8:
+            for copy in self.copies():
+                copy.start()
+
+    def run(self, count):
+        for _ in range(count if self.refs else 0):
+            for copy in self.copies():
+                copy.wait()
+            add_outer(self.bufs[0], self.bufs[1], self.sums[0], self.block == 0)
+            self.block += 1
+            self.start()
 
 
 def finish_sums(sum_bufs, final_bufs, final_refs, sem):
     for i, (total, buf, ref) in enumerate(zip(sum_bufs, final_bufs, final_refs)):
         copies = []
-        for block in range(total.shape[0] // BRAID):
+        size = buf.shape[1]
+        for block in range(total.shape[0] // size):
             slot = block % 2
-            span = pl.ds(block * BRAID, BRAID)
+            span = pl.ds(block * size, size)
             if block >= 2:
                 copies[block - 2].wait()
             buf[slot] = total[span, :].astype(buf.dtype)
@@ -406,14 +515,14 @@
     if job.weights:
         depth = job.weights[0].shape[0]
         scratch += [pltpu.VMEM((depth, braid_width(job.weights)), job.weights[0].dtype)]
-    for arrays in (job.extras, job.side):
-        scratch += [pltpu.VMEM((2 * rows, array.shape[2]), array.dtype) for array in arrays]
+    scratch += [pltpu.VMEM((2, 2 * rows, array.shape[2]), array.dtype) for array in job.extras]
+    scratch += [pltpu.VMEM((2 * rows, array.shape[2]), array.dtype) for array in job.side]
     scratch += [pltpu.VMEM((2, 2 * rows, wide), kind) for wide, kind in job.outs]
     scratch += [pltpu.VMEM(shape, jnp.float32) for shape in job.sums]
-    scratch += [pltpu.VMEM((2, BRAID, shape[1]), jnp.bfloat16) for shape in job.sums]
+    scratch += [pltpu.VMEM((2, HEAD_SIZE // 2, shape[1]), jnp.bfloat16) for shape in job.sums]
     scratch += [
         semaphores((copy_count(job.weights) if job.weights else 1,)),
-        semaphores((2 + len(job.extras),)),
+        semaphores((2 + len(job.extras), 2)),
         semaphores((max(1, len(job.side)),)),
         semaphores((2, max(1, len(job.outs)))),
         semaphores((max(1, len(job.sums)), 2)),
@@ -425,6 +534,7 @@
     inputs = [local, *job.weights, *job.extras, *job.side]
     in_specs = [any_space] * len(inputs)
     in_specs += [pl.BlockSpec(memory_space=pltpu.VMEM)] * len(job.tables)
+    inputs += job.tables
     out_specs = [any_space] * len(out_shape)
     if job.spare:
         out_shape += job.spare[1]
@@ -442,7 +552,7 @@
             flops=job.flops, bytes_accessed=SPAN_BYTES, transcendentals=0
         ),
         name=name,
-    )(*inputs, *job.tables)
+    )(*inputs)
 
 
 def scatter_kernel(job, rows, *refs):
@@ -453,11 +563,14 @@
         take(len(job.weights)),
         take(len(job.side)),
     )
+    spread_refs = take(1 if job.spread is not None else 0)
     (out_ref,), final_refs = take(1), take(len(job.sums))
+    spread_refs += take(len(spread_refs))
     part_buf, weight_buf, sums, held, from_core, from_link, out_buf = take(7)
     side_bufs, sum_bufs, final_bufs = take(len(job.side)), take(len(job.sums)), take(len(job.sums))
     weight_sem, load_sem, side_sem, final_sem, out_sem = take(5)
     core_send, core_recv, link_send, link_recv, credit = take(5)
+    spread = Spread(*spread_refs, *take(2)) if spread_refs else None
 
     me, other_core, along_x, along_y = plane_places()
     across = along_x + along_y - me
@@ -509,12 +622,14 @@
         )
         for step in range(6)
     ]
-    greet((other_core, along_x, along_y))
+    greet((other_core, along_x, along_y), spread)
+    if spread is not None:
+        spread.begin()
 
     def finish(step):
         gives[step].wait_recv()
-        total = sums[step % 2, kept].astype(jnp.float32)
-        total = total + from_core[step % 4].astype(jnp.float32)
+        kind = jnp.bfloat16 if step < 4 else jnp.float32
+        total = sums[step % 2, kept].astype(kind) + from_core[step % 4].astype(kind)
         if step < 4:
             pl.semaphore_signal(credit, inc=1, device_id={"seq": other_core}, device_id_type=MESH)
         for arrived in added.get(step, ()):
@@ -529,16 +644,7 @@
             out.start()
             out.wait()
 
-    done = {"side": 0}
-
-    def side(count):
-        if not job.side:
-            return
-        for _ in range(count):
-            chunk = done["side"]
-            done["side"] += 1
-            run_side(chunk, rows, side_refs, side_bufs, sum_bufs[0], side_sem)
-
+    side = Side(rows, side_refs, side_bufs, sum_bufs, side_sem)
     for step in range(8):
         for copy in loads[step]:
             copy.wait()
@@ -556,12 +662,14 @@
         gives[step].start()
         if step >= 1:
             finish(step - 1)
-        side((0, 0, 1, 1, 1, 1, 2, 2)[step])
+        side.run((0, 0, 1, 1, 1, 1, 2, 2)[step])
     if job.side:
         finish_sums(sum_bufs, final_bufs, final_refs, final_sem)
     finish(7)
     for move in gives[6:] + sends:
         move.wait_send()
+    if spread is not None:
+        spread.end()
 
 
 def plane_scatter(parts, width, ident, name, job):
@@ -582,7 +690,7 @@
     ]
     scratch += [pltpu.VMEM((2 * rows, array.shape[2]), array.dtype) for array in job.side]
     scratch += [pltpu.VMEM(shape, jnp.float32) for shape in job.sums]
-    scratch += [pltpu.VMEM((2, BRAID, shape[1]), jnp.bfloat16) for shape in job.sums]
+    scratch += [pltpu.VMEM((2, HEAD_SIZE // 2, shape[1]), jnp.bfloat16) for shape in job.sums]
     scratch += [
         semaphores((copy_count(weights),)),
         semaphores((2, copy_count(parts))),
@@ -598,6 +706,10 @@
     out_shape = [jax.ShapeDtypeStruct((batches, rows, width), jnp.float32)]
     out_shape += [jax.ShapeDtypeStruct(shape, jnp.bfloat16) for shape in job.sums]
     inputs = [*parts, *weights, *job.side]
+    if job.spread is not None:
+        inputs.append(job.spread)
+        out_shape.append(jax.ShapeDtypeStruct(job.spread.shape, job.spread.dtype))
+        scratch += [semaphores((job.spread.shape[0] + 1,)), semaphores((job.spread.shape[0],))]
     return pl.pallas_call(
         functools.partial(scatter_kernel, job, rows),
         in_specs=[any_space] * len(inputs),
@@ -716,7 +828,8 @@
         )
         total[span, :] = outer if first else total[span, :] + outer
 
-    tiles(left.shape[1], BRAID, body)
+    wide = left.shape[1]
+    tiles(wide, next(tile for tile in (2 * BRAID, BRAID, HEAD_SIZE) if wide % tile == 0), body)
 
 
 def hidden_compute(x_buf, weights, extras, outs, sums, first):
@@ -754,6 +867,7 @@
 
 def head_back_compute(x_buf, weights, extras, outs, sums, first):
     outs[0][...] = dot_back(x_buf[...], weights[0][...]).astype(outs[0].dtype)
+    add_outer(extras[0], x_buf, sums[1], first)
 
 
 def rows_compute(part, weight, out):
@@ -871,9 +985,15 @@
 
     @pl.when(index == steps - 1)
     def _():
+        half = HEAD_SIZE // 2
+        odd = lax.axis_index("seq") % 2 == 1
         dk = turn_back(dk_ref[...], cos_ref[...], sin_ref[...])
-        grad_ref[:, HEAD_SIZE : 2 * HEAD_SIZE] = dk.astype(jnp.bfloat16)
-        grad_ref[:, 2 * HEAD_SIZE :] = dv_ref[...].astype(jnp.bfloat16)
+        for part, grad in enumerate((dk, dv_ref[...])):
+            low, high = grad[:, :half], grad[:, half:]
+            own = HEAD_SIZE + half * part
+            grad_ref[:, own : own + half] = jnp.where(odd, high, low).astype(jnp.bfloat16)
+            own += HEAD_SIZE
+            grad_ref[:, own : own + half] = jnp.where(odd, low, high).astype(jnp.bfloat16)
 
 
 def block_shape(length):
@@ -892,17 +1012,24 @@
     return whole, half, rows, line
 
 
-def project_kernel(x_ref, w_ref, cos_ref, sin_ref, q_ref, k_ref, v_ref):
+def project_kernel(x_ref, w_ref, far_ref, cos_ref, sin_ref, q_ref, k_ref, v_ref):
     product = final_dot(x_ref[...], w_ref[...])
+    far = final_dot(x_ref[...], far_ref[...])
     cosine, sine = cos_ref[...], sin_ref[...]
-    query, key = product[:, :HEAD_SIZE], product[:, HEAD_SIZE : 2 * HEAD_SIZE]
+    half = HEAD_SIZE // 2
+    query = product[:, :HEAD_SIZE]
+    own_k, own_v = product[:, HEAD_SIZE : HEAD_SIZE + half], product[:, HEAD_SIZE + half :]
+    far_k, far_v = far[:, :half], far[:, half:]
+    odd = lax.axis_index("seq") % 2 == 1
+    key = jnp.concatenate([jnp.where(odd, far_k, own_k), jnp.where(odd, own_k, far_k)], axis=1)
     query = rotate(query, cosine, sine, 1.0) * (1.0 / math.sqrt(HEAD_SIZE))
     q_ref[...] = query.astype(jnp.bfloat16)
     k_ref[...] = rotate(key, cosine, sine, 1.0).astype(jnp.bfloat16)
-    v_ref[...] = product[:, 2 * HEAD_SIZE :].astype(jnp.bfloat16)
-
-
-def project(whole, weight, cosine, sine):
+    v_ref[:, :half] = jnp.where(odd, far_v, own_v).astype(jnp.bfloat16)
+    v_ref[:, half:] = jnp.where(odd, own_v, far_v).astype(jnp.bfloat16)
+
+
+def project(whole, weight, far, cosine, sine):
     batches, length, width = whole.shape
     block = block_shape(length)[0]
     _, _, rows, _ = attend_specs(length, block)
@@ -913,6 +1040,7 @@
         in_specs=[
             pl.BlockSpec((None, block, width), lambda m, i: (m, i, 0)),
             pl.BlockSpec(weight.shape, lambda m, i: (0, 0)),
+            pl.BlockSpec(far.shape, lambda m, i: (0, 0)),
             half,
             half,
         ],
@@ -925,7 +1053,7 @@
             transcendentals=0,
         ),
         name="project",
-    )(whole, weight, cosine, sine)
+    )(whole, weight, far, cosine, sine)
 
 
 def token_tables(tables, made):
@@ -1014,21 +1142,15 @@
             [columns(w_query, HEAD_SIZE), columns(key_weight, half), columns(value_weight, half)],
             axis=1,
         )
-        self.joined = gather_rows(joined)
-        own = self.joined[:, HEAD_SIZE:]
-        other = lax.ppermute(own, "seq", [(i, i ^ 1) for i in range(count)])
-        odd = place % 2 == 1
-        low, high = jnp.where(odd, other, own), jnp.where(odd, own, other)
-        self.weights = jnp.concatenate(
-            [self.joined[:, :HEAD_SIZE], low[:, :half], high[:, :half], low[:, half:], high[:, half:]],
-            axis=1,
-        )
         depth = HEAD_SIZE // count
         here = QUERY_HEADS // layers
         part = w_out.reshape(here, count, depth, w_out.shape[1])
         part = lax.dynamic_index_in_dim(part, place, axis=1, keepdims=False)
-        part = gather_rows(part.reshape(here * depth, -1))
-        self.out_rows = swap_parts(part, 0, 0)
+        rows = joined.shape[0]
+        both = jnp.concatenate([joined, part.reshape(-1, joined.shape[1])], axis=0)
+        self.both = lax.all_gather(both, "fsdp", axis=0)
+        self.split = rows
+        self.part_shape = (QUERY_HEADS * depth, w_out.shape[1])
 
     def forward(self, normed, segments):
         batches, rows, width = normed.shape
@@ -1055,7 +1177,13 @@
                 spare=(token_tables, [table, table, bound]),
             ),
         )
-        query, key, value = project(whole, self.weights, cosine, sine)
+        whole, both = lax.optimization_barrier((whole, self.both))
+        self.joined = both[:, : self.split].reshape(-1, both.shape[2])
+        self.out_rows = swap_parts(both[:, self.split :].reshape(self.part_shape), 0, 0)
+        self.far = lax.ppermute(
+            self.joined[:, HEAD_SIZE:], "seq", [(i, i ^ 1) for i in range(QUERY_HEADS)]
+        )
+        query, key, value = project(whole, self.joined, self.far, cosine, sine)
         attended, log_total = attend(query, key, value, low_bound)
         job = Job(
             rows_compute, weights=[self.out_rows], flops=2 * batches * length * HEAD_SIZE * width
@@ -1063,61 +1191,62 @@
         (mixed,) = plane_scatter([attended], width, 1, "scatter_mixed", job)
         return mixed, (whole, query, key, value, low_bound, log_total, cosine, sine, attended)
 
-    def backward(self, grad_mixed_b, saved, side, meanwhile):
-        whole, query, key, value, low_bound, log_total, cosine, sine, attended = saved
-        batches, length = key.shape[:2]
+    def open_back(self, grad_mixed_b, saved, side):
+        attended = saved[-1]
+        batches, length = attended.shape[:2]
         width = grad_mixed_b.shape[-1]
         job = Job(
             head_back_compute,
             weights=[self.out_rows],
+            extras=[attended],
             outs=[(HEAD_SIZE, jnp.bfloat16)],
             side=side,
-            sums=[(side[0].shape[2], side[1].shape[2])],
+            sums=[(side[0].shape[2], side[1].shape[2]), (HEAD_SIZE, width)],
             flops=2 * batches * length * (HEAD_SIZE * width + side[0].shape[2] * side[1].shape[2]),
         )
-        grad_whole, grad_att, side_sum = plane_gather(grad_mixed_b, 2, "gather_grad_mixed", job)
-        grad_att, meanwhile = lax.optimization_barrier((grad_att, scatter_rows(meanwhile)))
-        grads = attend_back(
-            query, key, value, grad_att, low_bound, log_total, cosine, sine
-        )
-        self.record = (whole, grads, attended, grad_whole)
+        _, grad_att, side_sum, self.out_sum = plane_gather(
+            grad_mixed_b, 2, "gather_grad_mixed", job
+        )
+        return grad_att, side_sum
+
+    def middle_back(self, grad_att, saved):
+        _, query, key, value, low_bound, log_total, cosine, sine, _ = saved
+        grads = attend_back(query, key, value, grad_att, low_bound, log_total, cosine, sine)
+        grads, self.out_own = lax.optimization_barrier((grads, scatter_rows(self.out_sum)))
+        return grads
+
+    def close_back(self, grads, saved, meanwhile):
+        count = lax.axis_size("seq")
+        joined = dot_rows(saved[0], grads).astype(jnp.bfloat16)
+        own, far = joined[:, HEAD_SIZE : 2 * HEAD_SIZE], joined[:, 2 * HEAD_SIZE :]
+        came = lax.ppermute(far, "seq", [(i, i ^ 1) for i in range(count)])
+        own = (own.astype(jnp.float32) + came.astype(jnp.float32)).astype(jnp.bfloat16)
+        joined = jnp.concatenate([joined[:, :HEAD_SIZE], own], axis=1)
+        grads, joined, meanwhile = lax.optimization_barrier((grads, joined, meanwhile))
+        self.joined_sum = joined
+
+        parts = self.out_own.reshape(self.out_own.shape[0], count, -1).transpose(1, 0, 2)
+        rows = grads.shape[0] * grads.shape[1]
+        width = self.joined.shape[0]
         job = Job(
-            back_compute, weights=[self.weights], flops=6 * batches * length * HEAD_SIZE * width
-        )
-        (grad_normed,) = plane_scatter([grads], width, 3, "scatter_grad_normed", job)
-        return grad_normed, side_sum, meanwhile
-
-    def weight_grads(self):
+            back_compute,
+            weights=[self.joined, self.far],
+            spread=parts,
+            flops=6 * rows * HEAD_SIZE * width,
+        )
+        grad_normed, self.placed = plane_scatter([grads], width, 3, "scatter_grad_normed", job)
+        return grad_normed, meanwhile
+
+    def weight_grads(self, gains):
         half = HEAD_SIZE // 2
-        count = lax.axis_size("seq")
-        layers = lax.axis_size("fsdp")
-        whole, grads, attended, grad_whole = self.record
-        joined = dot_rows(whole, grads).astype(jnp.bfloat16)
-        k_low, k_high, v_low, v_high = (
-            joined[:, HEAD_SIZE + half * i : HEAD_SIZE + half * (i + 1)] for i in range(4)
-        )
-        low = jnp.concatenate([k_low, v_low], axis=1)
-        high = jnp.concatenate([k_high, v_high], axis=1)
-        odd = lax.axis_index("seq") % 2 == 1
-        came = lax.ppermute(
-            jnp.where(odd, low, high), "seq", [(i, i ^ 1) for i in range(count)]
-        )
-        kept = jnp.where(odd, high, low)
-        kept = (kept.astype(jnp.float32) + came.astype(jnp.float32)).astype(jnp.bfloat16)
-        joined = scatter_rows(jnp.concatenate([joined[:, :HEAD_SIZE], kept], axis=1))
-
-        width = grad_whole.shape[-1]
-        out = dot_rows(attended, grad_whole).astype(jnp.bfloat16)
-        out = scatter_rows(swap_parts(out, 0, 0))
-        here = QUERY_HEADS // layers
-        out = swap_parts(out.reshape(1, here, HEAD_SIZE // count, width), 3, 0)
-        out = out.transpose(1, 0, 2, 3).reshape(here * HEAD_SIZE, -1)
-        joined = joined.astype(jnp.float32)
+        joined = scatter_rows(self.joined_sum).astype(jnp.float32)
+        gains = small_sum(jnp.pad(gains, ((0, 4), (0, 0))), True, 9, "sum_gains")
         return (
             joined[:, :HEAD_SIZE],
             joined[:, HEAD_SIZE : HEAD_SIZE + half],
             joined[:, HEAD_SIZE + half :],
-            out.astype(jnp.float32),
+            self.placed.astype(jnp.float32).reshape(-1, self.placed.shape[2]),
+            gains,
         )
 
 
@@ -1173,9 +1302,15 @@
         log_total = peak + jnp.log(total)
         return mixed, (normed, query, pair, allowed, log_total, cosine, sine, attended)
 
-    def backward(self, grad_mixed_b, saved, side, meanwhile):
+    def open_back(self, grad_mixed_b, saved, side):
+        return grad_mixed_b, dot_rows(*side)
+
+    def middle_back(self, grad_mixed_b, saved):
+        return grad_mixed_b
+
+    def close_back(self, grad_mixed_b, saved, meanwhile):
         grads = [self.backward_one(*pair) for pair in zip(grad_mixed_b, saved)]
-        return jnp.stack(grads), dot_rows(*side), scatter_rows(meanwhile)
+        return jnp.stack(grads), meanwhile
 
     def backward_one(self, grad_mixed_b, saved):
         normed, query, pair, allowed, log_total, cosine, sine, attended = saved
@@ -1210,7 +1345,7 @@
         self.records.append((normed, dq, dk, dv, attended, grad_mixed_b))
         return dot_back(dq, w_query) + dot_back(dk, key_weight) + dot_back(dv, value_weight)
 
-    def weight_grads(self):
+    def weight_grads(self, gains):
         normed, dq, dk, dv, attended, grad_mixed_b = (
             jnp.concatenate(parts, axis=0) for parts in zip(*self.records)
         )
@@ -1221,7 +1356,7 @@
             column_sum = dot_rows(rows, swap_parts(grads, 1, 0)).astype(jnp.bfloat16)
             owned = lax.psum_scatter(column_sum, "fsdp", scatter_dimension=0, tiled=True)
             sums.append(owned.astype(jnp.float32))
-        return tuple(sums)
+        return tuple(sums) + (lax.psum(gains, ("seq", "fsdp")),)
 
 
 class FeedForward:
@@ -1315,18 +1450,14 @@
         self.up_side = (whole, grad_up)
         return grad_ffn_in
 
-    def weight_grads(self, gate_own, up_own, down_own):
-        count = lax.axis_size("seq")
-
-        down = down_own
-        here = down.shape[0] // self.run
-        down = swap_parts(down.reshape(1, here, self.run, -1), 3, 0)
-        down = down.transpose(1, 0, 2, 3).reshape(here * count * self.run, -1)
-
-        def columns(own):
-            return swap_parts(own, 1, 1).astype(jnp.float32)
-
-        return columns(gate_own), columns(up_own), down.astype(jnp.float32)
+    def own_columns(self, own):
+        return swap_parts(own, 1, 1).astype(jnp.float32)
+
+    def own_rows(self, own):
+        here = own.shape[0] // self.run
+        moved = swap_parts(own, 1, 0)
+        moved = moved.reshape(-1, here, self.run, moved.shape[1]).transpose(1, 0, 2, 3)
+        return moved.astype(jnp.float32).reshape(-1, moved.shape[3])
 
 
 def on_device(
@@ -1370,25 +1501,24 @@
     grad_middle = grad_result + grad_middle
     _, pullback = jax.vjp(rms_gain, mixed, gain_attn_out)
     grad_mixed, grad_gain_two = pullback(grad_middle)
-    grad_mixed, down_own = lax.optimization_barrier(
+    grad_mixed, w_down_grad = lax.optimization_barrier(
         (grad_mixed.astype(jnp.bfloat16), scatter_rows(ffn.down_sum))
     )
-    grad_normed, up_sum, gate_own = attention.backward(
-        grad_mixed, attention_saved, ffn.up_side, ffn.gate_sum
+    grad_att, up_sum = attention.open_back(grad_mixed, attention_saved, ffn.up_side)
+    grad_att, w_gate_grad = lax.optimization_barrier((grad_att, scatter_rows(ffn.gate_sum)))
+    w_down_grad = ffn.own_rows(w_down_grad)
+    grads = attention.middle_back(grad_att, attention_saved)
+    grads, w_gate_grad, w_down_grad = lax.optimization_barrier((grads, w_gate_grad, w_down_grad))
+    grad_normed, w_gate_grad = attention.close_back(
+        grads, attention_saved, ffn.own_columns(w_gate_grad)
     )
     _, pullback = jax.vjp(rms_gain, stream, gain_attn_in)
     grad_stream, grad_gain_one = pullback(grad_normed)
     grad_stream = grad_middle + grad_stream
 
-    w_gate_grad, w_up_grad, w_down_grad = ffn.weight_grads(
-        gate_own, scatter_rows(up_sum), down_own
-    )
-    query_grad, key_grad, value_grad, out_grad = attention.weight_grads()
+    w_up_grad = ffn.own_columns(scatter_rows(up_sum))
     gains = jnp.stack([grad_gain_one, grad_gain_two, grad_gain_three, grad_gain_four])
-    if by_kernel:
-        gains = small_sum(jnp.pad(gains, ((0, 4), (0, 0))), True, 9, "sum_gains")
-    else:
-        gains = lax.psum(gains, ("seq", "fsdp"))
+    query_grad, key_grad, value_grad, out_grad, gains = attention.weight_grads(gains)
     return (
         result.astype(jnp.bfloat16)[:, None],
         grad_stream[:, None],

time: 1160 us -> 1060 us (0.914)
  waiting for transfers between devices: 58.8 us -> 17.7 us
  blocking collectives: 21.2 us -> 0 us
  Pallas kernels: 853 us -> 841 us
    all_gather x5 -> x3, waiting for transfers between devices: 36.2 us -> 6.98 us  [gather_rows(): return lax.all_gather(rows, 'fsdp', axis=0, tiled=True)]
    all_to_all x1 -> x0, blocking collectives: 21.2 us -> none  [swap_parts(): lax.all_to_all(value, 'seq', split_axis=split_axis, concat_axis=concat_ax...]
    all_to_all x5 -> x4, waiting for transfers between devices: 21.7 us -> 8.9 us  [swap_parts(): lax.all_to_all(value, 'seq', split_axis=split_axis, concat_axis=concat_ax...]
    dot_general x2 -> x1, matrix products: 29.1 us -> 19.1 us  [dot_rows(): lax.dot_general(left_side, right_side, (((0,), (0,)), ((), ())), preferre...]
    unnamed x125 -> x119, local copies, waits for them, and re-layouts: 36.6 us -> 40.7 us
  transfers between devices with their start and end apart: 17 -> 15, of which waited for: 2 -> 4; matrix products, arithmetic and copies ran while one was open for 13% -> 11% of each run, Pallas kernels for 57% -> 62%
where the time goes in v4:
time: 1060 us
  Pallas kernels  841 us (79%)
  local copies, waits for them, and re-layouts  92.5 us (9%)
  other arithmetic  51.9 us (5%)
  matrix products  19.1 us (2%)
  starting transfers between devices  18.7 us (2%)
  waiting for transfers between devices  17.7 us (2%)
  between operations  15.1 us (1%)
    pallas_call x4, Pallas kernels, plane_scatter(): pl.pallas_call(functools.partial(scatter_kernel, job, rows), in_specs=[an...  384 us
    pallas_call x4, Pallas kernels, plane_gather(): pl.pallas_call(functools.partial(gather_kernel, job, rows), in_specs=in_s...  364 us
    unnamed x119, local copies, waits for them, and re-layouts  40.7 us
    pallas_call x2, Pallas kernels, small_sum(): pl.pallas_call(functools.partial(small_sum_kernel, over_layers), in_specs...  31.3 us
    pallas_call x1, Pallas kernels, attend_back(): pl.pallas_call(functools.partial(attend_back_kernel, block, reach), grid=...  27.8 us
  transfers between devices with their start and end apart: 15, of which 4 were waited for; matrix products, arithmetic and copies ran while one was open for 11% of the time, Pallas kernels for 62%

profile of v4, /device:TPU:0, one launch (start us, length us, event | category | flops | bytes accessed | tf_op | source)
XLA Modules:
  0.0 1055.9 jit_solution(10460372771135638307)
XLA Ops:
  12.3 7.3 constant_dynamic-slice_fusion.1
  19.6 4.4 concatenate.18
  24.2 4.1 concatenate.17
  28.9 4.0 stack.42
  33.6 10.2 sum_counts.1.refs_1_
  46.8 81.6 %gather_normed.1 = (bf16[2,1920,2304]{2,1,0:T(8,128)(2,1)}, f32[2,1920,128]{2,1,0:T(8,128)}, f32[2,1920,128]{2,1,0:T(8,128)}, s32[2,1920,1]{2,1,0:T(8,128)}) custom-call(bf16[2,240,2304]{2,1,0:T(8,128)(2,1)} %fusion.4.refs_0_, f32[8,128]{1,0:T(8,128)} %sum_counts.1.refs_1_, f32[1,128]{1,0:T(1,128)} %multiply_power_fusion.refs_2_), custom_call_target="tpu_custom_call" | custom-call | bytes 270000000 | tf_op jit(solution)/shard_map/gather_normed/pallas_call | solution.py:542
  131.8 2.5 constant_dynamic-slice_fusion
  134.3 2.4 slice.55
  136.7 3.2 all_to_all.29
  139.9 4.3 all-to-all-start
  144.5 2.0 copy-done.3
  148.0 17.3 %project.1 = (bf16[2,1920,256]{2,1,0:T(8,128)(2,1)S(1)}, bf16[2,1920,256]{2,1,0:T(8,128)(2,1)S(1)}, bf16[2,1920,256]{2,1,0:T(8,128)(2,1)S(1)}) custom-call(bf16[2,1920,2304]{2,1,0:T(8,128)(2,1)} %get-tuple-element.51.x_ref, bf16[2304,512]{1,0:T(8,128)(2,1)S(1)} %bitcast.71, bf16[2304,256]{1,0:T(8,128)(2,1)S(1)} %collective-permute-done.far_ref.refs_2_, ...), custom_call_target="tpu_custom_call" | custom-call | flops 13589544960 | bytes 17694720 | tf_op jit(solution)/shard_map/project/pallas_call | solution.py:1037
  165.3 15.9 %attend.1 = (bf16[2,1920,256]{2,1,0:T(8,128)(2,1)S(1)}, f32[2,1920,1]{2,1,0:T(8,128)S(1)}) custom-call(bf16[2,1920,256]{2,1,0:T(8,128)(2,1)S(1)} %get-tuple-element.55.q_ref, bf16[2,1920,256]{2,1,0:T(8,128)(2,1)S(1)} %get-tuple-element.56.k_ref, bf16[2,1920,256]{2,1,0:T(8,128)(2,1)S(1)} %get-tuple-element.57.v_ref, s32[2,1920,1]{2,1,0:T(8,128)S(1)} %copy-done.5), custom_call_target="tpu_custom_call" | custom-call | flops 6039797760 | bytes 9830400 | tf_op jit(solution)/shard_map/attend/pallas_call | solution.py:1090
  187.7 85.1 %scatter_mixed.1 = f32[2,240,2304]{2,1,0:T(8,128)} custom-call(bf16[2,1920,256]{2,1,0:T(8,128)(2,1)} %copy-done.7, bf16[256,2304]{1,0:T(8,128)(2,1)} %bitcast.13.refs_1_), custom_call_target="tpu_custom_call" | custom-call | flops 4529848320 | bytes 270000000 | tf_op jit(solution)/shard_map/scatter_mixed/pallas_call | solution.py:713
  272.8 2.8 multiply_reduce_fusion.6
  277.5 2.0 copy-done.15
  281.4 2.8 all-gather.6.cloned.1.call-done.refs_1_.refs_2_
  284.1 94.7 %gather_ffn_in.1 = (bf16[2,1920,2304]{2,1,0:T(8,128)(2,1)}, bf16[2,1920,1152]{2,1,0:T(8,128)(2,1)}, bf16[2,1920,1152]{2,1,0:T(8,128)(2,1)}, bf16[2,1920,1152]{2,1,0:T(8,128)(2,1)}) custom-call(bf16[2,240,2304]{2,1,0:T(8,128)(2,1)} %multiply_convert_fusion.refs_0_, bf16[2304,1152]{1,0:T(8,128)(2,1)} %all-gather.6.cloned.1.call-done.refs_1_.refs_2_, ...), custom_call_target="tpu_custom_call" | custom-call | flops 40768634880 | bytes 270000000 | tf_op jit(solution)/shard_map/gather_ffn_in/pallas_call | solution.py:542
  378.9 4.2 all-gather.10.cloned.1.call-done.refs_1_
  383.1 91.3 %scatter_down.1 = f32[2,240,2304]{2,1,0:T(8,128)} custom-call(bf16[2,1920,1152]{2,1,0:T(8,128)(2,1)} %get-tuple-element.60.refs_0_.refs_4_, bf16[1152,2304]{1,0:T(8,128)(2,1)} %all-gather.10.cloned.1.call-done.refs_1_), custom_call_target="tpu_custom_call" | custom-call | flops 20384317440 | bytes 270000000 | tf_op jit(solution)/shard_map/scatter_down/pallas_call | solution.py:713
  474.5 2.8 multiply_reduce_fusion.4
  479.9 3.5 fusion.7
  483.5 98.7 %gather_grad_down.1 = (bf16[2,1920,2304]{2,1,0:T(8,128)(2,1)}, bf16[2,1920,1152]{2,1,0:T(8,128)(2,1)}, bf16[2,1920,1152]{2,1,0:T(8,128)(2,1)}, bf16[1152,2304]{1,0:T(8,128)(2,1)}) custom-call(bf16[2,240,2304]{2,1,0:T(8,128)(2,1)} %get-tuple-element.176.refs_0_, bf16[1152,2304]{1,0:T(8,128)(2,1)} %all-gather.10.cloned.1.call-done.refs_1_, ...), custom_call_target="tpu_custom_call" | custom-call | flops 40768634880 | bytes 270000000 | tf_op jit(solution)/shard_map/gather_grad_down/pallas_call | solution.py:542
  582.2 114.9 %scatter_grad_ffn_in.1 = (f32[2,240,2304]{2,1,0:T(8,128)}, bf16[2304,1152]{1,0:T(8,128)(2,1)}) custom-call(bf16[2,1920,1152]{2,1,0:T(8,128)(2,1)} %get-tuple-element.63.refs_0_.refs_5_, bf16[2,1920,1152]{2,1,0:T(8,128)(2,1)} %get-tuple-element.64.refs_1_.refs_4_, bf16[2304,1152]{1,0:T(8,128)(2,1)} %all-gather.6.cloned.1.call-done.refs_1_.refs_2_, ...), custom_call_target="tpu_custom_call" | custom-call | flops 61152952320 | bytes 270000000 | tf_op jit(solution)/shard_map/scatter_grad_ffn_in/pallas_call | solution.py:713
  697.9 4.8 multiply_reduce_fusion
  703.2 6.3 multiply_reduce_fusion.1
  709.5 2.1 copy-done.21
  711.6 2.3 fusion.8.refs_0_
  713.9 89.1 %gather_grad_mixed.1 = (bf16[2,1920,2304]{2,1,0:T(8,128)(2,1)}, bf16[2,1920,256]{2,1,0:T(8,128)(2,1)}, bf16[2304,1152]{1,0:T(8,128)(2,1)}, bf16[256,2304]{1,0:T(8,128)(2,1)}) custom-call(bf16[2,240,2304]{2,1,0:T(8,128)(2,1)} %fusion.8.refs_0_, bf16[256,2304]{1,0:T(8,128)(2,1)} %bitcast.13.refs_1_, bf16[2,1920,256]{2,1,0:T(8,128)(2,1)} %copy-done.7, ...), custom_call_target="tpu_custom_call" | custom-call | flops 24914165760 | bytes 270000000 | tf_op jit(solution)/shard_map/gather_grad_mixed/pallas_call | solution.py:542
  803.8 5.0 all_to_all.32
  808.7 2.9 copy.75
  811.6 4.5 all-to-all-start.1
  819.3 27.8 %attend_back.1.refs_0_ = bf16[2,1920,768]{2,1,0:T(8,128)(2,1)} custom-call(bf16[2,1920,256]{2,1,0:T(8,128)(2,1)S(1)} %copy-done.9, bf16[2,1920,256]{2,1,0:T(8,128)(2,1)S(1)} %copy-done.11, bf16[2,1920,256]{2,1,0:T(8,128)(2,1)S(1)} %copy-done.13, bf16[2,1920,256]{2,1,0:T(8,128)(2,1)} %get-tuple-element.71.g_ref, s32[2,1920,1]{2,1,0:T(8,128)} %get-tuple-element.58.low_ref, ...), custom_call_target="tpu_custom_call" | custom-call | flops 15099494400 | bytes 23592960 | tf_op jit(solution)/shard_map/attend_back/pallas_call | solution.py:1114
  848.8 2.1 copy.76
  852.5 4.2 all-to-all-start.2
  856.7 19.1 %bitcast_convert_fusion = bf16[2304,768]{0,1:T(8,128)(2,1)S(1)} fusion(bf16[2,1920,2304]{2,1,0:T(8,128)(2,1)} %get-tuple-element.51.x_ref, bf16[2,1920,768]{2,1,0:T(8,128)(2,1)} %attend_back.1.refs_0_), kind=kOutput, calls=%fused_computation.5 | convolution fusion | flops 13591314432 | bytes 27131904 | tf_op jit(solution)/shard_map/dot_general | solution.py:77
  883.4 2.5 copy.91
  887.4 3.7 copy.89
  891.1 93.1 %scatter_grad_normed.1 = (f32[2,240,2304]{2,1,0:T(8,128)}, bf16[8,64,288]{2,1,0:T(8,128)(2,1)}) custom-call(bf16[2,1920,768]{2,1,0:T(8,128)(2,1)} %attend_back.1.refs_0_, bf16[2304,512]{1,0:T(8,128)(2,1)} %bitcast.72, bf16[2304,256]{1,0:T(8,128)(2,1)} %copy-done.6, bf16[8,64,288]{2,1,0:T(8,128)(2,1)} %bitcast.84), custom_call_target="tpu_custom_call" | custom-call | flops 13589544960 | bytes 270000000 | tf_op jit(solution)/shard_map/scatter_grad_normed/pallas_call | solution.py:713
  984.3 3.6 fusion.5
  988.6 21.1 %sum_gains.1 = f32[8,2304]{1,0:T(8,128)} custom-call(f32[8,2304]{1,0:T(8,128)} %select_maximum_fusion.value_ref), custom_call_target="tpu_custom_call" | custom-call | tf_op jit(solution)/shard_map/sum_gains/pallas_call | solution.py:786
  1010.9 3.4 copy.87
  1015.1 2.9 copy.80
  1018.0 4.3 all-to-all-start.3
  1022.3 6.9 fusion.10
  1033.4 8.9 all-to-all-done.3
  1042.3 3.1 bitcast_convert_fusion.1
  1045.4 3.4 copy.88
  (187 shorter events, 51.8 us)
Async XLA Ops:
  7.2 121.2 %all-gather.12.cloned.1.call-start = ((), (), s32[]{:S(2)}) async-start(), calls=%async_computation.16 | async-start | bytes 4423680 | tf_op jit(solution)/shard_map/all_gather | solution.py:1151
  12.3 269.1 %all-gather.8.cloned.1.call-start = ((), (), s32[]{:S(2)}) async-start(), calls=%async_computation.10 | async-start | bytes 6635520 | tf_op jit(solution)/shard_map/all_gather | solution.py:122
  19.6 8.7 copy-start.50
  19.6 24.7 %copy-start.18 = (bf16[2,1,240,2304]{3,2,1,0:T(8,128)(2,1)S(1)}, bf16[2,1,240,2304]{3,2,1,0:T(8,128)(2,1)}, u32[]{:S(2)}) copy-start(bf16[2,1,240,2304]{3,2,1,0:T(8,128)(2,1)} %param.14) | copy-start | bytes 6635524
  24.1 20.7 %copy-start.33 = (f32[2304]{0:T(1024)S(1)}, f32[2304]{0:T(1024)}, u32[]{:S(2)}) copy-start(f32[2304]{0:T(1024)} %param.23) | copy-start | bytes 27652
  24.1 260.0 %all-gather.6.cloned.1.call-start = ((), (), s32[]{:S(2)}) async-start(), calls=%async_computation.9 | async-start | bytes 6635520 | tf_op jit(solution)/shard_map/all_gather | solution.py:122
  28.2 354.9 %all-gather.10.cloned.1.call-start = ((), (), s32[]{:S(2)}) async-start(), calls=%async_computation.11 | async-start | bytes 6635520 | tf_op jit(solution)/shard_map/all_gather | solution.py:122
  44.8 83.6 %copy-start.44 = (f32[2,240]{1,0:T(2,128)}, f32[2,240]{1,0:T(2,128)S(1)}, u32[]{:S(2)}) copy-start(f32[2,240]{1,0:T(2,128)S(1)} %fusion.12) | copy-start | bytes 5764
  44.8 83.6 %copy-start.40 = (f32[2,240]{1,0:T(2,128)}, f32[2,240]{1,0:T(2,128)S(1)}, u32[]{:S(2)}) copy-start(f32[2,240]{1,0:T(2,128)S(1)} %fusion.15) | copy-start | bytes 5764
  130.2 14.2 %copy-start.2 = (bf16[4,576,512]{2,1,0:T(8,128)(2,1)}, bf16[4,576,512]{2,1,0:T(8,128)(2,1)S(1)}, u32[]{:S(2)}) copy-start(bf16[4,576,512]{2,1,0:T(8,128)(2,1)S(1)} %slice.53) | copy-start | bytes 7077892
  131.4 13.0 %collective-permute-start = (bf16[2304,256]{1,0:T(8,128)(2,1)}, bf16[2304,256]{1,0:T(8,128)(2,1)S(1)}, u32[]{:S(2)}, u32[]{:S(2)}) collective-permute-start(bf16[2304,256]{1,0:T(8,128)(2,1)} %slice.66), channel_id=1, source_target_pairs={{0,4},{4,0},{8,12},{12,8},{16,20},{20,16},{24,28},{28,24},{1,5},{5... | collective-permute-start | bytes 3538952 | tf_op jit(solution)/shard_map/ppermute | solution.py:1183
  139.9 47.7 %all-to-all-start = ((bf16[8,32,2304]{2,1,0:T(8,128)(2,1)}), bf16[8,32,2304]{2,1,0:T(8,128)(2,1)}, u32[]{:S(2)}, u32[]{:S(2)}) async-start(bf16[8,32,2304]{2,1,0:T(8,128)(2,1)} %all_to_all.29), calls=%async_computation | async-start | bytes 2359296 | tf_op jit(solution)/shard_map/all_to_all | solution.py:132
  144.2 569.7 %reduce-scatter.8.cloned.1.call-start = ((), (), s32[]{:S(2)}) async-start(), calls=%async_computation.12 | async-start | bytes 6635520 | tf_op jit(solution)/shard_map/reduce_scatter | solution.py:126
  144.4 20.8 %copy-start.6 = (bf16[2304,256]{1,0:T(8,128)(2,1)}, bf16[2304,256]{1,0:T(8,128)(2,1)S(1)}, u32[]{:S(2)}) copy-start(bf16[2304,256]{1,0:T(8,128)(2,1)S(1)} %collective-permute-done.far_ref.refs_2_) | copy-start | bytes 3538948
  148.0 17.3 %copy-start.5 = (s32[2,1920,1]{2,1,0:T(8,128)S(1)}, s32[2,1920,1]{2,1,0:T(8,128)}, u32[]{:S(2)}) copy-start(s32[2,1920,1]{2,1,0:T(8,128)} %get-tuple-element.58.low_ref) | copy-start | bytes 46084
  187.6 88.5 %copy-start.19 = (bf16[2,1,240,2304]{3,2,1,0:T(8,128)(2,1)S(1)}, bf16[2,1,240,2304]{3,2,1,0:T(8,128)(2,1)}, u32[]{:S(2)}) copy-start(bf16[2,1,240,2304]{3,2,1,0:T(8,128)(2,1)} %param.14) | copy-start | bytes 6635524
  187.6 88.5 %copy-start.31 = (f32[2304]{0:T(1024)S(1)}, f32[2304]{0:T(1024)}, u32[]{:S(2)}) copy-start(f32[2304]{0:T(1024)} %param.24) | copy-start | bytes 27652
  272.8 3.6 copy-start.17
  276.4 3.2 copy-start.29
  277.5 101.4 %copy-start.48 = (f32[2,240]{1,0:T(2,128)}, f32[2,240]{1,0:T(2,128)S(1)}, u32[]{:S(2)}) copy-start(f32[2,240]{1,0:T(2,128)S(1)} %get-tuple-element.158) | copy-start | bytes 5764
  277.5 101.4 %copy-start.38 = (f32[2,240]{1,0:T(2,128)}, f32[2,240]{1,0:T(2,128)S(1)}, u32[]{:S(2)}) copy-start(f32[2,240]{1,0:T(2,128)S(1)} %fusion.17) | copy-start | bytes 5764
  383.1 94.2 %copy-start.23 = (bf16[2,1,240,2304]{3,2,1,0:T(8,128)(2,1)S(1)}, bf16[2,1,240,2304]{3,2,1,0:T(8,128)(2,1)}, u32[]{:S(2)}) copy-start(bf16[2,1,240,2304]{3,2,1,0:T(8,128)(2,1)} %param.27) | copy-start | bytes 6635524
  383.1 94.2 %copy-start.37 = (f32[2304]{0:T(1024)S(1)}, f32[2304]{0:T(1024)}, u32[]{:S(2)}) copy-start(f32[2304]{0:T(1024)} %param.26) | copy-start | bytes 27652
  474.4 3.6 copy-start.22
  582.2 221.6 %reduce-scatter.10.cloned.1.call-start = ((), (), s32[]{:S(2)}) async-start(), calls=%async_computation.13 | async-start | bytes 6635520 | tf_op jit(solution)/shard_map/reduce_scatter | solution.py:126
  697.2 5.6 slice-start
  697.2 153.7 %reduce-scatter.12.cloned.1.call-start = ((), (), s32[]{:S(2)}) async-start(), calls=%async_computation.14 | async-start | bytes 1474560 | tf_op jit(solution)/shard_map/reduce_scatter | solution.py:126
  697.8 4.8 copy-start.49
  697.9 5.4 slice-start.1
  697.9 5.4 copy-start.32
  697.9 5.4 copy-start.43
  697.9 13.7 %slice-start.2 = ((s8[4423680]{0:T(1024)(128)(4,1)}), s8[4194304]{0:T(1024)(128)(4,1)S(1)}, s32[]{:S(2)}) async-start(s8[4423680]{0:T(1024)(128)(4,1)} %bitcast.75), calls=%async_computation.20 | async-start | bytes 8388608
  703.2 6.3 copy-start.47
  703.2 8.4 slice-start.3
  803.0 212.1 %reduce-scatter.14.cloned.1.call-start = ((), (), s32[]{:S(2)}) async-start(), calls=%async_computation.15 | async-start | bytes 6635520 | tf_op jit(solution)/shard_map/reduce_scatter | solution.py:126
  803.7 12.4 %copy-start.9 = (bf16[2,1920,256]{2,1,0:T(8,128)(2,1)S(1)}, bf16[2,1920,256]{2,1,0:T(8,128)(2,1)}, u32[]{:S(2)}) copy-start(bf16[2,1920,256]{2,1,0:T(8,128)(2,1)} %copy-done.8) | copy-start | bytes 5898244
  811.6 35.4 %all-to-all-start.1 = ((bf16[288,8,288]{2,0,1:T(8,128)(2,1)}), bf16[288,8,288]{2,0,1:T(8,128)(2,1)}, u32[]{:S(2)}, u32[]{:S(2)}) async-start(bf16[288,8,288]{2,0,1:T(8,128)(2,1)} %copy.75), calls=%async_computation.4 | async-start | bytes 3538944 | tf_op jit(solution)/shard_map/all_to_all | solution.py:132
  852.5 26.0 %all-to-all-start.2 = ((bf16[576,8,144]{0,2,1:T(8,128)(2,1)}), bf16[576,8,144]{0,2,1:T(8,128)(2,1)S(1)}, u32[]{:S(2)}, u32[]{:S(2)}) async-start(bf16[576,8,144]{0,2,1:T(8,128)(2,1)} %bitcast.80), calls=%async_computation.5 | async-start | bytes 2949120 | tf_op jit(solution)/shard_map/all_to_all | solution.py:132
  856.7 172.4 %reduce-scatter.16.cloned.1.call-start = ((), (), s32[]{:S(2)}) async-start(), calls=%async_computation.17 | async-start | bytes 2949120
  878.0 3.3 collective-permute-start.1
  891.1 93.1 %copy-start.20 = (bf16[2,1,240,2304]{3,2,1,0:T(8,128)(2,1)S(1)}, bf16[2,1,240,2304]{3,2,1,0:T(8,128)(2,1)}, u32[]{:S(2)}) copy-start(bf16[2,1,240,2304]{3,2,1,0:T(8,128)(2,1)} %param.14) | copy-start | bytes 6635524
  891.1 93.1 %copy-start.34 = (f32[2304]{0:T(1024)S(1)}, f32[2304]{0:T(1024)}, u32[]{:S(2)}) copy-start(f32[2304]{0:T(1024)} %param.23) | copy-start | bytes 27652
  891.1 93.1 %copy-start.41 = (f32[2,240]{1,0:T(2,128)S(1)}, f32[2,240]{1,0:T(2,128)}, u32[]{:S(2)}) copy-start(f32[2,240]{1,0:T(2,128)} %copy-done.40) | copy-start | bytes 5764
  984.2 25.5 %copy-start.26 = (bf16[8,64,288]{2,1,0:T(8,128)(2,1)S(1)}, bf16[8,64,288]{2,1,0:T(8,128)(2,1)}, u32[]{:S(2)}) copy-start(bf16[8,64,288]{2,1,0:T(8,128)(2,1)} %get-tuple-element.83) | copy-start | bytes 884740
  987.9 27.1 %copy-start.45 = (f32[2,240]{1,0:T(2,128)S(1)}, f32[2,240]{1,0:T(2,128)}, u32[]{:S(2)}) copy-start(f32[2,240]{1,0:T(2,128)} %copy-done.44) | copy-start | bytes 5764
  1009.8 4.6 copy-start.28
  1018.0 24.3 %all-to-all-start.3 = ((bf16[576,8,144]{0,2,1:T(8,128)(2,1)}), bf16[576,8,144]{0,2,1:T(8,128)(2,1)}, u32[]{:S(2)}, u32[]{:S(2)}) async-start(bf16[576,8,144]{0,2,1:T(8,128)(2,1)} %bitcast.79), calls=%async_computation.7 | async-start | bytes 2949120 | tf_op jit(solution)/shard_map/all_to_all | solution.py:132
  1032.5 16.3 %copy-start.1 = (bf16[512,2304]{1,0:T(8,128)(2,1)S(1)}, bf16[512,2304]{1,0:T(8,128)(2,1)}, u32[]{:S(2)}) copy-start(bf16[512,2304]{1,0:T(8,128)(2,1)} %param.19) | copy-start | bytes 7077892
  (22 other events, 36.8 us)
Sparse Core Ops, SparseCore 0:
  12.4 72.6 all-gather.11
  86.7 97.7 all-gather.7
  186.6 97.4 all-gather.5
  285.5 97.4 all-gather.9
  582.3 94.2 reduce-scatter.7
  697.3 93.6 reduce-scatter.9
  803.1 27.5 reduce-scatter.11
  833.0 118.7 reduce-scatter.13
  954.2 47.9 reduce-scatter.15

commit v5 on v4

--- a/solution.py
+++ b/solution.py
@@ -145,13 +145,13 @@
     return me, other_core, along_x, along_y
 
 
-def greet(neighbours, spread=None):
+def greet(neighbours, *others):
     barrier = pltpu.get_barrier_semaphore()
     for neighbour in neighbours:
         pl.semaphore_signal(barrier, inc=1, device_id={"seq": neighbour}, device_id_type=MESH)
     count = len(neighbours)
-    if spread is not None:
-        count = count + spread.greet(barrier)
+    for other in others:
+        count = count + other.greet(barrier)
     pl.semaphore_wait(barrier, count)
 
 
@@ -170,6 +170,9 @@
             for from_layer in range(layers)
         ]
 
+    def turn(self):
+        pass
+
     def away(self, device):
         return (device[0] != self.me) | (device[1] != self.layer)
 
@@ -208,6 +211,90 @@
         for index, device in enumerate(self.sources):
             pl.when(self.away(device))(self.copy(0, index, device).wait_recv)
         pl.when(self.owner == self.layer)(self.own().wait)
+
+
+class SmallSum:
+    def __init__(self, over_layers, value_ref, out_ref, *scratch):
+        self.over_layers, self.value, self.out = over_layers, value_ref, out_ref
+        self.plane_buf, self.layer_buf, self.plane_sems, self.layer_sems = scratch
+        self.me, *neighbours = plane_places()
+        steps = [neighbour - self.me for neighbour in neighbours]
+        self.peers = [
+            self.me + sum(step for bit, step in enumerate(steps) if (index >> bit) % 2)
+            for index in range(1, 8)
+        ]
+        self.layer, self.layers = lax.axis_index("fsdp"), lax.axis_size("fsdp")
+        hops = range(1, self.layers) if over_layers else []
+        self.others = [lax.rem(self.layer + hop, self.layers) for hop in hops]
+
+    @staticmethod
+    def scratch(value):
+        layers = lax.axis_size("fsdp")
+        return [
+            pltpu.VMEM((8,) + value.shape, value.dtype),
+            pltpu.VMEM((layers,) + value.shape, value.dtype),
+            pltpu.SemaphoreType.DMA((2, 7)),
+            pltpu.SemaphoreType.DMA((2, layers)),
+        ]
+
+    def greet(self, barrier):
+        farther = [peer for index, peer in enumerate(self.peers) if index not in (0, 1, 3)]
+        for peer in farther:
+            pl.semaphore_signal(barrier, inc=1, device_id={"seq": peer}, device_id_type=MESH)
+        for other in self.others:
+            pl.semaphore_signal(barrier, inc=1, device_id={"fsdp": other}, device_id_type=MESH)
+        return len(farther) + len(self.others)
+
+    def copy(self, buf, sems, slot, index, device):
+        return pltpu.make_async_remote_copy(
+            src_ref=buf.at[slot],
+            dst_ref=buf.at[slot],
+            send_sem=sems.at[0, index],
+            recv_sem=sems.at[1, index],
+            device_id=device,
+            device_id_type=MESH,
+        )
+
+    def plane_copies(self):
+        return [
+            self.copy(self.plane_buf, self.plane_sems, self.me, index, {"seq": peer})
+            for index, peer in enumerate(self.peers)
+        ]
+
+    def layer_copies(self):
+        return [
+            self.copy(self.layer_buf, self.layer_sems, self.layer, index, {"fsdp": other})
+            for index, other in enumerate(self.others)
+        ]
+
+    def begin(self):
+        self.plane_buf[self.me] = self.value[...]
+        for copy in self.plane_copies():
+            copy.start()
+
+    def turn(self):
+        for copy in self.plane_copies():
+            copy.wait_recv()
+        total = self.plane_buf[0]
+        for index in range(1, 8):
+            total = total + self.plane_buf[index]
+        if not self.over_layers:
+            self.out[...] = total
+            return
+        self.layer_buf[self.layer] = total
+        for copy in self.layer_copies():
+            copy.start()
+
+    def end(self):
+        for copy in self.layer_copies():
+            copy.wait_recv()
+        if self.over_layers:
+            total = self.layer_buf[0]
+            for index in range(1, self.layers):
+                total = total + self.layer_buf[index]
+            self.out[...] = total
+        for copy in self.plane_copies() + self.layer_copies():
+            copy.wait_send()
 
 
 BRAID = 384
@@ -266,9 +353,10 @@
         tables=(),
         spare=None,
         spread=None,
+        small=None,
         flops=0,
     ):
-        self.spread = spread
+        self.spread, self.small = spread, small
         self.compute, self.flops, self.spare = compute, flops, spare
         self.tables = list(tables)
         self.weights, self.extras, self.outs = list(weights), list(extras), list(outs)
@@ -284,7 +372,7 @@
         take(len(job.extras)),
         take(len(job.side)),
     )
-    table_refs = take(len(job.tables))
+    table_refs, count_refs = take(len(job.tables)), take(1 if job.small is not None else 0)
     (whole_ref,), out_refs, final_refs = take(1), take(len(job.outs)), take(len(job.sums))
     made_refs = take(len(job.spare[1]) if job.spare else 0)
     send_sem, recv_sem, own_sem, x_buf = take(4)
@@ -296,6 +384,10 @@
     )
     sum_bufs, final_bufs = take(len(job.sums)), take(len(job.sums))
     weight_sem, load_sem, side_sem, store_sem, final_sem = take(5)
+    if count_refs:
+        summed = take(1)[0]
+        small = SmallSum(False, count_refs[0], summed, *take(4))
+        table_refs = [summed] + table_refs
 
     me, other_core, along_x, along_y = plane_places()
     across = along_x + along_y - me
@@ -333,7 +425,9 @@
         forward(12, 0, across, other_core),
         forward(13, 1, across, other_core),
     ]
-    greet((other_core, along_x, along_y))
+    greet((other_core, along_x, along_y), *([small] if count_refs else []))
+    if count_refs:
+        small.begin()
     for slot in (0, 2, 1, 3, 6, 7):
         moves[slot].start()
     owns = [
@@ -345,6 +439,8 @@
     fetches = copies_into(weight_refs, weight_bufs[0], weight_sem) if job.weights else []
     for fetch in fetches:
         fetch.start()
+    if count_refs:
+        small.turn()
     if job.spare:
         job.spare[0](table_refs, made_refs)
     stores = []
@@ -457,6 +553,8 @@
         move.wait_send()
     for own in owns:
         own.wait()
+    if count_refs:
+        small.end()
     for group in stores[-2:]:
         for store in group:
             store.wait()
@@ -535,6 +633,10 @@
     in_specs = [any_space] * len(inputs)
     in_specs += [pl.BlockSpec(memory_space=pltpu.VMEM)] * len(job.tables)
     inputs += job.tables
+    if job.small is not None:
+        inputs.append(job.small)
+        in_specs.append(pl.BlockSpec(memory_space=pltpu.VMEM))
+        scratch += [pltpu.VMEM(job.small.shape, job.small.dtype)] + SmallSum.scratch(job.small)
     out_specs = [any_space] * len(out_shape)
     if job.spare:
         out_shape += job.spare[1]
@@ -564,13 +666,19 @@
         take(len(job.side)),
     )
     spread_refs = take(1 if job.spread is not None else 0)
+    small_refs = take(1 if job.small is not None else 0)
     (out_ref,), final_refs = take(1), take(len(job.sums))
     spread_refs += take(len(spread_refs))
+    small_refs += take(len(small_refs))
     part_buf, weight_buf, sums, held, from_core, from_link, out_buf = take(7)
     side_bufs, sum_bufs, final_bufs = take(len(job.side)), take(len(job.sums)), take(len(job.sums))
     weight_sem, load_sem, side_sem, final_sem, out_sem = take(5)
     core_send, core_recv, link_send, link_recv, credit = take(5)
-    spread = Spread(*spread_refs, *take(2)) if spread_refs else None
+    riders = []
+    if spread_refs:
+        riders.append(Spread(*spread_refs, *take(2)))
+    if small_refs:
+        riders.insert(0, SmallSum(True, *small_refs, *take(4)))
 
     me, other_core, along_x, along_y = plane_places()
     across = along_x + along_y - me
@@ -622,9 +730,9 @@
         )
         for step in range(6)
     ]
-    greet((other_core, along_x, along_y), spread)
-    if spread is not None:
-        spread.begin()
+    greet((other_core, along_x, along_y), *riders)
+    for rider in riders:
+        rider.begin()
 
     def finish(step):
         gives[step].wait_recv()
@@ -662,14 +770,16 @@
         gives[step].start()
         if step >= 1:
             finish(step - 1)
+        for rider in riders if step == 4 else []:
+            rider.turn()
         side.run((0, 0, 1, 1, 1, 1, 2, 2)[step])
     if job.side:
         finish_sums(sum_bufs, final_bufs, final_refs, final_sem)
     finish(7)
     for move in gives[6:] + sends:
         move.wait_send()
-    if spread is not None:
-        spread.end()
+    for rider in riders:
+        rider.end()
 
 
 def plane_scatter(parts, width, ident, name, job):
@@ -706,14 +816,23 @@
     out_shape = [jax.ShapeDtypeStruct((batches, rows, width), jnp.float32)]
     out_shape += [jax.ShapeDtypeStruct(shape, jnp.bfloat16) for shape in job.sums]
     inputs = [*parts, *weights, *job.side]
+    in_specs, out_specs = [any_space] * len(inputs), [any_space] * len(out_shape)
     if job.spread is not None:
         inputs.append(job.spread)
+        in_specs.append(any_space)
         out_shape.append(jax.ShapeDtypeStruct(job.spread.shape, job.spread.dtype))
+        out_specs.append(any_space)
         scratch += [semaphores((job.spread.shape[0] + 1,)), semaphores((job.spread.shape[0],))]
+    if job.small is not None:
+        inputs.append(job.small)
+        in_specs.append(pl.BlockSpec(memory_space=pltpu.VMEM))
+        out_shape.append(jax.ShapeDtypeStruct(job.small.shape, job.small.dtype))
+        out_specs.append(pl.BlockSpec(memory_space=pltpu.VMEM))
+        scratch += SmallSum.scratch(job.small)
     return pl.pallas_call(
         functools.partial(scatter_kernel, job, rows),
-        in_specs=[any_space] * len(inputs),
-        out_specs=[any_space] * len(out_shape),
+        in_specs=in_specs,
+        out_specs=out_specs,
         out_shape=out_shape,
         scratch_shapes=scratch,
         compiler_params=pltpu.CompilerParams(
@@ -724,81 +843,6 @@
         ),
         name=name,
     )(*inputs)
-
-
-def small_sum_kernel(over_layers, value_ref, out_ref, plane_buf, layer_buf, *sems):
-    plane_send, plane_recv, layer_send, layer_recv = sems
-    neighbours = plane_places()[1:]
-    layer, layers = lax.axis_index("fsdp"), lax.axis_size("fsdp")
-    others = [lax.rem(layer + hop, layers) for hop in range(1, layers)] if over_layers else []
-    barrier = pltpu.get_barrier_semaphore()
-    for neighbour in neighbours:
-        pl.semaphore_signal(barrier, inc=1, device_id={"seq": neighbour}, device_id_type=MESH)
-    for other in others:
-        pl.semaphore_signal(barrier, inc=1, device_id={"fsdp": other}, device_id_type=MESH)
-    pl.semaphore_wait(barrier, len(neighbours) + len(others))
-    out_ref[...] = value_ref[...]
-    copies = []
-    for turn, neighbour in enumerate(neighbours):
-        plane_buf[turn, 0] = out_ref[...]
-        copies.append(
-            pltpu.make_async_remote_copy(
-                src_ref=plane_buf.at[turn, 0],
-                dst_ref=plane_buf.at[turn, 1],
-                send_sem=plane_send.at[turn],
-                recv_sem=plane_recv.at[turn],
-                device_id={"seq": neighbour},
-                device_id_type=MESH,
-            )
-        )
-        copies[-1].start()
-        copies[-1].wait_recv()
-        out_ref[...] = plane_buf[turn, 0] + plane_buf[turn, 1]
-    if over_layers:
-        layer_buf[layer] = out_ref[...]
-        layer_copies = [
-            pltpu.make_async_remote_copy(
-                src_ref=layer_buf.at[layer],
-                dst_ref=layer_buf.at[layer],
-                send_sem=layer_send.at[hop],
-                recv_sem=layer_recv.at[hop],
-                device_id={"fsdp": other},
-                device_id_type=MESH,
-            )
-            for hop, other in enumerate(others)
-        ]
-        for copy in layer_copies:
-            copy.start()
-        for copy in layer_copies:
-            copy.wait_recv()
-        total = layer_buf[0]
-        for index in range(1, layers):
-            total = total + layer_buf[index]
-        out_ref[...] = total
-        copies += layer_copies
-    for copy in copies:
-        copy.wait_send()
-
-
-def small_sum(value, over_layers, ident, name):
-    layers = lax.axis_size("fsdp")
-    semaphores = pltpu.SemaphoreType.DMA
-    return pl.pallas_call(
-        functools.partial(small_sum_kernel, over_layers),
-        in_specs=[pl.BlockSpec(memory_space=pltpu.VMEM)],
-        out_specs=pl.BlockSpec(memory_space=pltpu.VMEM),
-        out_shape=jax.ShapeDtypeStruct(value.shape, jnp.float32),
-        scratch_shapes=[
-            pltpu.VMEM((3, 2) + value.shape, jnp.float32),
-            pltpu.VMEM((layers,) + value.shape, jnp.float32),
-            semaphores((3,)),
-            semaphores((3,)),
-            semaphores((layers,)),
-            semaphores((layers,)),
-        ],
-        compiler_params=pltpu.CompilerParams(collective_id=ident, has_side_effects=True),
-        name=name,
-    )(value)
 
 
 def tiles(width, tile, body):
@@ -1148,6 +1192,7 @@
         part = lax.dynamic_index_in_dim(part, place, axis=1, keepdims=False)
         rows = joined.shape[0]
         both = jnp.concatenate([joined, part.reshape(-1, joined.shape[1])], axis=0)
+        self.first = both
         self.both = lax.all_gather(both, "fsdp", axis=0)
         self.split = rows
         self.part_shape = (QUERY_HEADS * depth, w_out.shape[1])
@@ -1156,14 +1201,10 @@
         batches, rows, width = normed.shape
         length = rows * lax.axis_size("seq")
         half = HEAD_SIZE // 2
-        counts = [
-            jnp.sum((segments[batch] < number).astype(jnp.float32))
-            for batch in range(batches)
-            for number in range(1, DOCUMENTS)
-        ]
-        counts += [jnp.zeros(())] * (8 - len(counts))
-        counts = jnp.broadcast_to(jnp.stack(counts)[:, None], (8, half))
-        counts = small_sum(counts, False, 8, "sum_counts")
+        numbers = jnp.arange(1, DOCUMENTS, dtype=segments.dtype)
+        counts = jnp.sum((segments[:, None] < numbers[:, None]).astype(jnp.float32), axis=2)
+        counts = jnp.pad(counts.reshape(-1), (0, 8 - batches * (DOCUMENTS - 1)))
+        counts = jnp.broadcast_to(counts[:, None], (8, half))
         frequency = 10000.0 ** (-jnp.arange(half, dtype=jnp.float32) * 2.0 / HEAD_SIZE)
         table = jax.ShapeDtypeStruct((batches, length, half), jnp.float32)
         bound = jax.ShapeDtypeStruct((batches, length, 1), jnp.int32)
@@ -1173,7 +1214,8 @@
             "gather_normed",
             Job(
                 None,
-                tables=[counts, frequency[None]],
+                tables=[frequency[None]],
+                small=counts,
                 spare=(token_tables, [table, table, bound]),
             ),
         )
@@ -1215,9 +1257,16 @@
         grads, self.out_own = lax.optimization_barrier((grads, scatter_rows(self.out_sum)))
         return grads
 
-    def close_back(self, grads, saved, meanwhile):
+    def close_back(self, grads, saved, meanwhile, gains):
         count = lax.axis_size("seq")
         joined = dot_rows(saved[0], grads).astype(jnp.bfloat16)
+        wide = 2 * HEAD_SIZE
+        pairs = ((joined[:, :wide], self.joined), (joined[:, wide:], self.far))
+        through = sum(
+            jnp.sum(grad.astype(jnp.float32) * weight.astype(jnp.float32), axis=1)
+            for grad, weight in pairs
+        )
+        gains = jnp.stack([through, *gains])
         own, far = joined[:, HEAD_SIZE : 2 * HEAD_SIZE], joined[:, 2 * HEAD_SIZE :]
         came = lax.ppermute(far, "seq", [(i, i ^ 1) for i in range(count)])
         own = (own.astype(jnp.float32) + came.astype(jnp.float32)).astype(jnp.bfloat16)
@@ -1232,28 +1281,29 @@
             back_compute,
             weights=[self.joined, self.far],
             spread=parts,
+            small=gains.reshape(-1, HEAD_SIZE // 2),
             flops=6 * rows * HEAD_SIZE * width,
         )
-        grad_normed, self.placed = plane_scatter([grads], width, 3, "scatter_grad_normed", job)
-        return grad_normed, meanwhile
-
-    def weight_grads(self, gains):
+        grad_normed, self.placed, gains = plane_scatter(
+            [grads], width, 3, "scatter_grad_normed", job
+        )
+        return grad_normed, meanwhile, gains.reshape(4, -1)
+
+    def weight_grads(self):
         half = HEAD_SIZE // 2
         joined = scatter_rows(self.joined_sum).astype(jnp.float32)
-        gains = small_sum(jnp.pad(gains, ((0, 4), (0, 0))), True, 9, "sum_gains")
         return (
             joined[:, :HEAD_SIZE],
             joined[:, HEAD_SIZE : HEAD_SIZE + half],
             joined[:, HEAD_SIZE + half :],
             self.placed.astype(jnp.float32).reshape(-1, self.placed.shape[2]),
-            gains,
         )
 
 
 class ByTokens:
     def __init__(self, w_query, key_weight, value_weight, w_out):
         self.weights = fetch_attention(w_query, key_weight, value_weight, w_out)
-        self.records = []
+        self.records, self.first = [], jnp.zeros(())
 
     def forward(self, normed, segments):
         seg_whole = lax.all_gather(segments, "seq", axis=1, tiled=True)
@@ -1308,9 +1358,9 @@
     def middle_back(self, grad_mixed_b, saved):
         return grad_mixed_b
 
-    def close_back(self, grad_mixed_b, saved, meanwhile):
+    def close_back(self, grad_mixed_b, saved, meanwhile, gains):
         grads = [self.backward_one(*pair) for pair in zip(grad_mixed_b, saved)]
-        return jnp.stack(grads), meanwhile
+        return jnp.stack(grads), meanwhile, None
 
     def backward_one(self, grad_mixed_b, saved):
         normed, query, pair, allowed, log_total, cosine, sine, attended = saved
@@ -1345,7 +1395,7 @@
         self.records.append((normed, dq, dk, dv, attended, grad_mixed_b))
         return dot_back(dq, w_query) + dot_back(dk, key_weight) + dot_back(dv, value_weight)
 
-    def weight_grads(self, gains):
+    def weight_grads(self):
         normed, dq, dk, dv, attended, grad_mixed_b = (
             jnp.concatenate(parts, axis=0) for parts in zip(*self.records)
         )
@@ -1356,12 +1406,12 @@
             column_sum = dot_rows(rows, swap_parts(grads, 1, 0)).astype(jnp.bfloat16)
             owned = lax.psum_scatter(column_sum, "fsdp", scatter_dimension=0, tiled=True)
             sums.append(owned.astype(jnp.float32))
-        return tuple(sums) + (lax.psum(gains, ("seq", "fsdp")),)
+        return tuple(sums)
 
 
 class FeedForward:
-    def __init__(self, w_gate, w_up, w_down, by_kernel):
-        place = lax.axis_index("seq")
+    def __init__(self, w_gate, w_up, w_down, by_kernel, first):
+        place = lax.optimization_barrier((lax.axis_index("seq"), first))[0]
         count = lax.axis_size("seq")
         self.by_kernel = by_kernel
         self.run = w_gate.shape[1] // (count * count)
@@ -1482,7 +1532,7 @@
         and QUERY_HEADS % lax.axis_size("fsdp") == 0
     )
     attention = (ByHeads if by_kernel else ByTokens)(w_query, key_weight, value_weight, w_out)
-    ffn = FeedForward(w_gate, w_up, w_down, by_kernel)
+    ffn = FeedForward(w_gate, w_up, w_down, by_kernel, attention.first)
 
     stream = tokens[:, 0].astype(jnp.float32)
     normed = rms_gain(stream, gain_attn_in).astype(jnp.bfloat16)
@@ -1509,16 +1559,24 @@
     w_down_grad = ffn.own_rows(w_down_grad)
     grads = attention.middle_back(grad_att, attention_saved)
     grads, w_gate_grad, w_down_grad = lax.optimization_barrier((grads, w_gate_grad, w_down_grad))
-    grad_normed, w_gate_grad = attention.close_back(
-        grads, attention_saved, ffn.own_columns(w_gate_grad)
+    grad_normed, w_gate_grad, gains = attention.close_back(
+        grads,
+        attention_saved,
+        ffn.own_columns(w_gate_grad),
+        [grad_gain_two, grad_gain_three, grad_gain_four],
     )
     _, pullback = jax.vjp(rms_gain, stream, gain_attn_in)
     grad_stream, grad_gain_one = pullback(grad_normed)
     grad_stream = grad_middle + grad_stream
 
     w_up_grad = ffn.own_columns(scatter_rows(up_sum))
-    gains = jnp.stack([grad_gain_one, grad_gain_two, grad_gain_three, grad_gain_four])
-    query_grad, key_grad, value_grad, out_grad, gains = attention.weight_grads(gains)
+    if gains is None:
+        gains = jnp.stack([grad_gain_one, grad_gain_two, grad_gain_three, grad_gain_four])
+        gains = lax.psum(gains, ("seq", "fsdp"))
+        grad_gain_one = gains[0]
+    else:
+        grad_gain_one = gains[0] / gain_attn_in
+    query_grad, key_grad, value_grad, out_grad = attention.weight_grads()
     return (
         result.astype(jnp.bfloat16)[:, None],
         grad_stream[:, None],
@@ -1529,7 +1587,7 @@
         w_gate_grad,
         w_up_grad,
         w_down_grad,
-        gains[0],
+        grad_gain_one,
         gains[1],
         gains[2],
         gains[3],

time: 1060 us -> 1060 us (level)
  Pallas kernels: 841 us -> 816 us
  waiting for transfers between devices: 17.7 us -> 28.5 us
    pallas_call x6 -> x4, Pallas kernels: 416 us -> 387 us  [plane_scatter(): pl.pallas_call(functools.partial(scatter_kernel, job, rows), in_specs=in_...]
    all_gather x3, waiting for transfers between devices: 6.98 us -> 18.2 us  [gather_rows(): return lax.all_gather(rows, 'fsdp', axis=0, tiled=True)]
    unnamed x119 -> x113, local copies, waits for them, and re-layouts: 40.7 us -> 35.9 us
  transfers between devices with their start and end apart: 15 -> 15, of which waited for: 4 -> 3; matrix products, arithmetic and copies ran while one was open for 11% -> 11% of each run, Pallas kernels for 62% -> 60%
where the time goes in v5:
time: 1060 us; the launch traced here: 1050 us
  Pallas kernels  816 us (77%)
  local copies, waits for them, and re-layouts  87.2 us (8%)
  other arithmetic  62.1 us (6%)
  waiting for transfers between devices  28.5 us (3%)
  starting transfers between devices  20.4 us (2%)
  matrix products  19.2 us (2%)
  between operations  15.1 us (1%)
    pallas_call x4, Pallas kernels, plane_scatter(): pl.pallas_call(functools.partial(scatter_kernel, job, rows), in_specs=in_...  387 us
    pallas_call x4, Pallas kernels, plane_gather(): pl.pallas_call(functools.partial(gather_kernel, job, rows), in_specs=in_s...  368 us
    unnamed x113, local copies, waits for them, and re-layouts  35.9 us
    pallas_call x1, Pallas kernels, attend_back(): pl.pallas_call(functools.partial(attend_back_kernel, block, reach), grid=...  27.8 us
  transfers between devices with their start and end apart: 15, of which 3 were waited for; matrix products, arithmetic and copies ran while one was open for 11% of the time, Pallas kernels for 60%

profile of v5, /device:TPU:0, one launch (start us, length us, event | category | flops | bytes accessed | tf_op | source)
XLA Modules:
  0.0 1048.2 jit_solution(6076746140436630317)
XLA Ops:
  12.3 3.2 constant_dynamic-slice_fusion.1
  15.5 2.4 concatenate.18
  18.0 4.3 constant_dynamic-slice_fusion.9
  22.3 4.1 concatenate.17
  30.5 85.1 %gather_normed.1 = (bf16[2,1920,2304]{2,1,0:T(8,128)(2,1)}, f32[2,1920,128]{2,1,0:T(8,128)}, f32[2,1920,128]{2,1,0:T(8,128)}, s32[2,1920,1]{2,1,0:T(8,128)}) custom-call(bf16[2,240,2304]{2,1,0:T(8,128)(2,1)} %fusion.10.refs_0_, f32[1,128]{1,0:T(1,128)} %multiply_power_fusion.refs_1_, f32[8,128]{1,0:T(8,128)} %broadcast_in_dim.14.refs_2_), custom_call_target="tpu_custom_call" | custom-call | bytes 270000000 | tf_op jit(solution)/shard_map/gather_normed/pallas_call | solution.py:644
  119.1 2.4 constant_dynamic-slice_fusion
  121.6 2.4 slice.49
  123.9 3.2 all_to_all.29
  127.1 4.3 all-to-all-start
  135.2 17.3 %project.1 = (bf16[2,1920,256]{2,1,0:T(8,128)(2,1)S(1)}, bf16[2,1920,256]{2,1,0:T(8,128)(2,1)S(1)}, bf16[2,1920,256]{2,1,0:T(8,128)(2,1)S(1)}) custom-call(bf16[2,1920,2304]{2,1,0:T(8,128)(2,1)} %get-tuple-element.53.x_ref, bf16[2304,512]{1,0:T(8,128)(2,1)S(1)} %bitcast.75, bf16[2304,256]{1,0:T(8,128)(2,1)S(1)} %collective-permute-done.far_ref.refs_2_, ...), custom_call_target="tpu_custom_call" | custom-call | flops 13589544960 | bytes 17694720 | tf_op jit(solution)/shard_map/project/pallas_call | solution.py:1081
  152.5 15.9 %attend.1 = (bf16[2,1920,256]{2,1,0:T(8,128)(2,1)S(1)}, f32[2,1920,1]{2,1,0:T(8,128)S(1)}) custom-call(bf16[2,1920,256]{2,1,0:T(8,128)(2,1)S(1)} %get-tuple-element.57.q_ref, bf16[2,1920,256]{2,1,0:T(8,128)(2,1)S(1)} %get-tuple-element.58.k_ref, bf16[2,1920,256]{2,1,0:T(8,128)(2,1)S(1)} %get-tuple-element.59.v_ref, s32[2,1920,1]{2,1,0:T(8,128)S(1)} %copy-done.6), custom_call_target="tpu_custom_call" | custom-call | flops 6039797760 | bytes 9830400 | tf_op jit(solution)/shard_map/attend/pallas_call | solution.py:1134
  174.8 85.1 %scatter_mixed.1 = f32[2,240,2304]{2,1,0:T(8,128)} custom-call(bf16[2,1920,256]{2,1,0:T(8,128)(2,1)} %copy-done.7, bf16[256,2304]{1,0:T(8,128)(2,1)} %bitcast.7.refs_1_), custom_call_target="tpu_custom_call" | custom-call | flops 4529848320 | bytes 270000000 | tf_op jit(solution)/shard_map/scatter_mixed/pallas_call | solution.py:832
  260.0 2.8 multiply_reduce_fusion.7
  263.5 2.7 multiply_reduce_fusion.6
  270.1 14.0 %all-gather.6.cloned.1.call-done.refs_1_.refs_2_ = bf16[2304,1152]{1,0:T(8,128)(2,1)} async-done(((bf16[576,1152]{1,0:T(8,128)(2,1)}), bf16[2304,1152]{1,0:T(8,128)(2,1)}) %all-gather.6.cloned.1.call-update) | async-done | bytes 5308432 | tf_op jit(solution)/shard_map/all_gather | solution.py:122
  284.1 94.7 %gather_ffn_in.1 = (bf16[2,1920,2304]{2,1,0:T(8,128)(2,1)}, bf16[2,1920,1152]{2,1,0:T(8,128)(2,1)}, bf16[2,1920,1152]{2,1,0:T(8,128)(2,1)}, bf16[2,1920,1152]{2,1,0:T(8,128)(2,1)}) custom-call(bf16[2,240,2304]{2,1,0:T(8,128)(2,1)} %multiply_convert_fusion.refs_0_, bf16[2304,1152]{1,0:T(8,128)(2,1)} %all-gather.6.cloned.1.call-done.refs_1_.refs_2_, ...), custom_call_target="tpu_custom_call" | custom-call | flops 40768634880 | bytes 270000000 | tf_op jit(solution)/shard_map/gather_ffn_in/pallas_call | solution.py:644
  378.9 4.2 all-gather.10.cloned.1.call-done.refs_1_
  383.1 91.2 %scatter_down.1 = f32[2,240,2304]{2,1,0:T(8,128)} custom-call(bf16[2,1920,1152]{2,1,0:T(8,128)(2,1)} %get-tuple-element.63.refs_0_.refs_4_, bf16[1152,2304]{1,0:T(8,128)(2,1)} %all-gather.10.cloned.1.call-done.refs_1_), custom_call_target="tpu_custom_call" | custom-call | flops 20384317440 | bytes 270000000 | tf_op jit(solution)/shard_map/scatter_down/pallas_call | solution.py:832
  474.3 2.8 multiply_reduce_fusion.5
  477.8 3.9 fusion.7
  481.8 3.5 fusion.3
  485.3 98.6 %gather_grad_down.1 = (bf16[2,1920,2304]{2,1,0:T(8,128)(2,1)}, bf16[2,1920,1152]{2,1,0:T(8,128)(2,1)}, bf16[2,1920,1152]{2,1,0:T(8,128)(2,1)}, bf16[1152,2304]{1,0:T(8,128)(2,1)}) custom-call(bf16[2,240,2304]{2,1,0:T(8,128)(2,1)} %get-tuple-element.168.refs_0_, bf16[1152,2304]{1,0:T(8,128)(2,1)} %all-gather.10.cloned.1.call-done.refs_1_, ...), custom_call_target="tpu_custom_call" | custom-call | flops 40768634880 | bytes 270000000 | tf_op jit(solution)/shard_map/gather_grad_down/pallas_call | solution.py:644
  584.0 114.9 %scatter_grad_ffn_in.1 = (f32[2,240,2304]{2,1,0:T(8,128)}, bf16[2304,1152]{1,0:T(8,128)(2,1)}) custom-call(bf16[2,1920,1152]{2,1,0:T(8,128)(2,1)} %get-tuple-element.66.refs_0_.refs_5_, bf16[2,1920,1152]{2,1,0:T(8,128)(2,1)} %get-tuple-element.67.refs_1_.refs_4_, bf16[2304,1152]{1,0:T(8,128)(2,1)} %all-gather.6.cloned.1.call-done.refs_1_.refs_2_, ...), custom_call_target="tpu_custom_call" | custom-call | flops 61152952320 | bytes 270000000 | tf_op jit(solution)/shard_map/scatter_grad_ffn_in/pallas_call | solution.py:832
  699.7 5.4 multiply_reduce_fusion.1
  705.2 6.9 multiply_reduce_fusion.2
  712.1 2.1 copy-done.20
  714.2 2.3 fusion.4.refs_0_
  716.5 89.4 %gather_grad_mixed.1 = (bf16[2,1920,2304]{2,1,0:T(8,128)(2,1)}, bf16[2,1920,256]{2,1,0:T(8,128)(2,1)}, bf16[2304,1152]{1,0:T(8,128)(2,1)}, bf16[256,2304]{1,0:T(8,128)(2,1)}) custom-call(bf16[2,240,2304]{2,1,0:T(8,128)(2,1)} %fusion.4.refs_0_, bf16[256,2304]{1,0:T(8,128)(2,1)} %bitcast.7.refs_1_, bf16[2,1920,256]{2,1,0:T(8,128)(2,1)} %copy-done.7, ...), custom_call_target="tpu_custom_call" | custom-call | flops 24914165760 | bytes 270000000 | tf_op jit(solution)/shard_map/gather_grad_mixed/pallas_call | solution.py:644
  806.7 4.8 all_to_all.32
  811.5 2.9 copy.70
  814.4 4.5 all-to-all-start.1
  823.6 27.8 %attend_back.1.refs_0_ = bf16[2,1920,768]{2,1,0:T(8,128)(2,1)} custom-call(bf16[2,1920,256]{2,1,0:T(8,128)(2,1)S(1)} %copy-done.9, bf16[2,1920,256]{2,1,0:T(8,128)(2,1)S(1)} %copy-done.11, bf16[2,1920,256]{2,1,0:T(8,128)(2,1)S(1)} %copy-done.13, bf16[2,1920,256]{2,1,0:T(8,128)(2,1)} %get-tuple-element.74.g_ref, s32[2,1920,1]{2,1,0:T(8,128)} %get-tuple-element.60.low_ref, ...), custom_call_target="tpu_custom_call" | custom-call | flops 15099494400 | bytes 23592960 | tf_op jit(solution)/shard_map/attend_back/pallas_call | solution.py:1158
  853.2 2.1 copy.71
  855.3 2.6 copy.74
  857.8 4.3 all-to-all-start.2
  862.2 19.2 %bitcast_convert_fusion = bf16[2304,768]{1,0:T(8,128)(2,1)S(1)} fusion(bf16[2,1920,2304]{2,1,0:T(8,128)(2,1)} %get-tuple-element.53.x_ref, bf16[2,1920,768]{2,1,0:T(8,128)(2,1)} %attend_back.1.refs_0_), kind=kOutput, calls=%fused_computation.5 | convolution fusion | flops 13591314432 | bytes 27131904 | tf_op jit(solution)/shard_map/dot_general | solution.py:77
  885.9 3.3 bitcast_convert_fusion.2
  894.4 3.6 copy.82
  898.0 2.4 multiply_reduce_fusion
  901.1 95.7 %scatter_grad_normed.1 = (f32[2,240,2304]{2,1,0:T(8,128)}, bf16[8,64,288]{2,1,0:T(8,128)(2,1)}, f32[72,128]{1,0:T(8,128)}) custom-call(bf16[2,1920,768]{2,1,0:T(8,128)(2,1)} %attend_back.1.refs_0_, bf16[2304,512]{1,0:T(8,128)(2,1)} %bitcast.76, bf16[2304,256]{1,0:T(8,128)(2,1)} %copy-done.3, bf16[8,64,288]{2,1,0:T(8,128)(2,1)} %bitcast.86, ...), custom_call_target="tpu_custom_call" | custom-call | flops 13589544960 | bytes 270000000 | tf_op jit(solution)/shard_map/scatter_grad_normed/pallas_call | solution.py:832
  999.1 3.4 copy.80
  1002.5 2.9 fusion.11
  1006.7 2.6 copy.76
  1009.3 5.3 all-to-all-start.3
  1014.6 6.8 fusion.6
  1025.3 9.4 all-to-all-done.3
  1034.7 3.1 bitcast_convert_fusion.1
  1037.8 3.4 copy.81
  (185 shorter events, 53.8 us)
Async XLA Ops:
  7.2 108.4 %all-gather.12.cloned.1.call-start = ((), (), s32[]{:S(2)}) async-start(), calls=%async_computation.17 | async-start | bytes 4423680 | tf_op jit(solution)/shard_map/all_gather | solution.py:1196
  12.3 257.9 %all-gather.8.cloned.1.call-start = ((), (), s32[]{:S(2)}) async-start(), calls=%async_computation.10 | async-start | bytes 6635520 | tf_op jit(solution)/shard_map/all_gather | solution.py:122
  17.9 8.6 copy-start.51
  18.0 9.5 copy-start.18
  18.0 266.2 %all-gather.6.cloned.1.call-start = ((), (), s32[]{:S(2)}) async-start(), calls=%async_computation.9 | async-start | bytes 6635520 | tf_op jit(solution)/shard_map/all_gather | solution.py:122
  22.3 5.6 copy-start.28
  26.5 356.6 %all-gather.10.cloned.1.call-start = ((), (), s32[]{:S(2)}) async-start(), calls=%async_computation.11 | async-start | bytes 6635520 | tf_op jit(solution)/shard_map/all_gather | solution.py:122
  27.9 87.7 %copy-start.43 = (f32[2,240]{1,0:T(2,128)}, f32[2,240]{1,0:T(2,128)S(1)}, u32[]{:S(2)}) copy-start(f32[2,240]{1,0:T(2,128)S(1)} %fusion.8) | copy-start | bytes 5764
  27.9 87.7 %copy-start.49 = (f32[2,240]{1,0:T(2,128)}, f32[2,240]{1,0:T(2,128)S(1)}, u32[]{:S(2)}) copy-start(f32[2,240]{1,0:T(2,128)S(1)} %fusion.14) | copy-start | bytes 5764
  117.5 780.4 %copy-start.2 = (bf16[4,576,512]{2,1,0:T(8,128)(2,1)}, bf16[4,576,512]{2,1,0:T(8,128)(2,1)S(1)}, u32[]{:S(2)}) copy-start(bf16[4,576,512]{2,1,0:T(8,128)(2,1)S(1)} %slice.47) | copy-start | bytes 7077892
  118.7 13.0 %collective-permute-start = (bf16[2304,256]{1,0:T(8,128)(2,1)}, bf16[2304,256]{1,0:T(8,128)(2,1)S(1)}, u32[]{:S(2)}, u32[]{:S(2)}) collective-permute-start(bf16[2304,256]{1,0:T(8,128)(2,1)} %slice.61), channel_id=1, source_target_pairs={{0,4},{4,0},{8,12},{12,8},{16,20},{20,16},{24,28},{28,24},{1,5},{5... | collective-permute-start | bytes 3538952 | tf_op jit(solution)/shard_map/ppermute | solution.py:1225
  127.1 47.6 %all-to-all-start = ((bf16[8,32,2304]{2,1,0:T(8,128)(2,1)}), bf16[8,32,2304]{2,1,0:T(8,128)(2,1)}, u32[]{:S(2)}, u32[]{:S(2)}) async-start(bf16[8,32,2304]{2,1,0:T(8,128)(2,1)} %all_to_all.29), calls=%async_computation | async-start | bytes 2359296 | tf_op jit(solution)/shard_map/all_to_all | solution.py:132
  131.4 585.1 %reduce-scatter.6.cloned.1.call-start = ((), (), s32[]{:S(2)}) async-start(), calls=%async_computation.12 | async-start | bytes 6635520 | tf_op jit(solution)/shard_map/reduce_scatter | solution.py:126
  131.7 757.5 %copy-start.3 = (bf16[2304,256]{1,0:T(8,128)(2,1)}, bf16[2304,256]{1,0:T(8,128)(2,1)S(1)}, u32[]{:S(2)}) copy-start(bf16[2304,256]{1,0:T(8,128)(2,1)S(1)} %collective-permute-done.far_ref.refs_2_) | copy-start | bytes 3538948
  135.2 17.3 %copy-start.6 = (s32[2,1920,1]{2,1,0:T(8,128)S(1)}, s32[2,1920,1]{2,1,0:T(8,128)}, u32[]{:S(2)}) copy-start(s32[2,1920,1]{2,1,0:T(8,128)} %get-tuple-element.60.low_ref) | copy-start | bytes 46084
  174.8 88.0 %copy-start.32 = (f32[2304]{0:T(1024)S(1)}, f32[2304]{0:T(1024)}, u32[]{:S(2)}) copy-start(f32[2304]{0:T(1024)} %param.24) | copy-start | bytes 27652
  259.9 3.6 copy-start.17
  262.7 3.5 copy-start.45
  263.5 2.7 copy-start.41
  263.5 4.8 copy-start.30
  266.3 2.1 copy-start.15
  383.1 94.0 %copy-start.38 = (f32[2304]{0:T(1024)S(1)}, f32[2304]{0:T(1024)}, u32[]{:S(2)}) copy-start(f32[2304]{0:T(1024)} %param.26) | copy-start | bytes 27652
  474.3 3.6 copy-start.21
  477.0 4.8 copy-start.16
  477.0 4.8 copy-start.22
  584.0 222.7 %reduce-scatter.8.cloned.1.call-start = ((), (), s32[]{:S(2)}) async-start(), calls=%async_computation.13 | async-start | bytes 6635520 | tf_op jit(solution)/shard_map/reduce_scatter | solution.py:126
  699.0 156.2 %reduce-scatter.10.cloned.1.call-start = ((), (), s32[]{:S(2)}) async-start(), calls=%async_computation.14 | async-start | bytes 1474560 | tf_op jit(solution)/shard_map/reduce_scatter | solution.py:126
  699.7 5.4 copy-start.48
  699.7 5.5 copy-start.23
  699.7 5.5 copy-start.33
  699.7 5.5 copy-start.42
  699.7 14.5 %slice-start = ((s8[4423680]{0:T(1024)(128)(4,1)}), s8[4194304]{0:T(1024)(128)(4,1)S(1)}, s32[]{:S(2)}) async-start(s8[4423680]{0:T(1024)(128)(4,1)} %bitcast.77), calls=%async_computation.18 | async-start | bytes 8388608
  705.2 7.0 copy-start.46
  705.2 9.0 slice-start.1
  805.9 200.8 %reduce-scatter.14.cloned.1.call-start = ((), (), s32[]{:S(2)}) async-start(), calls=%async_computation.16 | async-start | bytes 6635520 | tf_op jit(solution)/shard_map/reduce_scatter | solution.py:126
  814.4 37.0 %all-to-all-start.1 = ((bf16[288,8,288]{2,0,1:T(8,128)(2,1)}), bf16[288,8,288]{2,0,1:T(8,128)(2,1)}, u32[]{:S(2)}, u32[]{:S(2)}) async-start(bf16[288,8,288]{2,0,1:T(8,128)(2,1)} %copy.70), calls=%async_computation.4 | async-start | bytes 3538944 | tf_op jit(solution)/shard_map/all_to_all | solution.py:132
  857.8 28.0 %all-to-all-start.2 = ((bf16[576,8,144]{0,2,1:T(8,128)(2,1)}), bf16[576,8,144]{0,2,1:T(8,128)(2,1)}, u32[]{:S(2)}, u32[]{:S(2)}) async-start(bf16[576,8,144]{0,2,1:T(8,128)(2,1)} %bitcast.82), calls=%async_computation.5 | async-start | bytes 2949120 | tf_op jit(solution)/shard_map/all_to_all | solution.py:132
  862.1 159.3 %reduce-scatter.12.cloned.1.call-start = ((), (), s32[]{:S(2)}) async-start(), calls=%async_computation.15 | async-start | bytes 2949120 | tf_op jit(solution)/shard_map/reduce_scatter | solution.py:126
  884.8 4.4 collective-permute-start.1
  885.9 3.3 copy-start.25
  885.9 5.3 copy-start.26
  996.8 5.7 copy-start.19
  996.8 5.7 copy-start.29
  1002.5 2.9 copy-start.44
  1002.5 3.0 copy-start.34
  1005.5 9.2 copy-start.50
  1009.3 25.4 %all-to-all-start.3 = ((bf16[576,8,144]{0,2,1:T(8,128)(2,1)}), bf16[576,8,144]{0,2,1:T(8,128)(2,1)}, u32[]{:S(2)}, u32[]{:S(2)}) async-start(bf16[576,8,144]{0,2,1:T(8,128)(2,1)} %bitcast.81), calls=%async_computation.8 | async-start | bytes 2949120 | tf_op jit(solution)/shard_map/all_to_all | solution.py:132
  1023.3 18.0 %copy-start.1 = (bf16[512,2304]{1,0:T(8,128)(2,1)S(1)}, bf16[512,2304]{1,0:T(8,128)(2,1)}, u32[]{:S(2)}) copy-start(bf16[512,2304]{1,0:T(8,128)(2,1)} %param.19) | copy-start | bytes 7077892
  (21 other events, 30.6 us)
Sparse Core Ops, SparseCore 0:
  12.4 72.6 all-gather.11
  86.7 97.7 all-gather.7
  186.6 97.4 all-gather.5
  285.5 97.4 all-gather.9
  584.1 94.2 reduce-scatter.5
  699.1 93.6 reduce-scatter.7
  806.0 27.8 reduce-scatter.9
  836.2 121.1 reduce-scatter.13
  959.8 47.9 reduce-scatter.11

commit v6 on v5

--- a/solution.py
+++ b/solution.py
@@ -734,23 +734,31 @@
     for rider in riders:
         rider.begin()
 
+    outs = []
+
     def finish(step):
         gives[step].wait_recv()
-        kind = jnp.bfloat16 if step < 4 else jnp.float32
+        kind = jnp.bfloat16 if step < 6 else jnp.float32
         total = sums[step % 2, kept].astype(kind) + from_core[step % 4].astype(kind)
         if step < 4:
             pl.semaphore_signal(credit, inc=1, device_id={"seq": other_core}, device_id_type=MESH)
         for arrived in added.get(step, ()):
             sends[arrived].wait_recv()
-            total = total + from_link[arrived].astype(jnp.float32)
+            total = total + from_link[arrived].astype(kind)
         if step < 6:
-            held[step] = total.astype(jnp.bfloat16)
+            held[step] = total
             sends[step].start()
         else:
-            out = pltpu.make_async_copy(out_buf, out_ref.at[step - 6], out_sem.at[step - 6])
-            out_buf[...] = total
-            out.start()
-            out.wait()
+            if outs and out_buf.shape[0] == 1:
+                outs.pop().wait()
+            slot = (step - 6) % out_buf.shape[0]
+            out_buf[slot] = total
+            outs.append(
+                pltpu.make_async_copy(
+                    out_buf.at[slot], out_ref.at[step - 6], out_sem.at[step - 6]
+                )
+            )
+            outs[-1].start()
 
     side = Side(rows, side_refs, side_bufs, sum_bufs, side_sem)
     for step in range(8):
@@ -778,6 +786,8 @@
     finish(7)
     for move in gives[6:] + sends:
         move.wait_send()
+    for out in outs:
+        out.wait()
     for rider in riders:
         rider.end()
 
@@ -796,7 +806,7 @@
         pltpu.VMEM((6, rows, width), jnp.bfloat16),
         pltpu.VMEM((4, rows, width), jnp.bfloat16),
         pltpu.VMEM((6, rows, width), jnp.bfloat16),
-        pltpu.VMEM((rows, width), jnp.float32),
+        pltpu.VMEM((1 if job.side else 2, rows, width), jnp.float32),
     ]
     scratch += [pltpu.VMEM((2 * rows, array.shape[2]), array.dtype) for array in job.side]
     scratch += [pltpu.VMEM(shape, jnp.float32) for shape in job.sums]

time: 1060 us -> 1050 us (level)
  no operation moved by 1% of the time
where the time goes in v6:
time: 1050 us
  Pallas kernels  812 us (77%)
  local copies, waits for them, and re-layouts  87.2 us (8%)
  other arithmetic  62.1 us (6%)
  waiting for transfers between devices  29.9 us (3%)
  starting transfers between devices  20.4 us (2%)
  matrix products  19.2 us (2%)
  between operations  15.1 us (1%)
    pallas_call x4, Pallas kernels, plane_scatter(): pl.pallas_call(functools.partial(scatter_kernel, job, rows), in_specs=in_...  383 us
    pallas_call x4, Pallas kernels, plane_gather(): pl.pallas_call(functools.partial(gather_kernel, job, rows), in_specs=in_s...  368 us
    unnamed x113, local copies, waits for them, and re-layouts  35.9 us
    pallas_call x1, Pallas kernels, attend_back(): pl.pallas_call(functools.partial(attend_back_kernel, block, reach), grid=...  27.8 us
  transfers between devices with their start and end apart: 15, of which 3 were waited for; matrix products, arithmetic and copies ran while one was open for 11% of the time, Pallas kernels for 60%

profile of v6, /device:TPU:0, one launch (start us, length us, event | category | flops | bytes accessed | tf_op | source)
XLA Modules:
  0.0 1045.8 jit_solution(2115290904153741268)
XLA Ops:
  12.3 3.2 constant_dynamic-slice_fusion.1
  15.5 2.4 concatenate.18
  18.0 4.3 constant_dynamic-slice_fusion.9
  22.3 4.1 concatenate.17
  30.5 85.1 %gather_normed.1 = (bf16[2,1920,2304]{2,1,0:T(8,128)(2,1)}, f32[2,1920,128]{2,1,0:T(8,128)}, f32[2,1920,128]{2,1,0:T(8,128)}, s32[2,1920,1]{2,1,0:T(8,128)}) custom-call(bf16[2,240,2304]{2,1,0:T(8,128)(2,1)} %fusion.10.refs_0_, f32[1,128]{1,0:T(1,128)} %multiply_power_fusion.refs_1_, f32[8,128]{1,0:T(8,128)} %broadcast_in_dim.14.refs_2_), custom_call_target="tpu_custom_call" | custom-call | bytes 270000000 | tf_op jit(solution)/shard_map/gather_normed/pallas_call | solution.py:644
  119.1 2.4 constant_dynamic-slice_fusion
  121.6 2.4 slice.49
  123.9 3.2 all_to_all.29
  127.1 4.3 all-to-all-start
  135.2 17.3 %project.1 = (bf16[2,1920,256]{2,1,0:T(8,128)(2,1)S(1)}, bf16[2,1920,256]{2,1,0:T(8,128)(2,1)S(1)}, bf16[2,1920,256]{2,1,0:T(8,128)(2,1)S(1)}) custom-call(bf16[2,1920,2304]{2,1,0:T(8,128)(2,1)} %get-tuple-element.53.x_ref, bf16[2304,512]{1,0:T(8,128)(2,1)S(1)} %bitcast.75, bf16[2304,256]{1,0:T(8,128)(2,1)S(1)} %collective-permute-done.far_ref.refs_2_, ...), custom_call_target="tpu_custom_call" | custom-call | flops 13589544960 | bytes 17694720 | tf_op jit(solution)/shard_map/project/pallas_call | solution.py:1091
  152.5 15.9 %attend.1 = (bf16[2,1920,256]{2,1,0:T(8,128)(2,1)S(1)}, f32[2,1920,1]{2,1,0:T(8,128)S(1)}) custom-call(bf16[2,1920,256]{2,1,0:T(8,128)(2,1)S(1)} %get-tuple-element.57.q_ref, bf16[2,1920,256]{2,1,0:T(8,128)(2,1)S(1)} %get-tuple-element.58.k_ref, bf16[2,1920,256]{2,1,0:T(8,128)(2,1)S(1)} %get-tuple-element.59.v_ref, s32[2,1920,1]{2,1,0:T(8,128)S(1)} %copy-done.6), custom_call_target="tpu_custom_call" | custom-call | flops 6039797760 | bytes 9830400 | tf_op jit(solution)/shard_map/attend/pallas_call | solution.py:1144
  174.8 83.8 %scatter_mixed.1 = f32[2,240,2304]{2,1,0:T(8,128)} custom-call(bf16[2,1920,256]{2,1,0:T(8,128)(2,1)} %copy-done.7, bf16[256,2304]{1,0:T(8,128)(2,1)} %bitcast.7.refs_1_), custom_call_target="tpu_custom_call" | custom-call | flops 4529848320 | bytes 270000000 | tf_op jit(solution)/shard_map/scatter_mixed/pallas_call | solution.py:842
  258.6 2.8 multiply_reduce_fusion.7
  262.2 2.7 multiply_reduce_fusion.6
  268.8 15.3 %all-gather.6.cloned.1.call-done.refs_1_.refs_2_ = bf16[2304,1152]{1,0:T(8,128)(2,1)} async-done(((bf16[576,1152]{1,0:T(8,128)(2,1)}), bf16[2304,1152]{1,0:T(8,128)(2,1)}) %all-gather.6.cloned.1.call-update) | async-done | bytes 5308432 | tf_op jit(solution)/shard_map/all_gather | solution.py:122
  284.1 94.7 %gather_ffn_in.1 = (bf16[2,1920,2304]{2,1,0:T(8,128)(2,1)}, bf16[2,1920,1152]{2,1,0:T(8,128)(2,1)}, bf16[2,1920,1152]{2,1,0:T(8,128)(2,1)}, bf16[2,1920,1152]{2,1,0:T(8,128)(2,1)}) custom-call(bf16[2,240,2304]{2,1,0:T(8,128)(2,1)} %multiply_convert_fusion.refs_0_, bf16[2304,1152]{1,0:T(8,128)(2,1)} %all-gather.6.cloned.1.call-done.refs_1_.refs_2_, ...), custom_call_target="tpu_custom_call" | custom-call | flops 40768634880 | bytes 270000000 | tf_op jit(solution)/shard_map/gather_ffn_in/pallas_call | solution.py:644
  378.9 4.2 all-gather.10.cloned.1.call-done.refs_1_
  383.1 89.8 %scatter_down.1 = f32[2,240,2304]{2,1,0:T(8,128)} custom-call(bf16[2,1920,1152]{2,1,0:T(8,128)(2,1)} %get-tuple-element.63.refs_0_.refs_4_, bf16[1152,2304]{1,0:T(8,128)(2,1)} %all-gather.10.cloned.1.call-done.refs_1_), custom_call_target="tpu_custom_call" | custom-call | flops 20384317440 | bytes 270000000 | tf_op jit(solution)/shard_map/scatter_down/pallas_call | solution.py:842
  472.9 2.8 multiply_reduce_fusion.5
  476.4 3.9 fusion.7
  480.4 3.5 fusion.3
  483.9 98.6 %gather_grad_down.1 = (bf16[2,1920,2304]{2,1,0:T(8,128)(2,1)}, bf16[2,1920,1152]{2,1,0:T(8,128)(2,1)}, bf16[2,1920,1152]{2,1,0:T(8,128)(2,1)}, bf16[1152,2304]{1,0:T(8,128)(2,1)}) custom-call(bf16[2,240,2304]{2,1,0:T(8,128)(2,1)} %get-tuple-element.168.refs_0_, bf16[1152,2304]{1,0:T(8,128)(2,1)} %all-gather.10.cloned.1.call-done.refs_1_, ...), custom_call_target="tpu_custom_call" | custom-call | flops 40768634880 | bytes 270000000 | tf_op jit(solution)/shard_map/gather_grad_down/pallas_call | solution.py:644
  582.6 113.8 %scatter_grad_ffn_in.1 = (f32[2,240,2304]{2,1,0:T(8,128)}, bf16[2304,1152]{1,0:T(8,128)(2,1)}) custom-call(bf16[2,1920,1152]{2,1,0:T(8,128)(2,1)} %get-tuple-element.66.refs_0_.refs_5_, bf16[2,1920,1152]{2,1,0:T(8,128)(2,1)} %get-tuple-element.67.refs_1_.refs_4_, bf16[2304,1152]{1,0:T(8,128)(2,1)} %all-gather.6.cloned.1.call-done.refs_1_.refs_2_, ...), custom_call_target="tpu_custom_call" | custom-call | flops 61152952320 | bytes 270000000 | tf_op jit(solution)/shard_map/scatter_grad_ffn_in/pallas_call | solution.py:842
  697.2 5.4 multiply_reduce_fusion.1
  702.7 6.9 multiply_reduce_fusion.2
  709.6 2.1 copy-done.20
  711.7 2.3 fusion.4.refs_0_
  714.0 89.4 %gather_grad_mixed.1 = (bf16[2,1920,2304]{2,1,0:T(8,128)(2,1)}, bf16[2,1920,256]{2,1,0:T(8,128)(2,1)}, bf16[2304,1152]{1,0:T(8,128)(2,1)}, bf16[256,2304]{1,0:T(8,128)(2,1)}) custom-call(bf16[2,240,2304]{2,1,0:T(8,128)(2,1)} %fusion.4.refs_0_, bf16[256,2304]{1,0:T(8,128)(2,1)} %bitcast.7.refs_1_, bf16[2,1920,256]{2,1,0:T(8,128)(2,1)} %copy-done.7, ...), custom_call_target="tpu_custom_call" | custom-call | flops 24914165760 | bytes 270000000 | tf_op jit(solution)/shard_map/gather_grad_mixed/pallas_call | solution.py:644
  804.2 4.8 all_to_all.32
  809.0 2.9 copy.70
  811.9 4.5 all-to-all-start.1
  821.1 27.8 %attend_back.1.refs_0_ = bf16[2,1920,768]{2,1,0:T(8,128)(2,1)} custom-call(bf16[2,1920,256]{2,1,0:T(8,128)(2,1)S(1)} %copy-done.9, bf16[2,1920,256]{2,1,0:T(8,128)(2,1)S(1)} %copy-done.11, bf16[2,1920,256]{2,1,0:T(8,128)(2,1)S(1)} %copy-done.13, bf16[2,1920,256]{2,1,0:T(8,128)(2,1)} %get-tuple-element.74.g_ref, s32[2,1920,1]{2,1,0:T(8,128)} %get-tuple-element.60.low_ref, ...), custom_call_target="tpu_custom_call" | custom-call | flops 15099494400 | bytes 23592960 | tf_op jit(solution)/shard_map/attend_back/pallas_call | solution.py:1168
  850.7 2.1 copy.71
  852.8 2.6 copy.74
  855.4 4.3 all-to-all-start.2
  859.7 19.2 %bitcast_convert_fusion = bf16[2304,768]{1,0:T(8,128)(2,1)S(1)} fusion(bf16[2,1920,2304]{2,1,0:T(8,128)(2,1)} %get-tuple-element.53.x_ref, bf16[2,1920,768]{2,1,0:T(8,128)(2,1)} %attend_back.1.refs_0_), kind=kOutput, calls=%fused_computation.5 | convolution fusion | flops 13591314432 | bytes 27131904 | tf_op jit(solution)/shard_map/dot_general | solution.py:77
  883.4 3.3 bitcast_convert_fusion.2
  891.9 3.6 copy.82
  895.4 2.4 multiply_reduce_fusion
  898.6 95.7 %scatter_grad_normed.1 = (f32[2,240,2304]{2,1,0:T(8,128)}, bf16[8,64,288]{2,1,0:T(8,128)(2,1)}, f32[72,128]{1,0:T(8,128)}) custom-call(bf16[2,1920,768]{2,1,0:T(8,128)(2,1)} %attend_back.1.refs_0_, bf16[2304,512]{1,0:T(8,128)(2,1)} %bitcast.76, bf16[2304,256]{1,0:T(8,128)(2,1)} %copy-done.3, bf16[8,64,288]{2,1,0:T(8,128)(2,1)} %bitcast.86, ...), custom_call_target="tpu_custom_call" | custom-call | flops 13589544960 | bytes 270000000 | tf_op jit(solution)/shard_map/scatter_grad_normed/pallas_call | solution.py:842
  996.6 3.4 copy.80
  1000.1 2.9 fusion.11
  1004.3 2.6 copy.76
  1006.8 5.3 all-to-all-start.3
  1012.1 6.8 fusion.6
  1022.8 9.4 all-to-all-done.3
  1032.2 3.1 bitcast_convert_fusion.1
  1035.4 3.4 copy.81
  (185 shorter events, 53.7 us)
Async XLA Ops:
  7.2 108.4 %all-gather.12.cloned.1.call-start = ((), (), s32[]{:S(2)}) async-start(), calls=%async_computation.17 | async-start | bytes 4423680 | tf_op jit(solution)/shard_map/all_gather | solution.py:1206
  12.3 256.5 %all-gather.8.cloned.1.call-start = ((), (), s32[]{:S(2)}) async-start(), calls=%async_computation.10 | async-start | bytes 6635520 | tf_op jit(solution)/shard_map/all_gather | solution.py:122
  17.9 8.6 copy-start.51
  18.0 9.5 copy-start.18
  18.0 266.2 %all-gather.6.cloned.1.call-start = ((), (), s32[]{:S(2)}) async-start(), calls=%async_computation.9 | async-start | bytes 6635520 | tf_op jit(solution)/shard_map/all_gather | solution.py:122
  22.3 5.6 copy-start.28
  26.5 356.6 %all-gather.10.cloned.1.call-start = ((), (), s32[]{:S(2)}) async-start(), calls=%async_computation.11 | async-start | bytes 6635520 | tf_op jit(solution)/shard_map/all_gather | solution.py:122
  27.9 87.7 %copy-start.43 = (f32[2,240]{1,0:T(2,128)}, f32[2,240]{1,0:T(2,128)S(1)}, u32[]{:S(2)}) copy-start(f32[2,240]{1,0:T(2,128)S(1)} %fusion.8) | copy-start | bytes 5764
  27.9 87.7 %copy-start.49 = (f32[2,240]{1,0:T(2,128)}, f32[2,240]{1,0:T(2,128)S(1)}, u32[]{:S(2)}) copy-start(f32[2,240]{1,0:T(2,128)S(1)} %fusion.14) | copy-start | bytes 5764
  117.5 777.9 %copy-start.2 = (bf16[4,576,512]{2,1,0:T(8,128)(2,1)}, bf16[4,576,512]{2,1,0:T(8,128)(2,1)S(1)}, u32[]{:S(2)}) copy-start(bf16[4,576,512]{2,1,0:T(8,128)(2,1)S(1)} %slice.47) | copy-start | bytes 7077892
  118.7 13.0 %collective-permute-start = (bf16[2304,256]{1,0:T(8,128)(2,1)}, bf16[2304,256]{1,0:T(8,128)(2,1)S(1)}, u32[]{:S(2)}, u32[]{:S(2)}) collective-permute-start(bf16[2304,256]{1,0:T(8,128)(2,1)} %slice.61), channel_id=1, source_target_pairs={{0,4},{4,0},{8,12},{12,8},{16,20},{20,16},{24,28},{28,24},{1,5},{5... | collective-permute-start | bytes 3538952 | tf_op jit(solution)/shard_map/ppermute | solution.py:1235
  127.1 47.6 %all-to-all-start = ((bf16[8,32,2304]{2,1,0:T(8,128)(2,1)}), bf16[8,32,2304]{2,1,0:T(8,128)(2,1)}, u32[]{:S(2)}, u32[]{:S(2)}) async-start(bf16[8,32,2304]{2,1,0:T(8,128)(2,1)} %all_to_all.29), calls=%async_computation | async-start | bytes 2359296 | tf_op jit(solution)/shard_map/all_to_all | solution.py:132
  131.4 582.6 %reduce-scatter.6.cloned.1.call-start = ((), (), s32[]{:S(2)}) async-start(), calls=%async_computation.12 | async-start | bytes 6635520 | tf_op jit(solution)/shard_map/reduce_scatter | solution.py:126
  131.7 755.0 %copy-start.3 = (bf16[2304,256]{1,0:T(8,128)(2,1)}, bf16[2304,256]{1,0:T(8,128)(2,1)S(1)}, u32[]{:S(2)}) copy-start(bf16[2304,256]{1,0:T(8,128)(2,1)S(1)} %collective-permute-done.far_ref.refs_2_) | copy-start | bytes 3538948
  135.2 17.3 %copy-start.6 = (s32[2,1920,1]{2,1,0:T(8,128)S(1)}, s32[2,1920,1]{2,1,0:T(8,128)}, u32[]{:S(2)}) copy-start(s32[2,1920,1]{2,1,0:T(8,128)} %get-tuple-element.60.low_ref) | copy-start | bytes 46084
  174.8 86.6 %copy-start.32 = (f32[2304]{0:T(1024)S(1)}, f32[2304]{0:T(1024)}, u32[]{:S(2)}) copy-start(f32[2304]{0:T(1024)} %param.24) | copy-start | bytes 27652
  258.6 3.6 copy-start.17
  261.4 3.5 copy-start.45
  262.2 2.7 copy-start.41
  262.2 4.8 copy-start.30
  264.9 2.1 copy-start.15
  383.1 92.6 %copy-start.38 = (f32[2304]{0:T(1024)S(1)}, f32[2304]{0:T(1024)}, u32[]{:S(2)}) copy-start(f32[2304]{0:T(1024)} %param.26) | copy-start | bytes 27652
  472.9 3.6 copy-start.21
  475.6 4.8 copy-start.16
  475.6 4.8 copy-start.22
  582.6 221.6 %reduce-scatter.8.cloned.1.call-start = ((), (), s32[]{:S(2)}) async-start(), calls=%async_computation.13 | async-start | bytes 6635520 | tf_op jit(solution)/shard_map/reduce_scatter | solution.py:126
  696.5 156.3 %reduce-scatter.10.cloned.1.call-start = ((), (), s32[]{:S(2)}) async-start(), calls=%async_computation.14 | async-start | bytes 1474560 | tf_op jit(solution)/shard_map/reduce_scatter | solution.py:126
  697.2 5.4 copy-start.48
  697.2 5.5 copy-start.23
  697.2 5.5 copy-start.33
  697.2 5.5 copy-start.42
  697.2 14.5 %slice-start = ((s8[4423680]{0:T(1024)(128)(4,1)}), s8[4194304]{0:T(1024)(128)(4,1)S(1)}, s32[]{:S(2)}) async-start(s8[4423680]{0:T(1024)(128)(4,1)} %bitcast.77), calls=%async_computation.18 | async-start | bytes 8388608
  702.7 7.0 copy-start.46
  702.7 9.0 slice-start.1
  803.4 200.8 %reduce-scatter.14.cloned.1.call-start = ((), (), s32[]{:S(2)}) async-start(), calls=%async_computation.16 | async-start | bytes 6635520 | tf_op jit(solution)/shard_map/reduce_scatter | solution.py:126
  811.9 37.0 %all-to-all-start.1 = ((bf16[288,8,288]{2,0,1:T(8,128)(2,1)}), bf16[288,8,288]{2,0,1:T(8,128)(2,1)}, u32[]{:S(2)}, u32[]{:S(2)}) async-start(bf16[288,8,288]{2,0,1:T(8,128)(2,1)} %copy.70), calls=%async_computation.4 | async-start | bytes 3538944 | tf_op jit(solution)/shard_map/all_to_all | solution.py:132
  855.4 28.0 %all-to-all-start.2 = ((bf16[576,8,144]{0,2,1:T(8,128)(2,1)}), bf16[576,8,144]{0,2,1:T(8,128)(2,1)}, u32[]{:S(2)}, u32[]{:S(2)}) async-start(bf16[576,8,144]{0,2,1:T(8,128)(2,1)} %bitcast.82), calls=%async_computation.5 | async-start | bytes 2949120 | tf_op jit(solution)/shard_map/all_to_all | solution.py:132
  859.7 159.3 %reduce-scatter.12.cloned.1.call-start = ((), (), s32[]{:S(2)}) async-start(), calls=%async_computation.15 | async-start | bytes 2949120 | tf_op jit(solution)/shard_map/reduce_scatter | solution.py:126
  882.3 4.4 collective-permute-start.1
  883.4 3.3 copy-start.25
  883.4 5.3 copy-start.26
  994.3 5.7 copy-start.19
  994.3 5.7 copy-start.29
  1000.0 2.9 copy-start.44
  1000.0 3.0 copy-start.34
  1003.0 9.1 copy-start.50
  1006.8 25.4 %all-to-all-start.3 = ((bf16[576,8,144]{0,2,1:T(8,128)(2,1)}), bf16[576,8,144]{0,2,1:T(8,128)(2,1)}, u32[]{:S(2)}, u32[]{:S(2)}) async-start(bf16[576,8,144]{0,2,1:T(8,128)(2,1)} %bitcast.81), calls=%async_computation.8 | async-start | bytes 2949120 | tf_op jit(solution)/shard_map/all_to_all | solution.py:132
  1020.8 18.0 %copy-start.1 = (bf16[512,2304]{1,0:T(8,128)(2,1)S(1)}, bf16[512,2304]{1,0:T(8,128)(2,1)}, u32[]{:S(2)}) copy-start(bf16[512,2304]{1,0:T(8,128)(2,1)} %param.19) | copy-start | bytes 7077892
  (21 other events, 30.6 us)
Sparse Core Ops, SparseCore 0:
  12.4 72.6 all-gather.11
  86.7 97.7 all-gather.7
  186.6 97.4 all-gather.5
  285.5 97.4 all-gather.9
  582.7 94.2 reduce-scatter.5
  696.6 93.6 reduce-scatter.7
  803.5 27.8 reduce-scatter.9
  833.7 121.1 reduce-scatter.13
  957.3 47.9 reduce-scatter.11
